TPU v7x, 512 devices: a whole 4x4x16 slice. The times are simulated.
512 devices in a mesh: ctx: 64 (over x, z), tp: 8 (over y, core).
Axes of the slice: x: 4, y: 4, z: 16, core: 2. Of those that a mesh axis runs over, the one named last changes fastest.
Arguments:
- hidden_states: bfloat16 [8192, 8192], P('ctx', 'tp'), may hold values from -6 to 6
- select_weight: bfloat16 [8192, 2048], P('tp', 'ctx'), may hold values from -0.0625 to 0.0625
- conv_taps: float32 [4, 2048], P(None, 'tp'), may hold values from -1.5 to 1.5
- inner_input: bfloat16 [8192, 8192], P('ctx', 'tp'), may hold values from -6 to 6
- gate_input: bfloat16 [8192, 8192], P('ctx', 'tp'), may hold values from -6 to 6
- step_size: float32 [8192, 128], P('ctx', 'tp'), as said below
- decay_rate: float32 [128], P('tp'), as said below
- skip_gain: float32 [128], P('tp'), may hold values from 0.5 to 1.5
- tenant_scale: bfloat16 [16, 8192], P(None, 'tp'), may hold values from 0.099609375 to 1.8984375
- tenant_index: int32 [64], P('ctx'), may hold values from 0 to 15
- norm_gain: bfloat16 [8192], P('tp'), may hold values from 0.099609375 to 1.8984375
Outputs:
- mixer_output: bfloat16 [8192, 8192], P('ctx', 'tp')
Inputs may be any that keep to these rules, and one draw needn't show every extreme that they name: `step_size`: step sizes are positive. `decay_rate`: decay rates are positive.
All inputs are finite; a program needn't handle non-finite values.
Results may differ from a plain program's by a relative error of at most 0.012.
Values may be sent and summed in bfloat16 or wider, within the bound.
No kernel may reach another device: no remote copies, remote signals or barrier semaphores. Data moves between devices by JAX's collectives and lax.ppermute only.
A program may use at most 128 MiB of HBM per device.

v0:
```python
import jax
import jax.numpy as jnp
from jax import lax
from jax.sharding import PartitionSpec as P

N = 128
Q = 128


epsilon = 1e-05


def from_behind(shard, axis, by):
    peers = lax.axis_size(axis)
    pairs = [(i, i + by) for i in range(peers) if 0 <= i + by < peers]
    return lax.ppermute(shard, axis, pairs)


def entering(shard, axis, join, neutral):
    place = lax.axis_index(axis)
    gathered = jax.tree.map(
        lambda a, kind: lax.all_gather(a.astype(kind), axis), shard, (jnp.bfloat16, jnp.bfloat16)
    )
    state = jax.tree.map(lambda a, e: jnp.zeros_like(a) + jnp.asarray(e, a.dtype), shard, neutral)

    def one(lap, state):
        return join(
            state,
            jax.tree.map(
                lambda a, own: lax.dynamic_index_in_dim(a, lap, 0, False).astype(own.dtype),
                gathered,
                shard,
            ),
        )

    return lax.fori_loop(0, place, one, state)


def taps_apply(raw_rows, earlier, conv_taps):
    padded = jnp.concatenate([earlier, raw_rows], axis=0)
    length = raw_rows.shape[0]
    summed = jnp.zeros_like(raw_rows)
    for offset in range(conv_taps.shape[0]):
        summed = summed + conv_taps[offset][None, :] * padded[offset : offset + length]
    return jax.nn.silu(summed).astype(jnp.bfloat16)


def combine_states(earlier, latter):
    return (earlier[0] * latter[0], latter[0][:, :, None, None] * earlier[1] + latter[1])


def per_device(
    hidden_states,
    select_weight,
    conv_taps,
    inner_input,
    gate_input,
    step_size,
    decay_rate,
    skip_gain,
    tenant_scale,
    tenant_index,
    norm_gain,
):
    tok_rows = hidden_states.shape[0]
    heads_here = decay_rate.shape[0]
    inner_cols = inner_input.shape[1]
    head_width = inner_cols // heads_here
    partial_value = jnp.dot(
        hidden_states,
        lax.all_gather(select_weight, "ctx", axis=1, tiled=True),
        preferred_element_type=jnp.float32,
    )
    raw_rows = lax.psum_scatter(partial_value, "tp", scatter_dimension=1, tiled=True)
    lag_rows = conv_taps.shape[0] - 1
    earlier = from_behind(raw_rows[tok_rows - lag_rows :], "ctx", 1)
    selected = taps_apply(raw_rows, earlier, conv_taps)
    groups_here = selected.shape[1] // (2 * N)
    heads_group = heads_here // groups_here
    span_count = tok_rows // Q
    selected = selected.reshape(span_count, Q, groups_here, 2, N)
    write_key = selected[:, :, :, 0]
    read_key = selected[:, :, :, 1]
    segs_here = tenant_index.shape[0]
    onehot = (tenant_index[:, None] == jnp.arange(tenant_scale.shape[0])[None, :]).astype(
        jnp.bfloat16
    )
    seg_scale = jnp.dot(onehot, tenant_scale, preferred_element_type=jnp.float32)
    scaled = (
        inner_input.reshape(segs_here, tok_rows // segs_here, inner_cols).astype(jnp.float32)
        * seg_scale[:, None, :]
    ).reshape(tok_rows, heads_here, head_width)
    driven = (scaled * step_size[:, :, None]).astype(jnp.bfloat16)
    driven_c = driven.reshape(span_count, Q, groups_here, heads_group, head_width)
    log_decay = -step_size * decay_rate[None, :]
    cumulative = jnp.cumsum(log_decay.reshape(span_count, Q, heads_here), axis=1)
    cumul_g = cumulative.reshape(span_count, Q, groups_here, heads_group)
    scores = jnp.einsum("ctgn,csgn->cgts", read_key, write_key, preferred_element_type=jnp.float32)
    cumul_gh = jnp.transpose(cumul_g, (0, 2, 3, 1))
    lag_log = cumul_gh[..., :, None] - cumul_gh[..., None, :]
    causal = jnp.tril(jnp.ones((Q, Q), dtype=bool))
    weights = jnp.where(
        causal, scores[:, :, None] * jnp.exp(jnp.where(causal, lag_log, 0.0)), 0.0
    ).astype(jnp.bfloat16)
    within = jnp.einsum("cghts,csghp->ctghp", weights, driven_c, preferred_element_type=jnp.float32)
    tail_decay = jnp.exp(cumul_g[:, -1:] - cumul_g)
    weighted = (tail_decay[..., None] * driven_c.astype(jnp.float32)).astype(jnp.bfloat16)
    update = jnp.einsum(
        "csghp,csgn->cghpn", weighted, write_key, preferred_element_type=jnp.float32
    )
    span_ends = cumul_g[:, -1]
    span_decay = jnp.exp(span_ends)

    def advance(state_now, pieces):
        decay_now, update_now = pieces
        return (decay_now[:, :, None, None] * state_now + update_now, state_now)

    zero_state = jnp.zeros((groups_here, heads_group, head_width, N), jnp.float32)
    local_final, local_starts = lax.scan(advance, zero_state, (span_decay, update))
    before = jnp.cumsum(span_ends, axis=0) - span_ends
    device_decay = jnp.exp(jnp.sum(span_ends, axis=0))
    identity = (jnp.ones((groups_here, heads_group), jnp.float32), zero_state)
    incoming = entering((device_decay, local_final), "ctx", combine_states, identity)[1]
    read_wide = read_key.astype(jnp.float32)
    starts = jnp.exp(before)[:, :, :, None, None] * incoming[None] + local_starts
    carried = jnp.exp(cumul_g)[..., None] * jnp.einsum(
        "ctgn,cghpn->ctghp", read_wide, starts, precision=lax.Precision.HIGHEST
    )
    mixture = (
        within
        + carried
        + skip_gain.reshape(groups_here, heads_group)[None, None, :, :, None]
        * scaled.reshape(span_count, Q, groups_here, heads_group, head_width)
    )
    gate_vals = jax.nn.silu(gate_input.astype(jnp.float32)).reshape(
        span_count, Q, groups_here, heads_group * head_width
    )
    gated_out = mixture.reshape(span_count, Q, groups_here, heads_group * head_width) * gate_vals
    meansq = jnp.mean(gated_out * gated_out, axis=-1, keepdims=True)
    normed = (
        gated_out
        * lax.rsqrt(meansq + epsilon)
        * norm_gain.astype(jnp.float32).reshape(groups_here, heads_group * head_width)
    )
    return normed.reshape(tok_rows, inner_cols).astype(jnp.bfloat16)


def solution(mesh):
    in_specs = (
        P("ctx", "tp"),
        P("tp", "ctx"),
        P(None, "tp"),
        P("ctx", "tp"),
        P("ctx", "tp"),
        P("ctx", "tp"),
        P("tp"),
        P("tp"),
        P(None, "tp"),
        P("ctx"),
        P("tp"),
    )
    out_specs = P("ctx", "tp")
    return jax.shard_map(
        per_device, mesh=mesh, in_specs=in_specs, out_specs=out_specs, check_vma=False
    )
```

profile of v0, /device:TPU:486, one launch (start us, length us, event | category | flops | bytes accessed | tf_op | source)
XLA Modules:
  0.0 474.4 jit_solution(11549515616568934987)
XLA Ops:
  7.3 144.8 %all-gather.5.cloned.1.call-done = bf16[1024,2048]{0,1:T(8,128)(2,1)} async-done(((bf16[1024,32]{0,1:T(8,128)(2,1)}), bf16[1024,2048]{0,1:T(8,128)(2,1)}) %all-gather.5.cloned.1.call-update) | async-done | bytes 4194320 | tf_op jit(solution)/shard_map/all_gather | solution.py:71
  152.1 4.7 fusion.45
  158.2 36.8 %reduce-scatter.2.cloned.1.call-done = f32[128,256]{1,0:T(8,128)} async-done(((f32[128,2048]{1,0:T(8,128)}), f32[128,256]{1,0:T(8,128)}) %reduce-scatter.2.cloned.1.call-update) | async-done | bytes 131088 | tf_op jit(solution)/shard_map/reduce_scatter | solution.py:74
  195.7 1.3 collective-permute-start
  197.4 3.8 collective-permute-done
  201.2 1.2 multiply_convert_fusion.3
  203.5 73.1 %all-gather = bf16[64,1,1,16]{3,2,1,0:T(2,128)(2,1)S(1)} all-gather(bf16[1,1,1,16]{3,2,1,0:T(2,128)(2,1)S(1)} %get-tuple-element.102), channel_id=2, replica_groups=mesh['ctx'=64,'tp'=8] {'ctx'}, dimensions={0}, use_global_device_ids=true | all-gather | bytes 2080 | tf_op jit(solution)/shard_map/all_gather | solution.py:22
  277.0 115.8 %all-gather.7.cloned.1.call-done = bf16[1024,64,128]{2,1,0:T(8,128)(2,1)} async-done(((bf16[16,64,128]{2,1,0:T(8,128)(2,1)}), bf16[1024,64,128]{2,1,0:T(8,128)(2,1)}) %all-gather.7.cloned.1.call-update) | async-done | bytes 16777232 | tf_op jit(solution)/shard_map/all_gather | solution.py:22
  392.8 72.7 %while.3 = (s32[]{:T(128)}, f32[1,16,64,128]{3,2,1,0:T(8,128)S(1)}, s32[]{:T(128)}, bf16[64,1,16]{2,1,0:T(2,128)(2,1)S(1)}, bf16[64,1,16,64,128]{4,3,2,1,0:T(8,128)(2,1)}, /*index=5*/s32[]{:T(128)}, s32[]{:T(128)}, s32[]{:T(128)}) while((s32[]{:T(128)}, f32[1,16,64,128]{3,2,1,0:T(8,128)S(1)}, s32[]{:T(128)}, bf16[64,1,16]{2,1,0:T(2,128)(2,1)S(1)}, ...), condition=%wide.region_3.4_spmd, body=%wide.region_2.3_spmd.sunk | while | flops 393237 | bytes 1311015 | solution.py:36
  392.9 1.1 convert_add_fusion.2
  394.1 1.1 convert_add_fusion.2
  395.2 1.1 convert_add_fusion.2
  396.4 1.1 convert_add_fusion.2
  397.5 1.1 convert_add_fusion.2
  398.7 1.1 convert_add_fusion.2
  399.8 1.1 convert_add_fusion.2
  401.0 1.1 convert_add_fusion.2
  402.1 1.1 convert_add_fusion.2
  403.3 1.1 convert_add_fusion.2
  404.4 1.1 convert_add_fusion.2
  405.6 1.1 convert_add_fusion.2
  406.7 1.1 convert_add_fusion.2
  407.9 1.1 convert_add_fusion.2
  410.2 1.1 convert_add_fusion.2
  411.4 1.1 convert_add_fusion.2
  412.5 1.1 convert_add_fusion.2
  413.7 1.1 convert_add_fusion.2
  414.8 1.1 convert_add_fusion.2
  416.0 1.1 convert_add_fusion.2
  417.1 1.1 convert_add_fusion.2
  418.3 1.1 convert_add_fusion.2
  419.4 1.1 convert_add_fusion.2
  (155 shorter events, 51.4 us)
Async XLA Ops:
  6.5 145.6 %copy-start = (bf16[128,1024]{1,0:T(8,128)(2,1)S(1)}, bf16[128,1024]{1,0:T(8,128)(2,1)}, u32[]{:S(2)}) copy-start(bf16[128,1024]{1,0:T(8,128)(2,1)} %param.13) | copy-start | bytes 786436
  6.5 151.0 %copy-start.3 = (f32[128,16]{0,1:T(8,128)S(1)}, f32[128,16]{0,1:T(8,128)}, u32[]{:S(2)}) copy-start(f32[128,16]{0,1:T(8,128)} %param.18) | copy-start | bytes 24580
  6.5 151.0 %copy-start.7 = (f32[16]{0:T(128)S(1)}, f32[16]{0:T(128)}, u32[]{:S(2)}) copy-start(f32[16]{0:T(128)} %param.19) | copy-start | bytes 196
  6.5 151.4 %copy-start.5 = (f32[4,256]{1,0:T(4,128)S(1)}, f32[4,256]{1,0:T(4,128)}, u32[]{:S(2)}) copy-start(f32[4,256]{1,0:T(4,128)} %param.15) | copy-start | bytes 12292
  6.5 151.5 %copy-start.4 = (bf16[16,1024]{1,0:T(8,128)(2,1)S(1)}, bf16[16,1024]{1,0:T(8,128)(2,1)}, u32[]{:S(2)}) copy-start(bf16[16,1024]{1,0:T(8,128)(2,1)} %param.21) | copy-start | bytes 98308
  6.5 190.4 %copy-start.2 = (bf16[128,1024]{1,0:T(8,128)(2,1)S(1)}, bf16[128,1024]{1,0:T(8,128)(2,1)}, u32[]{:S(2)}) copy-start(bf16[128,1024]{1,0:T(8,128)(2,1)} %param.16) | copy-start | bytes 786436
  6.6 145.6 %all-gather.5.cloned.1.call-start = ((), (), s32[]{:S(2)}) async-start(), calls=%async_computation.1 | async-start | bytes 4259840 | tf_op jit(solution)/shard_map/all_gather | solution.py:71
  7.3 196.2 %copy-start.6 = (bf16[1024]{0:T(1024)(128)(2,1)S(1)}, bf16[1024]{0:T(1024)(128)(2,1)}, u32[]{:S(2)}) copy-start(bf16[1024]{0:T(1024)(128)(2,1)} %param.23) | copy-start | bytes 6148
  7.3 187.7 %reduce-scatter.2.cloned.1.call-start = ((), (), s32[]{:S(2)}) async-start(), calls=%async_computation.2 | async-start | bytes 1179648 | tf_op jit(solution)/shard_map/reduce_scatter | solution.py:74
  156.8 236.0 %all-gather.7.cloned.1.call-start = ((), (), s32[]{:S(2)}) async-start(), calls=%async_computation.3 | async-start | bytes 17039360 | tf_op jit(solution)/shard_map/all_gather | solution.py:22
  195.7 5.5 %collective-permute-start = (f32[3,256]{1,0:T(4,128)S(1)}, f32[3,256]{1,0:T(4,128)S(1)}, u32[]{:S(2)}, u32[]{:S(2)}) collective-permute-start(f32[3,256]{1,0:T(4,128)S(1)} %slice.45), channel_id=1, source_target_pairs={{0,8},{8,16},{16,24},{24,32},{32,40},{40,48},{48,56},{56,64},{64,7... | collective-permute-start | bytes 9224 | tf_op jit(solution)/shard_map/ppermute | solution.py:16
  392.8 73.2 %copy-start.8 = (f32[16]{0:T(128)S(1)}, f32[16]{0:T(128)}, u32[]{:S(2)}) copy-start(f32[16]{0:T(128)} %param.20) | copy-start | bytes 196
  392.8 73.9 %copy-start.1 = (bf16[128,1024]{1,0:T(8,128)(2,1)S(1)}, bf16[128,1024]{1,0:T(8,128)(2,1)}, u32[]{:S(2)}) copy-start(bf16[128,1024]{1,0:T(8,128)(2,1)} %param.17) | copy-start | bytes 786436
Sparse Core Ops, SparseCore 0:
  10.3 141.7 all-gather.4
  156.9 37.9 reduce-scatter.1
  203.6 189.1 all-gather.6
where the time goes:
time: 477 us; the launch traced here: 474 us
  waiting for transfers between devices  302 us (63%)
  other arithmetic  73.5 us (15%)
  blocking collectives  73.1 us (15%)
  between operations  14 us (3%)
  matrix products  6.86 us (1%)
    all_gather x1, waiting for transfers between devices, per_device(): lax.all_gather(select_weight, 'ctx', axis=1, tiled=True)  145 us
    all_gather x1, waiting for transfers between devices, entering(): lax.all_gather(a.astype(kind), axis)  116 us
    all_gather x1, blocking collectives, entering(): lax.all_gather(a.astype(kind), axis)  73.1 us
    add x63, other arithmetic, combine_states(): latter[0][:, :, None, None] * earlier[1] + latter[1]  70.1 us
    reduce_scatter x1, waiting for transfers between devices, per_device(): lax.psum_scatter(partial_value, 'tp', scatter_dimension=1, tiled=True)  36.8 us
  transfers between devices with their start and end apart: 4, of which 4 were waited for; matrix products, arithmetic and copies ran while one was open for 0% of the time, Pallas kernels for 0%

commit v1 on v0

v1 whole, which is shorter than its diff:
```python
import jax
import jax.numpy as jnp
from jax import lax
from jax.sharding import Mesh, PartitionSpec as P

N = 128
Q = 128
HALO = 16
EXTRA = 128
CTX = ("x", "zh", "zl")
TP = ("y", "core")

epsilon = 1e-05
bf16 = jnp.bfloat16
f32 = jnp.float32


def swap(blocks, axis):
    return lax.all_to_all(blocks, axis, 0, 0, tiled=True)


def share(block, axis):
    peers = lax.axis_size(axis)
    return swap(jnp.broadcast_to(block[None], (peers,) + block.shape), axis)


def split3(v):
    hi = lax.reduce_precision(v, 8, 7)
    mid = lax.reduce_precision(v - hi, 8, 7)
    return jnp.stack([hi, mid, v - hi - mid]).astype(bf16)


def with_logs(block, logs):
    parts = split3(logs)
    rows = block.shape[0]
    tail = jnp.pad(parts, ((0, rows - 3), (0, EXTRA - logs.shape[0])))
    return jnp.concatenate([block, tail], axis=1)


def logs_of(blocks, width, heads):
    return blocks[:, 0:3, width : width + heads].astype(f32).sum(1)


def per_device(
    hidden_states,
    select_weight,
    conv_taps,
    inner_input,
    gate_input,
    step_size,
    decay_rate,
    skip_gain,
    tenant_scale,
    tenant_index,
    norm_gain,
):
    heads = decay_rate.shape[0]
    width = inner_input.shape[1]
    head_width = width // heads
    x, zh, zl = (lax.axis_index(a) for a in CTX)
    n_ctx = lax.axis_size(CTX)
    quad = lax.axis_size("zl")
    n_part = N // quad

    def lanes(v):
        return jnp.repeat(v, head_width, axis=-1)

    halo = lax.ppermute(hidden_states[Q - HALO :], CTX, [(i, i + 1) for i in range(n_ctx - 1)])
    rows_q = lax.all_gather(
        jnp.concatenate([halo, hidden_states], axis=0), "zl", axis=0, tiled=True
    )

    w_t = select_weight.T
    w_zh = share(w_t, "zh").reshape(-1, w_t.shape[1])
    w_all = share(w_zh, "x").reshape(-1, w_t.shape[1])

    seg_scale = lax.dynamic_index_in_dim(tenant_scale, tenant_index[0], 0, True).astype(f32)
    scaled = inner_input.astype(f32) * seg_scale
    driven = (scaled * lanes(step_size)).astype(bf16)
    cum = jnp.cumsum(-step_size * decay_rate[None, :], axis=0)
    weighted = (lanes(jnp.exp(cum[-1:] - cum)) * driven.astype(f32)).astype(bf16)
    weighted_q = lax.all_gather(with_logs(weighted, cum[-1]), "zl")

    part = lax.dot_general(
        w_all, rows_q, (((1,), (1,)), ((), ())), preferred_element_type=f32
    ).astype(bf16)
    raw = swap(part.reshape(lax.axis_size(TP), 2 * n_part, -1), TP).astype(f32).sum(0)
    taps = conv_taps.shape[0]
    own_taps = lax.dynamic_index_in_dim(
        conv_taps.reshape(taps, 2, quad, n_part), zl, 2, False
    ).reshape(taps, 2 * n_part)
    raw = raw.reshape(2 * n_part, quad, Q + HALO)
    summed = 0.0
    for k in range(taps):
        at = HALO - (taps - 1) + k
        summed = summed + own_taps[k][:, None, None] * raw[:, :, at : at + Q]
    keys = jnp.transpose(jax.nn.silu(summed).astype(bf16), (1, 0, 2))
    write_t, read_t = keys[:, :n_part], keys[:, n_part:]

    update = jnp.einsum(
        "bns,bsq->bnq", write_t, weighted_q[:, :, :width], preferred_element_type=f32
    )
    ends = logs_of(weighted_q, width, heads)
    state = jnp.zeros_like(update[0])
    starts = []
    for b in range(quad):
        starts.append(state)
        state = lanes(jnp.exp(ends[b]))[None] * state + update[b]

    def entering(total, logs, axis, place):
        got = share(with_logs(total.astype(bf16), logs), axis)
        got_logs = logs_of(got, width, heads)
        got = got[:, :, :width].astype(f32)
        acc, kept, all_acc = jnp.zeros_like(total), jnp.zeros_like(total), None
        log_kept = jnp.zeros_like(logs)
        log_acc = jnp.zeros_like(logs)
        for i in range(lax.axis_size(axis)):
            kept = jnp.where(place == i, acc, kept)
            log_kept = jnp.where(place == i, log_acc, log_kept)
            acc = lanes(jnp.exp(got_logs[i]))[None] * acc + got[i]
            log_acc = log_acc + got_logs[i]
        return kept, log_kept, acc, log_acc

    before, log_before, row, log_row = entering(state, ends.sum(0), "zh", zh)
    carry, _, _, _ = entering(row, log_row, "x", x)
    carry = lanes(jnp.exp(log_before))[None] * carry + before
    sent = []
    log_now = jnp.zeros_like(log_before)
    for b in range(quad):
        now = (starts[b] + lanes(jnp.exp(log_now))[None] * carry).astype(bf16)
        log_now = log_now + ends[b]
        sent.append(jnp.concatenate([now, write_t[b], read_t[b]], axis=1))
    own = swap(jnp.stack(sent), "zl").reshape(N, width + 2 * Q)
    start, write_t, read_t = own[:, :width], own[:, width : width + Q], own[:, width + Q :]

    scores = lax.dot_general(
        read_t, write_t, (((0,), (0,)), ((), ())), preferred_element_type=f32
    )
    cum_t = cum.T
    lag = cum_t[:, :, None] - cum_t[:, None, :]
    causal = jnp.tril(jnp.ones((Q, Q), dtype=bool))
    weights = jnp.where(causal, scores[None] * jnp.exp(jnp.where(causal, lag, 0.0)), 0.0).astype(bf16)
    within = jnp.einsum(
        "hts,shp->thp", weights, driven.reshape(Q, heads, head_width), preferred_element_type=f32
    ).reshape(Q, width)
    carried = lanes(jnp.exp(cum)) * lax.dot_general(
        read_t, start, (((0,), (0,)), ((), ())), preferred_element_type=f32
    )
    mixture = within + carried + lanes(skip_gain)[None] * scaled
    gated = mixture * jax.nn.silu(gate_input.astype(f32))
    meansq = jnp.mean(gated * gated, axis=-1, keepdims=True)
    normed = gated * lax.rsqrt(meansq + epsilon) * norm_gain.astype(f32)[None]
    return normed.astype(bf16)


def solution(mesh):
    fine = Mesh(mesh.devices.reshape(4, 4, 4, 4, 2), CTX + TP)
    in_specs = (
        P(CTX, TP),
        P(TP, CTX),
        P(None, TP),
        P(CTX, TP),
        P(CTX, TP),
        P(CTX, TP),
        P(TP),
        P(TP),
        P(None, TP),
        P(CTX),
        P(TP),
    )
    return jax.shard_map(
        per_device, mesh=fine, in_specs=in_specs, out_specs=P(CTX, TP), check_vma=False
    )
```

time: 477 us -> 194 us (0.41)
  the two profiles are of different devices: /device:TPU:486 before, /device:TPU:32 now
where the time goes in v1:
time: 194 us
  waiting for transfers between devices  89.8 us (46%)
  blocking collectives  38.3 us (20%)
  starting transfers between devices  32 us (16%)
  between operations  14.4 us (7%)
  local copies, waits for them, and re-layouts  9.06 us (5%)
  other arithmetic  6.47 us (3%)
  matrix products  3.55 us (2%)
    all_to_all x5, waiting for transfers between devices, swap(): return lax.all_to_all(blocks, axis, 0, 0, tiled=True)  55.4 us
    all_to_all x1, blocking collectives, swap(): return lax.all_to_all(blocks, axis, 0, 0, tiled=True)  38.3 us
    all_gather x1, waiting for transfers between devices, per_device(): lax.all_gather(jnp.concatenate([halo, hidden_states], axis=0), 'zl', axis...  29.6 us
    all_to_all x5, starting transfers between devices, swap(): return lax.all_to_all(blocks, axis, 0, 0, tiled=True)  28.1 us
    ppermute x1, waiting for transfers between devices, per_device(): lax.ppermute(hidden_states[Q - HALO:], CTX, [(i, i + 1) for i in range(n_...  4.82 us
  transfers between devices with their start and end apart: 8, of which 7 were waited for; matrix products, arithmetic and copies ran while one was open for 2% of the time, Pallas kernels for 0%

profile of v1, /device:TPU:32, one launch (start us, length us, event | category | flops | bytes accessed | tf_op | source)
XLA Modules:
  0.0 193.6 jit_solution(10303314281404578227)
XLA Ops:
  6.5 0.8 negate_multiply_fusion
  8.9 0.7 dynamic-slice_convert_fusion
  9.8 0.7 pad_maximum_fusion.1
  10.7 3.8 %collective-permute-start = (bf16[16,1024]{1,0:T(8,128)(2,1)S(1)}, bf16[16,1024]{1,0:T(8,128)(2,1)S(1)}, u32[]{:S(2)}, u32[]{:S(2)}) collective-permute-start(bf16[16,1024]{1,0:T(8,128)(2,1)S(1)} %slice.178), channel_id=1, source_target_pairs={{0,8},{8,16},{16,24},{24,32},{32,40},{40,48},{48,56},{56,64},{64,7... | collective-permute-start | bytes 98312 | tf_op jit(solution)/shard_map/ppermute | solution.py:68
  14.5 4.8 %collective-permute-done = bf16[16,1024]{1,0:T(8,128)(2,1)S(1)} collective-permute-done((bf16[16,1024]{1,0:T(8,128)(2,1)S(1)}, bf16[16,1024]{1,0:T(8,128)(2,1)S(1)}, u32[]{:S(2)}, u32[]{:S(2)}) %collective-permute-start) | collective-permute-done | bytes 32800 | tf_op jit(solution)/shard_map/ppermute | solution.py:68
  19.3 0.7 pad_maximum_fusion.2
  20.1 38.3 %all_to_all.30 = bf16[4,32,1024]{2,1,0:T(8,128)(2,1)S(1)} all-to-all(bf16[4,32,1024]{2,1,0:T(8,128)(2,1)S(1)} %broadcast_in_dim.108), channel_id=1, replica_groups=mesh['x'=4,'zh'=4,'zl'=4,'y'=4,'core'=2] {'zh'}, dimensions={0} | all-to-all | bytes 524288 | tf_op jit(solution)/shard_map/all_to_all | solution.py:19
  58.4 1.1 broadcast_in_dim.110
  59.5 4.4 %all-to-all-start.1 = ((bf16[4,128,1024]{2,1,0:T(8,128)(2,1)}), bf16[4,128,1024]{2,1,0:T(8,128)(2,1)S(1)}, u32[]{:S(2)}, u32[]{:S(2)}) async-start(bf16[4,128,1024]{2,1,0:T(8,128)(2,1)} %broadcast_in_dim.110), calls=%async_computation.1 | async-start | bytes 2097152 | tf_op jit(solution)/shard_map/all_to_all | solution.py:19
  64.3 0.7 convert_reduce_fusion.2
  65.7 9.7 %all-to-all-done.1 = bf16[4,128,1024]{2,1,0:T(8,128)(2,1)S(1)} async-done(((bf16[4,128,1024]{2,1,0:T(8,128)(2,1)}), bf16[4,128,1024]{2,1,0:T(8,128)(2,1)S(1)}, u32[]{:S(2)}, u32[]{:S(2)}) %all-to-all-start.1) | async-done | bytes 1048608 | tf_op jit(solution)/shard_map/all_to_all | solution.py:19
  75.3 29.6 %all-gather.4.cloned.1.call-done = bf16[576,1024]{1,0:T(8,128)(2,1)} async-done(((bf16[144,1024]{1,0:T(8,128)(2,1)}), bf16[576,1024]{1,0:T(8,128)(2,1)}) %all-gather.4.cloned.1.call-update) | async-done | bytes 1179664 | tf_op jit(solution)/shard_map/all_gather | solution.py:69
  104.9 2.1 %fusion = bf16[512,576]{0,1:T(8,128)(2,1)S(1)} fusion(bf16[576,1024]{1,0:T(8,128)(2,1)} %all-gather.4.cloned.1.call-done, bf16[512,1024]{1,0:T(8,128)(2,1)S(1)} %bitcast.194), kind=kOutput, calls=%fused_computation.2 | convolution fusion | flops 604274688 | bytes 2818048 | tf_op jit(solution)/shard_map/dot_general | solution.py:84
  107.0 1.1 copy.25
  108.1 4.3 %all-to-all-start.2 = ((bf16[8,64,576]{2,1,0:T(8,128)(2,1)}), bf16[8,64,576]{2,1,0:T(8,128)(2,1)S(1)}, u32[]{:S(2)}, u32[]{:S(2)}) async-start(bf16[8,64,576]{2,1,0:T(8,128)(2,1)} %bitcast.15), calls=%async_computation.2 | async-start | bytes 1310720 | tf_op jit(solution)/shard_map/all_to_all | solution.py:19
  112.4 11.7 %all-to-all-done.2 = bf16[8,64,576]{2,1,0:T(8,128)(2,1)S(1)} async-done(((bf16[8,64,576]{2,1,0:T(8,128)(2,1)}), bf16[8,64,576]{2,1,0:T(8,128)(2,1)S(1)}, u32[]{:S(2)}, u32[]{:S(2)}) %all-to-all-start.2) | async-done | bytes 589856 | tf_op jit(solution)/shard_map/all_to_all | solution.py:19
  124.2 0.2 reshape.139
  124.4 0.3 fusion.76
  124.9 0.6 copy-done
  125.5 0.3 fusion.4
  125.8 0.7 broadcast_in_dim.111
  126.5 11.0 %all-to-all-start.3 = ((bf16[4,32,1152]{2,1,0:T(8,128)(2,1)}), bf16[4,32,1152]{2,1,0:T(8,128)(2,1)S(1)}, u32[]{:S(2)}, u32[]{:S(2)}) async-start(bf16[4,32,1152]{2,1,0:T(8,128)(2,1)} %broadcast_in_dim.111), calls=%async_computation.3 | async-start | bytes 589824 | tf_op jit(solution)/shard_map/all_to_all | solution.py:19
  137.8 21.4 %all-to-all-done.3 = bf16[4,32,1152]{2,1,0:T(8,128)(2,1)S(1)} async-done(((bf16[4,32,1152]{2,1,0:T(8,128)(2,1)}), bf16[4,32,1152]{2,1,0:T(8,128)(2,1)S(1)}, u32[]{:S(2)}, u32[]{:S(2)}) %all-to-all-start.3) | async-done | bytes 294944 | tf_op jit(solution)/shard_map/all_to_all | solution.py:19
  160.0 0.7 broadcast_in_dim.117
  160.8 4.2 %all-to-all-start.4 = ((bf16[4,32,1152]{2,1,0:T(8,128)(2,1)}), bf16[4,32,1152]{2,1,0:T(8,128)(2,1)S(1)}, u32[]{:S(2)}, u32[]{:S(2)}) async-start(bf16[4,32,1152]{2,1,0:T(8,128)(2,1)} %broadcast_in_dim.117), calls=%async_computation.4 | async-start | bytes 589824 | tf_op jit(solution)/shard_map/all_to_all | solution.py:19
  165.2 6.7 %all-to-all-done.4 = bf16[4,32,1152]{2,1,0:T(8,128)(2,1)S(1)} async-done(((bf16[4,32,1152]{2,1,0:T(8,128)(2,1)}), bf16[4,32,1152]{2,1,0:T(8,128)(2,1)S(1)}, u32[]{:S(2)}, u32[]{:S(2)}) %all-to-all-start.4) | async-done | bytes 294944 | tf_op jit(solution)/shard_map/all_to_all | solution.py:19
  172.6 0.8 pad_maximum_fusion
  173.4 4.1 %all-to-all-start.5 = ((bf16[4,32,1280]{2,1,0:T(8,128)(2,1)}), bf16[4,32,1280]{2,1,0:T(8,128)(2,1)S(1)}, u32[]{:S(2)}, u32[]{:S(2)}) async-start(bf16[4,32,1280]{2,1,0:T(8,128)(2,1)} %pad_maximum_fusion), calls=%async_computation.5 | async-start | bytes 655360 | tf_op jit(solution)/shard_map/all_to_all | solution.py:19
  178.4 5.9 %all-to-all-done.5 = bf16[4,32,1280]{2,1,0:T(8,128)(2,1)S(1)} async-done(((bf16[4,32,1280]{2,1,0:T(8,128)(2,1)}), bf16[4,32,1280]{2,1,0:T(8,128)(2,1)S(1)}, u32[]{:S(2)}, u32[]{:S(2)}) %all-to-all-start.5) | async-done | bytes 327712 | tf_op jit(solution)/shard_map/all_to_all | solution.py:19
  184.5 0.5 fusion.6
  185.4 0.5 multiply_reduce_fusion
  185.9 0.8 multiply_convert_fusion
  (104 shorter events, 5.7 us)
Async XLA Ops:
  6.5 2.1 %copy-start.4 = (f32[128,16]{0,1:T(8,128)S(1)}, f32[128,16]{0,1:T(8,128)}, u32[]{:S(2)}) copy-start(f32[128,16]{0,1:T(8,128)} %param.16) | copy-start | bytes 24580
  6.5 57.8 %all-gather.6.cloned.1.call-start = ((), (), s32[]{:S(2)}) async-start(), calls=%async_computation.7 | async-start | bytes 1474560 | tf_op jit(solution)/shard_map/all_gather | solution.py:82
  7.8 1.9 copy-start.2
  9.7 1.0 copy-start.1
  9.8 10.2 %copy-start.3 = (bf16[1024,32]{0,1:T(8,128)(2,1)S(1)}, bf16[1024,32]{0,1:T(8,128)(2,1)}, u32[]{:S(2)}) copy-start(bf16[1024,32]{0,1:T(8,128)(2,1)} %param.12) | copy-start | bytes 196612
  10.6 94.3 %all-gather.4.cloned.1.call-start = ((), (), s32[]{:S(2)}) async-start(), calls=%async_computation.6 | async-start | bytes 1474560 | tf_op jit(solution)/shard_map/all_gather | solution.py:69
  10.7 8.7 %collective-permute-start = (bf16[16,1024]{1,0:T(8,128)(2,1)S(1)}, bf16[16,1024]{1,0:T(8,128)(2,1)S(1)}, u32[]{:S(2)}, u32[]{:S(2)}) collective-permute-start(bf16[16,1024]{1,0:T(8,128)(2,1)S(1)} %slice.178), channel_id=1, source_target_pairs={{0,8},{8,16},{16,24},{24,32},{32,40},{40,48},{48,56},{56,64},{64,7... | collective-permute-start | bytes 98312 | tf_op jit(solution)/shard_map/ppermute | solution.py:68
  59.5 4.4 %copy-start.5 = (f32[4,256]{1,0:T(4,128)S(1)}, f32[4,256]{1,0:T(4,128)}, u32[]{:S(2)}) copy-start(f32[4,256]{1,0:T(4,128)} %param.13) | copy-start | bytes 12292
  59.5 15.8 %all-to-all-start.1 = ((bf16[4,128,1024]{2,1,0:T(8,128)(2,1)}), bf16[4,128,1024]{2,1,0:T(8,128)(2,1)S(1)}, u32[]{:S(2)}, u32[]{:S(2)}) async-start(bf16[4,128,1024]{2,1,0:T(8,128)(2,1)} %broadcast_in_dim.110), calls=%async_computation.1 | async-start | bytes 2097152 | tf_op jit(solution)/shard_map/all_to_all | solution.py:19
  108.1 16.0 %all-to-all-start.2 = ((bf16[8,64,576]{2,1,0:T(8,128)(2,1)}), bf16[8,64,576]{2,1,0:T(8,128)(2,1)S(1)}, u32[]{:S(2)}, u32[]{:S(2)}) async-start(bf16[8,64,576]{2,1,0:T(8,128)(2,1)} %bitcast.15), calls=%async_computation.2 | async-start | bytes 1310720 | tf_op jit(solution)/shard_map/all_to_all | solution.py:19
  124.2 1.3 copy-start
  126.5 32.7 %all-to-all-start.3 = ((bf16[4,32,1152]{2,1,0:T(8,128)(2,1)}), bf16[4,32,1152]{2,1,0:T(8,128)(2,1)S(1)}, u32[]{:S(2)}, u32[]{:S(2)}) async-start(bf16[4,32,1152]{2,1,0:T(8,128)(2,1)} %broadcast_in_dim.111), calls=%async_computation.3 | async-start | bytes 589824 | tf_op jit(solution)/shard_map/all_to_all | solution.py:19
  160.8 11.1 %all-to-all-start.4 = ((bf16[4,32,1152]{2,1,0:T(8,128)(2,1)}), bf16[4,32,1152]{2,1,0:T(8,128)(2,1)S(1)}, u32[]{:S(2)}, u32[]{:S(2)}) async-start(bf16[4,32,1152]{2,1,0:T(8,128)(2,1)} %broadcast_in_dim.117), calls=%async_computation.4 | async-start | bytes 589824 | tf_op jit(solution)/shard_map/all_to_all | solution.py:19
  173.4 10.9 %all-to-all-start.5 = ((bf16[4,32,1280]{2,1,0:T(8,128)(2,1)}), bf16[4,32,1280]{2,1,0:T(8,128)(2,1)S(1)}, u32[]{:S(2)}, u32[]{:S(2)}) async-start(bf16[4,32,1280]{2,1,0:T(8,128)(2,1)} %pad_maximum_fusion), calls=%async_computation.5 | async-start | bytes 655360 | tf_op jit(solution)/shard_map/all_to_all | solution.py:19
  177.5 0.7 copy-start.7
  177.5 0.8 copy-start.6
  184.5 1.0 copy-start.8
Sparse Core Ops, SparseCore 0:
  10.7 52.3 all-gather.5
  65.2 39.6 all-gather.3

commit v2 on v1

v2 whole, which is shorter than its diff:
```python
import functools

import jax
import jax.numpy as jnp
from jax import lax
from jax.experimental import pallas as pl
from jax.experimental.pallas import tpu as pltpu
from jax.sharding import Mesh, PartitionSpec as P

N = 128
Q = 128
QUAD = 4
HALO = 16
LOG_ROWS = 16
CTX = ("x", "zh", "zl")
TP = ("y", "core")

epsilon = 1e-05
bf16 = jnp.bfloat16
f32 = jnp.float32
EXACT = lax.Precision.HIGHEST

VMEM = pl.BlockSpec(memory_space=pltpu.VMEM)
SMEM = pl.BlockSpec(memory_space=pltpu.SMEM)


def swap(blocks, axis):
    return lax.all_to_all(blocks, axis, 0, 0, tiled=True)


def share(block, axis):
    peers = lax.axis_size(axis)
    return swap(jnp.broadcast_to(block[None], (peers,) + block.shape), axis)


def shape(dims, kind):
    return jax.ShapeDtypeStruct(dims, kind)


def kernel_call(body, outs, place, args, scratch=(), flops=1_000_000):
    return pl.pallas_call(
        body,
        out_shape=outs,
        in_specs=[SMEM] + [VMEM] * len(args),
        out_specs=jax.tree.map(lambda _: VMEM, outs),
        scratch_shapes=scratch,
        compiler_params=pltpu.CompilerParams(vmem_limit_bytes=32 * 1024 * 1024),
        cost_estimate=pl.CostEstimate(flops=flops, bytes_accessed=1_000_000, transcendentals=0),
    )(place, *args)


def expand(columns, head_width):
    heads = columns.shape[1]
    shape2 = (heads, heads * head_width)
    head = lax.broadcasted_iota(jnp.int32, shape2, 0)
    lane = lax.broadcasted_iota(jnp.int32, shape2, 1)
    first = head * head_width
    onehot = jnp.where((lane >= first) & (lane < first + head_width), 1.0, 0.0)
    return jnp.dot(columns, onehot, precision=EXACT, preferred_element_type=f32)


def log_rows(row):
    hi = row.astype(bf16).astype(f32)
    mid = (row - hi).astype(bf16).astype(f32)
    low = row - hi - mid
    at = lax.broadcasted_iota(jnp.int32, (LOG_ROWS, row.shape[1]), 0)
    rows = jnp.where(at == 0, hi, jnp.where(at == 1, mid, jnp.where(at == 2, low, 0.0)))
    return rows.astype(bf16)


def log_row(rows):
    return jnp.sum(rows.astype(f32), axis=0, keepdims=True)


def scaled_by_tenant(tenant, inner_ref, scale_ref):
    row = lax.broadcasted_iota(jnp.int32, scale_ref.shape, 0)
    chosen = jnp.where(row == tenant, scale_ref[...].astype(f32), 0.0)
    return inner_ref[...].astype(f32) * jnp.sum(chosen, axis=0, keepdims=True)


def drive_kernel(
    place, inner, scale, step, decay, halo, driven, cum, cum_t, p0, p1, p2, p3, ext
):
    zl, tenant = place[2], place[3]
    width = inner.shape[1]
    head_width = width // step.shape[1]
    part_width = width // QUAD
    logs = -step[...] * decay[...]
    rows = lax.broadcasted_iota(jnp.int32, (Q, Q), 0)
    cols = lax.broadcasted_iota(jnp.int32, (Q, Q), 1)
    lower = jnp.where(rows >= cols, 1.0, 0.0)
    so_far = jnp.dot(lower, logs, precision=EXACT, preferred_element_type=f32)
    cum[...] = so_far
    cum_t[...] = lax.dot_general(
        logs, lower, (((0,), (1,)), ((), ())), precision=EXACT, preferred_element_type=f32
    )
    end = so_far[Q - 1 :]
    drive = (scaled_by_tenant(tenant, inner, scale) * expand(step[...], head_width)).astype(bf16)
    driven[...] = drive
    tail = expand(jnp.exp(end - so_far), head_width)
    ext[:Q] = (tail * drive.astype(f32)).astype(bf16)
    ext[Q : Q + LOG_ROWS] = log_rows(expand(end, head_width))
    ext[Q + LOG_ROWS :] = halo[...]
    for s, part in enumerate((p0, p1, p2, p3)):
        to = lax.rem(zl + s, QUAD)
        part[: Q + LOG_ROWS] = ext[
            : Q + LOG_ROWS, pl.ds(pl.multiple_of(to * part_width, part_width), part_width)
        ]
        for q in range(QUAD):
            at = Q + LOG_ROWS + q * HALO
            part[at : at + HALO] = ext[
                Q + LOG_ROWS :, q * part_width : (q + 1) * part_width
            ]


def project_kernel(place, w, h0, h1, h2, h3, p0, p1, p2, p3, out, halo):
    zl = place[2]
    at = Q + LOG_ROWS
    rows = [p[at:] for p in (p0, p1, p2, p3)]
    mine = rows[3]
    for s in range(QUAD - 1):
        mine = jnp.where(zl == s, rows[s], mine)
    part_width = mine.shape[1]
    halo[...] = jnp.zeros_like(halo)
    for q in range(QUAD):
        halo[Q - HALO :, q * part_width : (q + 1) * part_width] = mine[q * HALO : (q + 1) * HALO]
    for s, h in enumerate((h0, h1, h2, h3, halo)):
        out[:, s * Q : (s + 1) * Q] = lax.dot_general(
            w[...], h[...], (((1,), (1,)), ((), ())), preferred_element_type=f32
        ).astype(bf16)


def keys_kernel(place, parts, taps, out, selected):
    zl = place[2]
    raw = parts[0].astype(f32)
    for i in range(1, parts.shape[0]):
        raw = raw + parts[i].astype(f32)
    blocks = [raw[:, s * Q : (s + 1) * Q] for s in range(QUAD + 1)]
    lane = lax.broadcasted_iota(jnp.int32, blocks[0].shape, 1)
    n_taps = taps.shape[1]
    for s in range(QUAD):
        before = jnp.where(zl == s, blocks[QUAD], blocks[(s + 1) % QUAD])
        summed = taps[:, n_taps - 1 :] * blocks[s]
        for d in range(1, n_taps):
            moved = jnp.where(
                lane < d, pltpu.roll(before, d, 1), pltpu.roll(blocks[s], d, 1)
            )
            summed = summed + taps[:, n_taps - 1 - d : n_taps - d] * moved
        selected[:, s * Q : (s + 1) * Q] = (summed / (1.0 + jnp.exp(-summed))).astype(bf16)
    n_part = out.shape[1]
    for b in range(QUAD):
        s = lax.rem(zl - b + QUAD, QUAD)
        block = selected[:, pl.ds(pl.multiple_of(s * Q, Q), Q)]
        for to in range(QUAD):
            out[to, :, b * Q : (b + 1) * Q] = block[:n_part]
        out[b, :, QUAD * Q :] = block[n_part:]


def update_kernel(place, keys, p0, p1, p2, p3, starts, ends, total, update, logs):
    zl = place[2]
    for s, part in enumerate((p0, p1, p2, p3)):
        b = lax.rem(zl - s + QUAD, QUAD)
        block = keys[:, pl.ds(pl.multiple_of(b * Q, Q), Q)]
        update[b] = jnp.dot(block, part[:Q], preferred_element_type=f32)
        logs[b] = jnp.broadcast_to(log_row(part[Q : Q + LOG_ROWS]), logs.shape[1:])
    state = jnp.zeros(update.shape[1:], f32)
    all_logs = jnp.zeros((1, update.shape[2]), f32)
    for b in range(QUAD):
        starts[b] = state
        log = logs[b][:1]
        ends[b : b + 1] = log
        state = jnp.exp(log) * state + update[b]
        all_logs = all_logs + log
    total[:N] = state.astype(bf16)
    total[N:] = log_rows(all_logs)


def entering(got, place):
    acc = kept = jnp.zeros((N, got.shape[2]), f32)
    log_acc = log_kept = jnp.zeros((1, got.shape[2]), f32)
    for i in range(got.shape[0]):
        kept = jnp.where(place == i, acc, kept)
        log_kept = jnp.where(place == i, log_acc, log_kept)
        log = log_row(got[i, N:])
        acc = jnp.exp(log) * acc + got[i, :N].astype(f32)
        log_acc = log_acc + log
    return kept, log_kept, acc, log_acc


def row_kernel(place, got, before, log_before, total):
    kept, log_kept, acc, log_acc = entering(got, place[1])
    before[...] = kept
    log_before[...] = log_kept
    acc, log_acc = acc.astype(bf16), log_rows(log_acc)
    for i in range(total.shape[0]):
        total[i, :N] = acc
        total[i, N:] = log_acc


def states_kernel(place, got, before, log_before, starts, ends, out):
    carry = entering(got, place[0])[0]
    carry = jnp.exp(log_before[...]) * carry + before[...]
    log_now = jnp.zeros_like(log_before[...])
    for b in range(QUAD):
        out[b] = (starts[b] + jnp.exp(log_now) * carry).astype(bf16)
        log_now = log_now + ends[b : b + 1]


def within_kernel(place, keys, driven, cum, cum_t, inner, scale, skip, out):
    zl, tenant = place[2], place[3]
    read_t = keys[:, QUAD * Q :]
    write_t = keys[:, pl.ds(pl.multiple_of(zl * Q, Q), Q)]
    scores = lax.dot_general(
        read_t, write_t, (((0,), (0,)), ((), ())), preferred_element_type=f32
    )
    rows = lax.broadcasted_iota(jnp.int32, (Q, Q), 0)
    cols = lax.broadcasted_iota(jnp.int32, (Q, Q), 1)
    causal = rows >= cols
    heads = cum.shape[1]
    head_width = driven.shape[1] // heads
    per_tile = Q // head_width
    skipped = expand(skip[...], head_width) * scaled_by_tenant(tenant, inner, scale)
    for tile in range(heads // per_tile):
        at = slice(tile * Q, (tile + 1) * Q)
        mixed = None
        for i in range(per_tile):
            h = tile * per_tile + i
            lag = cum[:, h : h + 1] - cum_t[h : h + 1]
            weights = jnp.where(causal, scores * jnp.exp(jnp.where(causal, lag, 0.0)), 0.0)
            summed = jnp.dot(weights.astype(bf16), driven[:, at], preferred_element_type=f32)
            mixed = summed if mixed is None else jnp.where(cols < i * head_width, mixed, summed)
        out[:, at] = mixed + skipped[:, at]


def output_kernel(place, keys, start, cum, mixed, gate, gain, out):
    read_t = keys[:, QUAD * Q :]
    head_width = out.shape[1] // cum.shape[1]
    grown = expand(jnp.exp(cum[...]), head_width)
    part_width = start.shape[2]
    gated = []
    squares = jnp.zeros((Q, 1), f32)
    for q in range(QUAD):
        at = slice(q * part_width, (q + 1) * part_width)
        carried = lax.dot_general(
            read_t, start[q], (((0,), (0,)), ((), ())), preferred_element_type=f32
        )
        g = gate[:, at].astype(f32)
        value = (mixed[:, at] + grown[:, at] * carried) * (g / (1.0 + jnp.exp(-g)))
        squares = squares + jnp.sum(value * value, axis=1, keepdims=True)
        gated.append(value)
    inverse = lax.rsqrt(squares / out.shape[1] + epsilon)
    for q in range(QUAD):
        at = slice(q * part_width, (q + 1) * part_width)
        out[:, at] = (gated[q] * inverse * gain[:, at].astype(f32)).astype(bf16)


def per_device(
    hidden_states,
    select_weight,
    conv_taps,
    inner_input,
    gate_input,
    step_size,
    decay_rate,
    skip_gain,
    tenant_scale,
    tenant_index,
    norm_gain,
):
    heads = decay_rate.shape[0]
    width = inner_input.shape[1]
    x, zh, zl = (lax.axis_index(a) for a in CTX)
    place = jnp.stack([x, zh, zl, tenant_index[0]])
    n_ctx = lax.axis_size(CTX)
    n_part = N // QUAD
    part_width = width // QUAD
    part_rows = Q + LOG_ROWS + QUAD * HALO

    def by(s):
        return [(i, (i + s) % QUAD) for i in range(QUAD)]

    w_t = select_weight.T
    w_zh = lax.all_gather(w_t, "zh", axis=0, tiled=True)

    near = [lax.ppermute(hidden_states, "zl", by(s)) for s in (1, QUAD - 1)]
    halo = lax.ppermute(
        hidden_states[Q - HALO :], CTX, [(i, i + 1) for i in range(n_ctx - 1)]
    )
    w_zh, near, halo = lax.optimization_barrier((w_zh, near, halo))
    w_all = share(w_zh, "x").reshape(-1, w_t.shape[1])
    far = lax.ppermute(hidden_states, "zl", by(2))

    part = shape((part_rows, part_width), bf16)
    driven, cum, cum_t, *parts = kernel_call(
        drive_kernel,
        [shape((Q, width), bf16), shape((Q, heads), f32), shape((heads, Q), f32)] + [part] * QUAD,
        place,
        [inner_input, tenant_scale, step_size, decay_rate[None], halo],
        [pltpu.VMEM((Q + LOG_ROWS + HALO, width), bf16)],
    )
    parts[1:] = [lax.ppermute(parts[s], "zl", by(s)) for s in range(1, QUAD)]

    sums = kernel_call(
        project_kernel,
        shape((w_all.shape[0], (QUAD + 1) * Q), bf16),
        place,
        [w_all, hidden_states, near[0], far, near[1], *parts],
        [pltpu.VMEM((Q, w_all.shape[1]), bf16)],
    )
    raw = swap(sums.reshape(lax.axis_size(TP), 2 * n_part, -1), TP)
    taps = conv_taps.shape[0]
    own_taps = lax.dynamic_index_in_dim(
        conv_taps.reshape(taps, 2, QUAD, n_part), zl, 2, False
    ).reshape(taps, 2 * n_part)
    keys = kernel_call(
        keys_kernel,
        shape((QUAD, n_part, (QUAD + 1) * Q), bf16),
        place,
        [raw, own_taps.T],
        [pltpu.VMEM((2 * n_part, QUAD * Q), bf16)],
    )
    keys = swap(keys, "zl").reshape(N, -1)

    starts, ends, total = kernel_call(
        update_kernel,
        [
            shape((QUAD, N, part_width), f32),
            shape((QUAD, part_width), f32),
            shape((N + LOG_ROWS, part_width), bf16),
        ],
        place,
        [keys, *parts],
        [pltpu.VMEM((QUAD, N, part_width), f32), pltpu.VMEM((QUAD, 8, part_width), f32)],
    )
    got = lax.all_gather(total, "zh")
    before, log_before, row = kernel_call(
        row_kernel,
        [
            shape((N, part_width), f32),
            shape((1, part_width), f32),
            shape((lax.axis_size("x"), N + LOG_ROWS, part_width), bf16),
        ],
        place,
        [got],
    )
    states = kernel_call(
        states_kernel,
        shape((QUAD, N, part_width), bf16),
        place,
        [swap(row, "x"), before, log_before, starts, ends],
    )
    start = swap(states, "zl")

    mixed = kernel_call(
        within_kernel,
        shape((Q, width), f32),
        place,
        [keys, driven, cum, cum_t, inner_input, tenant_scale, skip_gain[None]],
    )
    return kernel_call(
        output_kernel,
        shape((Q, width), bf16),
        place,
        [keys, start, cum, mixed, gate_input, norm_gain[None]],
    )


def solution(mesh):
    fine = Mesh(mesh.devices.reshape(4, 4, 4, 4, 2), CTX + TP)
    in_specs = (
        P(CTX, TP),
        P(TP, CTX),
        P(None, TP),
        P(CTX, TP),
        P(CTX, TP),
        P(CTX, TP),
        P(TP),
        P(TP),
        P(None, TP),
        P(CTX),
        P(TP),
    )
    return jax.shard_map(
        per_device, mesh=fine, in_specs=in_specs, out_specs=P(CTX, TP), check_vma=False
    )
```

time: 194 us -> 145 us (0.75)
  waiting for transfers between devices: 89.8 us -> 23 us
  blocking collectives: 38.3 us -> 65.1 us
  between operations: 14.4 us -> 0.81 us
  Pallas kernels: 0 us -> 11.8 us
  starting transfers between devices: 32 us -> 39.2 us
  other arithmetic: 6.47 us -> 0.08 us
  local copies, waits for them, and re-layouts: 9.06 us -> 4.22 us
  matrix products: 3.55 us -> 0 us
    all_gather x0 -> x2, blocking collectives: none -> 45.3 us  [the longest x1 25.6 us: per_device(): w_zh = lax.all_gather(w_t, 'zh', axis=0, tiled=True)]
    all_to_all x5 -> x3, waiting for transfers between devices: 55.4 us -> 15.9 us  [swap(): return lax.all_to_all(blocks, axis, 0, 0, tiled=True)]
    all_gather x2 -> x0, waiting for transfers between devices: 29.6 us -> none  [the longest x1 29.6 us: per_device(): lax.all_gather(jnp.concatenate([halo, hidden_states], axis=0), 'zl', axis...]
    ppermute x0 -> x6, starting transfers between devices: none -> 22.5 us  [the longest x2 9.43 us: per_device(): near = [lax.ppermute(hidden_states, 'zl', by(s)) for s in (1, QUAD - 1)]]
    all_to_all x1 -> x2, blocking collectives: 38.3 us -> 19.9 us  [swap(): return lax.all_to_all(blocks, axis, 0, 0, tiled=True)]
    all_to_all x5 -> x3, starting transfers between devices: 28.1 us -> 14.7 us  [swap(): return lax.all_to_all(blocks, axis, 0, 0, tiled=True)]
    pallas_call x0 -> x8, Pallas kernels: none -> 11.8 us  [kernel_call(): pl.pallas_call(body, out_shape=outs, in_specs=[SMEM] + [VMEM] * len(args)...]
    ppermute x0 -> x6, waiting for transfers between devices: none -> 7.03 us  [the longest x3 7.02 us: per_device(): parts[1:] = [lax.ppermute(parts[s], 'zl', by(s)) for s in range(1, QUAD)]]
  transfers between devices with their start and end apart: 8 -> 10, of which waited for: 7 -> 5; matrix products, arithmetic and copies ran while one was open for 2% -> 1% of each run, Pallas kernels for 0% -> 2%
where the time goes in v2:
time: 145 us; the launch traced here: 144 us
  blocking collectives  65.1 us (45%)
  starting transfers between devices  39.2 us (27%)
  waiting for transfers between devices  23 us (16%)
  Pallas kernels  11.8 us (8%)
  local copies, waits for them, and re-layouts  4.22 us (3%)
    all_gather x1, blocking collectives, per_device(): w_zh = lax.all_gather(w_t, 'zh', axis=0, tiled=True)  25.6 us
    all_to_all x2, blocking collectives, swap(): return lax.all_to_all(blocks, axis, 0, 0, tiled=True)  19.9 us
    all_gather x1, blocking collectives, per_device(): got = lax.all_gather(total, 'zh')  19.6 us
    all_to_all x3, waiting for transfers between devices, swap(): return lax.all_to_all(blocks, axis, 0, 0, tiled=True)  15.9 us
    all_to_all x3, starting transfers between devices, swap(): return lax.all_to_all(blocks, axis, 0, 0, tiled=True)  14.7 us
    pallas_call x8, Pallas kernels, kernel_call(): pl.pallas_call(body, out_shape=outs, in_specs=[SMEM] + [VMEM] * len(args)...  11.8 us
    ppermute x2, starting transfers between devices, per_device(): near = [lax.ppermute(hidden_states, 'zl', by(s)) for s in (1, QUAD - 1)]  9.43 us
    ppermute x3, starting transfers between devices, per_device(): parts[1:] = [lax.ppermute(parts[s], 'zl', by(s)) for s in range(1, QUAD)]  8.26 us
  transfers between devices with their start and end apart: 10, of which 5 were waited for; matrix products, arithmetic and copies ran while one was open for 1% of the time, Pallas kernels for 2%

profile of v2, /device:TPU:32, one launch (start us, length us, event | category | flops | bytes accessed | tf_op | source)
XLA Modules:
  0.0 144.1 jit_solution(18354313200826612037)
XLA Ops:
  0.0 3.9 %collective-permute-start = (bf16[128,1024]{1,0:T(8,128)(2,1)}, bf16[128,1024]{1,0:T(8,128)(2,1)S(1)}, u32[]{:S(2)}, u32[]{:S(2)}) collective-permute-start(bf16[128,1024]{1,0:T(8,128)(2,1)} %h0.1), channel_id=1, source_target_pairs={{0,8},{8,16},{16,24},{24,0},{1,9},{9,17},{17,25},{25,1},{2,10},{10... | collective-permute-start | bytes 786440 | tf_op jit(solution)/shard_map/ppermute | solution.py:285
  4.0 5.5 %collective-permute-start.1 = (bf16[128,1024]{1,0:T(8,128)(2,1)}, bf16[128,1024]{1,0:T(8,128)(2,1)S(1)}, u32[]{:S(2)}, u32[]{:S(2)}) collective-permute-start(bf16[128,1024]{1,0:T(8,128)(2,1)} %h0.1), channel_id=1, source_target_pairs={{0,24},{8,0},{16,8},{24,16},{1,25},{9,1},{17,9},{25,17},{2,26},{10... | collective-permute-start | bytes 786440 | tf_op jit(solution)/shard_map/ppermute | solution.py:285
  9.5 0.8 slice.3
  10.2 1.9 %collective-permute-start.2 = (bf16[16,1024]{1,0:T(8,128)(2,1)S(1)}, bf16[16,1024]{1,0:T(8,128)(2,1)S(1)}, u32[]{:S(2)}, u32[]{:S(2)}) collective-permute-start(bf16[16,1024]{1,0:T(8,128)(2,1)S(1)} %slice.3), channel_id=1, source_target_pairs={{0,8},{8,16},{16,24},{24,32},{32,40},{40,48},{48,56},{56,64},{64,7... | collective-permute-start | bytes 98312 | tf_op jit(solution)/shard_map/ppermute | solution.py:286
  12.2 25.6 %all_gather.9 = bf16[128,1024]{1,0:T(8,128)(2,1)S(1)} all-gather(bf16[32,1024]{1,0:T(8,128)(2,1)S(1)} %bitcast.21), channel_id=1, replica_groups=mesh['x'=4,'zh'=4,'zl'=4,'y'=4,'core'=2] {'zh'}, dimensions={0}, use_global_device_ids=true | all-gather | bytes 327680 | tf_op jit(solution)/shard_map/all_gather | solution.py:283
  37.8 1.1 broadcast_in_dim.15
  38.9 4.4 %all-to-all-start = ((bf16[4,128,1024]{2,1,0:T(8,128)(2,1)}), bf16[4,128,1024]{2,1,0:T(8,128)(2,1)S(1)}, u32[]{:S(2)}, u32[]{:S(2)}) async-start(bf16[4,128,1024]{2,1,0:T(8,128)(2,1)} %broadcast_in_dim.15), calls=%async_computation | async-start | bytes 2097152 | tf_op jit(solution)/shard_map/all_to_all | solution.py:28
  43.3 4.8 %collective-permute-start.3 = (bf16[128,1024]{1,0:T(8,128)(2,1)S(1)}, bf16[128,1024]{1,0:T(8,128)(2,1)S(1)}, u32[]{:S(2)}, u32[]{:S(2)}) collective-permute-start(bf16[128,1024]{1,0:T(8,128)(2,1)S(1)} %copy-done.1), channel_id=1, source_target_pairs={{0,16},{8,24},{16,0},{24,8},{1,17},{9,25},{17,1},{25,9},{2,18},{10... | collective-permute-start | bytes 786440 | tf_op jit(solution)/shard_map/ppermute | solution.py:291
  48.9 0.7 copy-done.7
  49.7 0.6 copy-done.3
  50.4 1.8 %shard_map.109 = (bf16[128,1024]{1,0:T(8,128)(2,1)S(1)}, f32[128,16]{1,0:T(8,128)S(1)}, f32[16,128]{1,0:T(8,128)S(1)}, bf16[208,256]{1,0:T(8,128)(2,1)S(1)}, bf1...) custom-call(s32[4]{0:T(128)S(1)} %pad_add_fusion.place, ...), custom_call_target="tpu_custom_call" | custom-call | flops 1000000 | bytes 1000000 | tf_op jit(solution)/shard_map/pallas_call | solution.py:41
  52.1 1.9 %collective-permute-start.4 = (bf16[208,256]{1,0:T(8,128)(2,1)S(1)}, bf16[208,256]{1,0:T(8,128)(2,1)S(1)}, u32[]{:S(2)}, u32[]{:S(2)}) collective-permute-start(bf16[208,256]{1,0:T(8,128)(2,1)S(1)} %get-tuple-element.27), channel_id=1, source_target_pairs={{0,8},{8,16},{16,24},{24,0},{1,9},{9,17},{17,25},{25,1},{2,10},{10... | collective-permute-start | bytes 319496 | tf_op jit(solution)/shard_map/ppermute | solution.py:301
  54.1 4.4 %collective-permute-start.5 = (bf16[208,256]{1,0:T(8,128)(2,1)S(1)}, bf16[208,256]{1,0:T(8,128)(2,1)S(1)}, u32[]{:S(2)}, u32[]{:S(2)}) collective-permute-start(bf16[208,256]{1,0:T(8,128)(2,1)S(1)} %get-tuple-element.28), channel_id=1, source_target_pairs={{0,16},{8,24},{16,0},{24,8},{1,17},{9,25},{17,1},{25,9},{2,18},{10... | collective-permute-start | bytes 319496 | tf_op jit(solution)/shard_map/ppermute | solution.py:301
  58.5 1.9 %collective-permute-start.6 = (bf16[208,256]{1,0:T(8,128)(2,1)S(1)}, bf16[208,256]{1,0:T(8,128)(2,1)S(1)}, u32[]{:S(2)}, u32[]{:S(2)}) collective-permute-start(bf16[208,256]{1,0:T(8,128)(2,1)S(1)} %get-tuple-element.29), channel_id=1, source_target_pairs={{0,24},{8,0},{16,8},{24,16},{1,25},{9,1},{17,9},{25,17},{2,26},{10... | collective-permute-start | bytes 319496 | tf_op jit(solution)/shard_map/ppermute | solution.py:301
  60.4 2.1 %collective-permute-done.4.p1 = bf16[208,256]{1,0:T(8,128)(2,1)S(1)} collective-permute-done((bf16[208,256]{1,0:T(8,128)(2,1)S(1)}, bf16[208,256]{1,0:T(8,128)(2,1)S(1)}, u32[]{:S(2)}, u32[]{:S(2)}) %collective-permute-start.4) | collective-permute-done | bytes 106528 | tf_op jit(solution)/shard_map/ppermute | solution.py:301
  62.5 2.3 %collective-permute-done.5.p2 = bf16[208,256]{1,0:T(8,128)(2,1)S(1)} collective-permute-done((bf16[208,256]{1,0:T(8,128)(2,1)S(1)}, bf16[208,256]{1,0:T(8,128)(2,1)S(1)}, u32[]{:S(2)}, u32[]{:S(2)}) %collective-permute-start.5) | collective-permute-done | bytes 106528 | tf_op jit(solution)/shard_map/ppermute | solution.py:301
  64.8 2.7 %collective-permute-done.6.p3 = bf16[208,256]{1,0:T(8,128)(2,1)S(1)} collective-permute-done((bf16[208,256]{1,0:T(8,128)(2,1)S(1)}, bf16[208,256]{1,0:T(8,128)(2,1)S(1)}, u32[]{:S(2)}, u32[]{:S(2)}) %collective-permute-start.6) | collective-permute-done | bytes 106528 | tf_op jit(solution)/shard_map/ppermute | solution.py:301
  67.5 2.9 %shard_map.110 = bf16[512,640]{1,0:T(8,128)(2,1)} custom-call(s32[4]{0:T(128)S(1)} %pad_add_fusion.place, bf16[512,1024]{1,0:T(8,128)(2,1)S(1)} %bitcast.13, bf16[128,1024]{1,0:T(8,128)(2,1)S(1)} %copy-done.1, bf16[128,1024]{1,0:T(8,128)(2,1)S(1)} %collective-permute-done.h1, bf16[128,1024]{1,0:T(8,128)(2,1)S(1)} %collective-permute-done.3.h2, ...), custom_call_target="tpu_custom_call" | custom-call | flops 1000000 | bytes 1000000 | tf_op jit(solution)/shard_map/pallas_call | solution.py:41
  70.4 4.6 %all-to-all-start.1 = ((bf16[8,64,640]{2,1,0:T(8,128)(2,1)}), bf16[8,64,640]{2,1,0:T(8,128)(2,1)S(1)}, u32[]{:S(2)}, u32[]{:S(2)}) async-start(bf16[8,64,640]{2,1,0:T(8,128)(2,1)} %bitcast.6), calls=%async_computation.1 | async-start | bytes 1310720 | tf_op jit(solution)/shard_map/all_to_all | solution.py:28
  75.2 11.6 %all-to-all-done.1.parts = bf16[8,64,640]{2,1,0:T(8,128)(2,1)S(1)} async-done(((bf16[8,64,640]{2,1,0:T(8,128)(2,1)}), bf16[8,64,640]{2,1,0:T(8,128)(2,1)S(1)}, u32[]{:S(2)}, u32[]{:S(2)}) %all-to-all-start.1) | async-done | bytes 655392 | tf_op jit(solution)/shard_map/all_to_all | solution.py:28
  86.7 1.0 shard_map.111
  87.8 8.7 %all_to_all.25 = bf16[4,32,640]{2,1,0:T(8,128)(2,1)S(1)} all-to-all(bf16[4,32,640]{2,1,0:T(8,128)(2,1)S(1)} %shard_map.111), channel_id=1, replica_groups=mesh['x'=4,'zh'=4,'zl'=4,'y'=4,'core'=2] {'zl'}, dimensions={0} | all-to-all | bytes 327680 | tf_op jit(solution)/shard_map/all_to_all | solution.py:28
  96.5 0.8 shard_map.112
  97.3 19.6 %all-gather = bf16[576,256]{1,0:T(8,128)(2,1)S(1)} all-gather(bf16[144,256]{1,0:T(8,128)(2,1)S(1)} %get-tuple-element.30), channel_id=2, replica_groups=mesh['x'=4,'zh'=4,'zl'=4,'y'=4,'core'=2] {'zh'}, dimensions={0}, use_global_device_ids=true | all-gather | bytes 368640 | tf_op jit(solution)/shard_map/all_gather | solution.py:335
  117.0 0.6 shard_map.113
  117.6 11.2 %all_to_all.26.got = bf16[4,144,256]{2,1,0:T(8,128)(2,1)S(1)} all-to-all(bf16[4,144,256]{2,1,0:T(8,128)(2,1)S(1)} %get-tuple-element.31), channel_id=1, replica_groups=mesh['x'=4,'zh'=4,'zl'=4,'y'=4,'core'=2] {'x'}, dimensions={0} | all-to-all | bytes 589824 | tf_op jit(solution)/shard_map/all_to_all | solution.py:28
  128.8 1.4 shard_map.114
  130.1 5.7 %all-to-all-start.4 = ((bf16[4,128,256]{2,1,0:T(8,128)(2,1)}), bf16[4,128,256]{2,1,0:T(8,128)(2,1)S(1)}, u32[]{:S(2)}, u32[]{:S(2)}) async-start(bf16[4,128,256]{2,1,0:T(8,128)(2,1)} %shard_map.114), calls=%async_computation.4 | async-start | bytes 524288 | tf_op jit(solution)/shard_map/all_to_all | solution.py:28
  135.9 0.6 copy-done.5
  136.5 1.2 shard_map.115.mixed
  137.7 4.4 %all-to-all-done.4.start = bf16[4,128,256]{2,1,0:T(8,128)(2,1)S(1)} async-done(((bf16[4,128,256]{2,1,0:T(8,128)(2,1)}), bf16[4,128,256]{2,1,0:T(8,128)(2,1)S(1)}, u32[]{:S(2)}, u32[]{:S(2)}) %all-to-all-start.4) | async-done | bytes 262176 | tf_op jit(solution)/shard_map/all_to_all | solution.py:28
  142.1 2.0 %shard_map.116 = bf16[128,1024]{1,0:T(8,128)(2,1)} custom-call(s32[4]{0:T(128)S(1)} %pad_add_fusion.place, bf16[128,640]{1,0:T(8,128)(2,1)S(1)} %bitcast.16, bf16[4,128,256]{2,1,0:T(8,128)(2,1)S(1)} %all-to-all-done.4.start, f32[128,16]{1,0:T(8,128)S(1)} %get-tuple-element.36.cum, f32[128,1024]{1,0:T(8,128)S(1)} %shard_map.115.mixed, ...), custom_call_target="tpu_custom_call" | custom-call | flops 1000000 | bytes 1000000 | tf_op jit(solution)/shard_map/pallas_call | solution.py:41
  (28 shorter events, 0.5 us)
Async XLA Ops:
  0.0 12.1 %copy-start.6 = (bf16[1024,32]{0,1:T(8,128)(2,1)S(1)}, bf16[1024,32]{0,1:T(8,128)(2,1)}, u32[]{:S(2)}) copy-start(bf16[1024,32]{0,1:T(8,128)(2,1)} %param.12) | copy-start | bytes 196612
  0.0 37.8 %collective-permute-start = (bf16[128,1024]{1,0:T(8,128)(2,1)}, bf16[128,1024]{1,0:T(8,128)(2,1)S(1)}, u32[]{:S(2)}, u32[]{:S(2)}) collective-permute-start(bf16[128,1024]{1,0:T(8,128)(2,1)} %h0.1), channel_id=1, source_target_pairs={{0,8},{8,16},{16,24},{24,0},{1,9},{9,17},{17,25},{25,1},{2,10},{10... | collective-permute-start | bytes 786440 | tf_op jit(solution)/shard_map/ppermute | solution.py:285
  4.0 33.8 %collective-permute-start.1 = (bf16[128,1024]{1,0:T(8,128)(2,1)}, bf16[128,1024]{1,0:T(8,128)(2,1)S(1)}, u32[]{:S(2)}, u32[]{:S(2)}) collective-permute-start(bf16[128,1024]{1,0:T(8,128)(2,1)} %h0.1), channel_id=1, source_target_pairs={{0,24},{8,0},{16,8},{24,16},{1,25},{9,1},{17,9},{25,17},{2,26},{10... | collective-permute-start | bytes 786440 | tf_op jit(solution)/shard_map/ppermute | solution.py:285
  10.2 27.5 %collective-permute-start.2 = (bf16[16,1024]{1,0:T(8,128)(2,1)S(1)}, bf16[16,1024]{1,0:T(8,128)(2,1)S(1)}, u32[]{:S(2)}, u32[]{:S(2)}) collective-permute-start(bf16[16,1024]{1,0:T(8,128)(2,1)S(1)} %slice.3), channel_id=1, source_target_pairs={{0,8},{8,16},{16,24},{24,32},{32,40},{40,48},{48,56},{56,64},{64,7... | collective-permute-start | bytes 98312 | tf_op jit(solution)/shard_map/ppermute | solution.py:286
  38.9 4.4 %copy-start.1 = (bf16[128,1024]{1,0:T(8,128)(2,1)S(1)}, bf16[128,1024]{1,0:T(8,128)(2,1)}, u32[]{:S(2)}) copy-start(bf16[128,1024]{1,0:T(8,128)(2,1)} %h0.1) | copy-start | bytes 786436
  38.9 10.8 %copy-start = (bf16[128,1024]{1,0:T(8,128)(2,1)S(1)}, bf16[128,1024]{1,0:T(8,128)(2,1)}, u32[]{:S(2)}) copy-start(bf16[128,1024]{1,0:T(8,128)(2,1)} %inner.3) | copy-start | bytes 786436
  38.9 28.5 %all-to-all-start = ((bf16[4,128,1024]{2,1,0:T(8,128)(2,1)}), bf16[4,128,1024]{2,1,0:T(8,128)(2,1)S(1)}, u32[]{:S(2)}, u32[]{:S(2)}) async-start(bf16[4,128,1024]{2,1,0:T(8,128)(2,1)} %broadcast_in_dim.15), calls=%async_computation | async-start | bytes 2097152 | tf_op jit(solution)/shard_map/all_to_all | solution.py:28
  43.3 17.1 %collective-permute-start.3 = (bf16[128,1024]{1,0:T(8,128)(2,1)S(1)}, bf16[128,1024]{1,0:T(8,128)(2,1)S(1)}, u32[]{:S(2)}, u32[]{:S(2)}) collective-permute-start(bf16[128,1024]{1,0:T(8,128)(2,1)S(1)} %copy-done.1), channel_id=1, source_target_pairs={{0,16},{8,24},{16,0},{24,8},{1,17},{9,25},{17,1},{25,9},{2,18},{10... | collective-permute-start | bytes 786440 | tf_op jit(solution)/shard_map/ppermute | solution.py:291
  48.8 0.7 copy-start.7
  49.5 0.8 copy-start.3
  49.7 0.7 copy-start.4
  52.1 10.4 %collective-permute-start.4 = (bf16[208,256]{1,0:T(8,128)(2,1)S(1)}, bf16[208,256]{1,0:T(8,128)(2,1)S(1)}, u32[]{:S(2)}, u32[]{:S(2)}) collective-permute-start(bf16[208,256]{1,0:T(8,128)(2,1)S(1)} %get-tuple-element.27), channel_id=1, source_target_pairs={{0,8},{8,16},{16,24},{24,0},{1,9},{9,17},{17,25},{25,1},{2,10},{10... | collective-permute-start | bytes 319496 | tf_op jit(solution)/shard_map/ppermute | solution.py:301
  54.1 10.7 %collective-permute-start.5 = (bf16[208,256]{1,0:T(8,128)(2,1)S(1)}, bf16[208,256]{1,0:T(8,128)(2,1)S(1)}, u32[]{:S(2)}, u32[]{:S(2)}) collective-permute-start(bf16[208,256]{1,0:T(8,128)(2,1)S(1)} %get-tuple-element.28), channel_id=1, source_target_pairs={{0,16},{8,24},{16,0},{24,8},{1,17},{9,25},{17,1},{25,9},{2,18},{10... | collective-permute-start | bytes 319496 | tf_op jit(solution)/shard_map/ppermute | solution.py:301
  58.5 9.0 %collective-permute-start.6 = (bf16[208,256]{1,0:T(8,128)(2,1)S(1)}, bf16[208,256]{1,0:T(8,128)(2,1)S(1)}, u32[]{:S(2)}, u32[]{:S(2)}) collective-permute-start(bf16[208,256]{1,0:T(8,128)(2,1)S(1)} %get-tuple-element.29), channel_id=1, source_target_pairs={{0,24},{8,0},{16,8},{24,16},{1,25},{9,1},{17,9},{25,17},{2,26},{10... | collective-permute-start | bytes 319496 | tf_op jit(solution)/shard_map/ppermute | solution.py:301
  70.4 4.6 %copy-start.8 = (f32[4,256]{1,0:T(4,128)S(1)}, f32[4,256]{1,0:T(4,128)}, u32[]{:S(2)}) copy-start(f32[4,256]{1,0:T(4,128)} %param.13) | copy-start | bytes 12292
  70.4 16.4 %all-to-all-start.1 = ((bf16[8,64,640]{2,1,0:T(8,128)(2,1)}), bf16[8,64,640]{2,1,0:T(8,128)(2,1)S(1)}, u32[]{:S(2)}, u32[]{:S(2)}) async-start(bf16[8,64,640]{2,1,0:T(8,128)(2,1)} %bitcast.6), calls=%async_computation.1 | async-start | bytes 1310720 | tf_op jit(solution)/shard_map/all_to_all | solution.py:28
  130.1 5.7 %copy-start.9 = (bf16[1024]{0:T(1024)(128)(2,1)S(1)}, bf16[1024]{0:T(1024)(128)(2,1)}, u32[]{:S(2)}) copy-start(bf16[1024]{0:T(1024)(128)(2,1)} %param.21) | copy-start | bytes 6148
  130.1 11.9 %all-to-all-start.4 = ((bf16[4,128,256]{2,1,0:T(8,128)(2,1)}), bf16[4,128,256]{2,1,0:T(8,128)(2,1)S(1)}, u32[]{:S(2)}, u32[]{:S(2)}) async-start(bf16[4,128,256]{2,1,0:T(8,128)(2,1)} %shard_map.114), calls=%async_computation.4 | async-start | bytes 524288 | tf_op jit(solution)/shard_map/all_to_all | solution.py:28
  135.9 0.7 copy-start.5
  136.5 5.5 %copy-start.2 = (bf16[128,1024]{1,0:T(8,128)(2,1)S(1)}, bf16[128,1024]{1,0:T(8,128)(2,1)}, u32[]{:S(2)}) copy-start(bf16[128,1024]{1,0:T(8,128)(2,1)} %gate.1) | copy-start | bytes 786436

commit v3 on v2

v3 whole, which is shorter than its diff:
```python
import jax
import jax.numpy as jnp
from jax import lax
from jax.experimental import pallas as pl
from jax.experimental.pallas import tpu as pltpu
from jax.sharding import Mesh, PartitionSpec as P

N = 128
Q = 128
QUAD = 4
W_STEPS = (0, 2, -1, 1)
HALO = 16
LOG_ROWS = 16
Z = ("zh", "zl")
CTX = ("x",) + Z
NEAR = ("x", "zl")
TP = ("y", "core")

epsilon = 1e-05
bf16 = jnp.bfloat16
f32 = jnp.float32
EXACT = lax.Precision.HIGHEST

VMEM = pl.BlockSpec(memory_space=pltpu.VMEM)
SMEM = pl.BlockSpec(memory_space=pltpu.SMEM)


def swap(blocks, axis):
    return lax.all_to_all(blocks, axis, 0, 0, tiled=True)


def share(block, axis):
    peers = lax.axis_size(axis)
    return swap(jnp.broadcast_to(block[None], (peers,) + block.shape), axis)


def transpose_xy(block):
    side = lax.axis_size("x")
    pairs = [(i * side + j, j * side + i) for i in range(side) for j in range(side)]
    return lax.ppermute(block, ("x", "y"), pairs)


def shape(dims, kind):
    return jax.ShapeDtypeStruct(dims, kind)


def kernel_call(body, outs, place, args, scratch=(), flops=1_000_000):
    return pl.pallas_call(
        body,
        out_shape=outs,
        in_specs=[SMEM] + [VMEM] * len(args),
        out_specs=jax.tree.map(lambda _: VMEM, outs),
        scratch_shapes=scratch,
        compiler_params=pltpu.CompilerParams(vmem_limit_bytes=32 * 1024 * 1024),
        cost_estimate=pl.CostEstimate(flops=flops, bytes_accessed=1_000_000, transcendentals=0),
    )(place, *args)


def expand(columns, head_width):
    heads = columns.shape[1]
    shape2 = (heads, heads * head_width)
    head = lax.broadcasted_iota(jnp.int32, shape2, 0)
    lane = lax.broadcasted_iota(jnp.int32, shape2, 1)
    first = head * head_width
    onehot = jnp.where((lane >= first) & (lane < first + head_width), 1.0, 0.0)
    return jnp.dot(columns, onehot, precision=EXACT, preferred_element_type=f32)


def log_rows(row):
    hi = row.astype(bf16).astype(f32)
    mid = (row - hi).astype(bf16).astype(f32)
    low = row - hi - mid
    at = lax.broadcasted_iota(jnp.int32, (LOG_ROWS, row.shape[1]), 0)
    rows = jnp.where(at == 0, hi, jnp.where(at == 1, mid, jnp.where(at == 2, low, 0.0)))
    return rows.astype(bf16)


def log_row(rows):
    return jnp.sum(rows.astype(f32), axis=0, keepdims=True)


def scaled_by_tenant(tenant, inner_ref, scale_ref):
    row = lax.broadcasted_iota(jnp.int32, scale_ref.shape, 0)
    chosen = jnp.where(row == tenant, scale_ref[...].astype(f32), 0.0)
    return inner_ref[...].astype(f32) * jnp.sum(chosen, axis=0, keepdims=True)


def drive_kernel(place, inner, scale, step, decay, driven, cum, cum_t, weighted_t, logs):
    heads = step.shape[1]
    head_width = inner.shape[1] // heads
    log_decay = -step[...] * decay[...]
    rows = lax.broadcasted_iota(jnp.int32, (Q, Q), 0)
    cols = lax.broadcasted_iota(jnp.int32, (Q, Q), 1)
    lower = jnp.where(rows >= cols, 1.0, 0.0)
    so_far = jnp.dot(lower, log_decay, precision=EXACT, preferred_element_type=f32)
    cum[...] = so_far
    cum_t[...] = lax.dot_general(
        log_decay, lower, (((0,), (1,)), ((), ())), precision=EXACT, preferred_element_type=f32
    )
    end = so_far[Q - 1 :]
    scaled = scaled_by_tenant(place[3], inner, scale)
    drive = (scaled * expand(step[...], head_width)).astype(bf16)
    driven[...] = drive
    tail = expand(jnp.exp(end - so_far), head_width)
    weighted_t[...] = jnp.transpose(tail * drive.astype(f32)).astype(bf16)
    for h in range(heads):
        logs[h] = log_rows(jnp.broadcast_to(end[:, h : h + 1], (1, N)))


def share_kernel(place, block, out):
    for i in range(out.shape[0]):
        out[i] = block[...]


def project_kernel(place, w0, w1, w2, w3, rows, tails, out, w_in_order, all_rows):
    halves, n_part = w0.shape[:2]
    for w, step in zip((w0, w1, w2, w3), W_STEPS):
        s = lax.rem(place[2] + step + QUAD, QUAD)
        for i in range(halves):
            at = pl.multiple_of(i * N + s * n_part, n_part)
            w_in_order[pl.ds(at, n_part)] = w[i]
    first = (place[1] == 0) & (place[2] == 0)
    size = HALO + Q
    for block in range(rows.shape[0]):
        behind = tails[block - 1] if block > 0 else jnp.zeros_like(tails[0])
        all_rows[block * size : block * size + HALO] = jnp.where(first, behind, tails[block])
        all_rows[block * size + HALO : (block + 1) * size] = rows[block]
    for c in range(out.shape[1]):
        sums = lax.dot_general(
            all_rows[...],
            w_in_order[c * 2 * N : (c + 1) * 2 * N],
            (((1,), (1,)), ((), ())),
            preferred_element_type=f32,
        ).astype(bf16)
        for block in range(rows.shape[0]):
            out[block, c] = sums[block * size : (block + 1) * size]


def sum_kernel(place, parts, out):
    raw = parts[0].astype(f32)
    for i in range(1, parts.shape[0]):
        raw = raw + parts[i].astype(f32)
    out[...] = raw.astype(bf16)


def keys_kernel(place, sums, taps, weighted_t, logs, keys_out, out):
    raw = sums[...].astype(f32)
    n_taps = taps.shape[0]
    summed = taps[n_taps - 1 :] * raw[HALO:]
    for d in range(1, n_taps):
        summed = summed + taps[n_taps - 1 - d : n_taps - d] * raw[HALO - d : HALO - d + Q]
    keys = (summed / (1.0 + jnp.exp(-summed))).astype(bf16)
    keys_out[...] = keys
    update = jnp.dot(weighted_t[...], keys[:, :N], preferred_element_type=f32).astype(bf16)
    heads = out.shape[0]
    head_width = update.shape[0] // heads
    for h in range(heads):
        out[h, :head_width] = update[h * head_width : (h + 1) * head_width]
        out[h, head_width:] = logs[h]


def total_kernel(place, got, total):
    head_width = got.shape[1] - LOG_ROWS
    for row in range(total.shape[0]):
        acc = jnp.zeros((head_width, N), f32)
        log_acc = jnp.zeros((1, N), f32)
        for b in range(QUAD):
            log = log_row(got[row * QUAD + b, head_width:])
            acc = jnp.exp(log) * acc + got[row * QUAD + b, :head_width].astype(f32)
            log_acc = log_acc + log
        total[row, :head_width] = acc.astype(bf16)
        total[row, head_width:] = log_rows(log_acc)


def states_kernel(place, totals, got, out):
    head_width = out.shape[1]
    acc = jnp.zeros((head_width, N), f32)
    for row in range(totals.shape[1]):
        carry = acc
        for quad in range(totals.shape[0]):
            carry = jnp.where(place[1] == quad, acc, carry)
            log = log_row(totals[quad, row, head_width:])
            acc = jnp.exp(log) * acc + totals[quad, row, :head_width].astype(f32)
        for b in range(QUAD):
            at = row * QUAD + b
            out[at] = carry.astype(bf16)
            if b < QUAD - 1:
                log = log_row(got[at, head_width:])
                carry = jnp.exp(log) * carry + got[at, :head_width].astype(f32)


def within_kernel(place, keys, driven, cum, cum_t, inner, scale, skip, gate, out, grown):
    scores = lax.dot_general(
        keys[:, N:], keys[:, :N], (((1,), (1,)), ((), ())), preferred_element_type=f32
    )
    rows = lax.broadcasted_iota(jnp.int32, (Q, Q), 0)
    cols = lax.broadcasted_iota(jnp.int32, (Q, Q), 1)
    causal = rows >= cols
    heads = cum.shape[1]
    head_width = driven.shape[1] // heads
    per_tile = Q // head_width
    skipped = expand(skip[...], head_width) * scaled_by_tenant(place[3], inner, scale)
    g = gate[...].astype(f32)
    gates = g / (1.0 + jnp.exp(-g))
    grown[...] = gates * expand(jnp.exp(cum[...]), head_width)
    for tile in range(heads // per_tile):
        at = slice(tile * Q, (tile + 1) * Q)
        mixed = None
        for i in range(per_tile):
            h = tile * per_tile + i
            lag = cum[:, h : h + 1] - cum_t[h : h + 1]
            weights = jnp.where(causal, scores * jnp.exp(jnp.where(causal, lag, 0.0)), 0.0)
            summed = jnp.dot(weights.astype(bf16), driven[:, at], preferred_element_type=f32)
            mixed = summed if mixed is None else jnp.where(cols < i * head_width, mixed, summed)
        out[:, at] = (mixed + skipped[:, at]) * gates[:, at]


def output_kernel(place, keys, start, mixed, grown, gain, out):
    width = out.shape[1]
    quarter = width // QUAD
    gated = []
    squares = jnp.zeros((Q, 1), f32)
    for q in range(QUAD):
        at = slice(q * quarter, (q + 1) * quarter)
        carried = lax.dot_general(
            keys[:, N:], start[at], (((1,), (1,)), ((), ())), preferred_element_type=f32
        )
        value = mixed[:, at] + grown[:, at] * carried
        squares = squares + jnp.sum(value * value, axis=1, keepdims=True)
        gated.append(value)
    inverse = lax.rsqrt(squares / width + epsilon)
    for q in range(QUAD):
        at = slice(q * quarter, (q + 1) * quarter)
        out[:, at] = (gated[q] * inverse * gain[:, at].astype(f32)).astype(bf16)


def per_device(
    hidden_states,
    select_weight,
    conv_taps,
    inner_input,
    gate_input,
    step_size,
    decay_rate,
    skip_gain,
    tenant_scale,
    tenant_index,
    norm_gain,
):
    heads = decay_rate.shape[0]
    width = inner_input.shape[1]
    head_width = width // heads
    x, zh, zl = (lax.axis_index(a) for a in CTX)
    place = jnp.stack([x, zh, zl, tenant_index[0]])
    n_z = lax.axis_size(Z)
    n_x = lax.axis_size("x")
    depth = hidden_states.shape[1]

    rows = swap(
        kernel_call(
            share_kernel, shape((n_x,) + hidden_states.shape, bf16), place, [hidden_states]
        ),
        "x",
    )

    n_part = select_weight.shape[1]
    w_zh = lax.all_gather(select_weight.T, "zh")
    w_zh, rows = lax.optimization_barrier((w_zh, rows))
    w_all = [w_zh] + [
        lax.ppermute(w_zh, Z, [(i, (i - step) % n_z) for i in range(n_z)]) for step in W_STEPS[1:]
    ]

    tails = lax.ppermute(rows[:, Q - HALO :], Z, [(i, (i + 1) % n_z) for i in range(n_z)])

    driven, cum, cum_t, weighted_t, logs = kernel_call(
        drive_kernel,
        [
            shape((Q, width), bf16),
            shape((Q, heads), f32),
            shape((heads, Q), f32),
            shape((width, Q), bf16),
            shape((heads, LOG_ROWS, N), bf16),
        ],
        place,
        [inner_input, tenant_scale, step_size, decay_rate[None]],
    )


    size = HALO + Q
    sums = kernel_call(
        project_kernel,
        shape((n_x, lax.axis_size("core"), size, 2 * N), bf16),
        place,
        [*w_all, rows, tails],
        [
            pltpu.VMEM((w_zh.shape[0] * QUAD * n_part, depth), bf16),
            pltpu.VMEM((n_x * size, depth), bf16),
        ],
    )
    sums = swap(sums.reshape(-1, size, 2 * N), TP)
    sums, weighted_t, logs = lax.optimization_barrier((sums, weighted_t, logs))
    sums = transpose_xy(kernel_call(sum_kernel, shape((size, 2 * N), bf16), place, [sums]))
    keys, update = kernel_call(
        keys_kernel,
        [shape((Q, 2 * N), bf16), shape((heads, head_width + LOG_ROWS, N), bf16)],
        place,
        [sums, conv_taps, weighted_t, logs],
    )

    got = swap(update, NEAR)
    total = kernel_call(
        total_kernel, shape((n_x, head_width + LOG_ROWS, N), bf16), place, [got]
    )
    states = kernel_call(
        states_kernel,
        shape((heads, head_width, N), bf16),
        place,
        [lax.all_gather(total, "zh"), got],
    )
    start = swap(states, NEAR).reshape(width, N)

    mixed, grown = kernel_call(
        within_kernel,
        [shape((Q, width), f32)] * 2,
        place,
        [keys, driven, cum, cum_t, inner_input, tenant_scale, skip_gain[None], gate_input],
    )
    return kernel_call(
        output_kernel,
        shape((Q, width), bf16),
        place,
        [keys, start, mixed, grown, norm_gain[None]],
    )


def solution(mesh):
    fine = Mesh(mesh.devices.reshape(4, 4, 4, 4, 2), CTX + TP)
    in_specs = (
        P(CTX, TP),
        P(TP, CTX),
        P(None, TP),
        P(CTX, TP),
        P(CTX, TP),
        P(CTX, TP),
        P(TP),
        P(TP),
        P(None, TP),
        P(CTX),
        P(TP),
    )
    return jax.shard_map(
        per_device, mesh=fine, in_specs=in_specs, out_specs=P(CTX, TP), check_vma=False
    )
```

time: 145 us -> 140 us (0.966)
  starting transfers between devices: 39.2 us -> 26.7 us
  blocking collectives: 65.1 us -> 75.1 us
  local copies, waits for them, and re-layouts: 4.22 us -> 2.38 us
    ppermute x7 -> x5, starting transfers between devices: 24.4 us -> 12.7 us  [the longest x3 10 us: per_device(): lax.ppermute(w_zh, Z, [(i, (i - step) % n_z) for i in range(n_z)])]
    all_to_all x2 -> x1, blocking collectives: 19.9 us -> 27.9 us  [swap(): return lax.all_to_all(blocks, axis, 0, 0, tiled=True)]
    all_gather x2, blocking collectives: 45.3 us -> 47.1 us  [the longest x1 25.7 us: per_device(): w_zh = lax.all_gather(select_weight.T, 'zh')]
    pallas_call x8 -> x9, Pallas kernels: 11.8 us -> 12.1 us  [kernel_call(): pl.pallas_call(body, out_shape=outs, in_specs=[SMEM] + [VMEM] * len(args)...]
    ppermute x7 -> x5, waiting for transfers between devices: 7.03 us -> 7.05 us  [the longest x1 4.82 us: per_device(): lax.ppermute(rows[:, Q - HALO:], Z, [(i, (i + 1) % n_z) for i in range(n_...]
  transfers between devices with their start and end apart: 10 -> 8, of which waited for: 5 -> 4; matrix products, arithmetic and copies ran while one was open for 1% -> 0% of each run, Pallas kernels for 2% -> 2%
where the time goes in v3:
time: 140 us; the launch traced here: 139 us
  blocking collectives  75.1 us (54%)
  starting transfers between devices  26.7 us (19%)
  waiting for transfers between devices  22 us (16%)
  Pallas kernels  12.1 us (9%)
  local copies, waits for them, and re-layouts  2.38 us (2%)
    all_to_all x1, blocking collectives, swap(): return lax.all_to_all(blocks, axis, 0, 0, tiled=True)  27.9 us
    all_gather x1, blocking collectives, per_device(): w_zh = lax.all_gather(select_weight.T, 'zh')  25.7 us
    all_gather x1, blocking collectives, per_device(): lax.all_gather(total, 'zh')  21.4 us
    all_to_all x3, waiting for transfers between devices, swap(): return lax.all_to_all(blocks, axis, 0, 0, tiled=True)  14.9 us
    all_to_all x3, starting transfers between devices, swap(): return lax.all_to_all(blocks, axis, 0, 0, tiled=True)  14 us
    pallas_call x9, Pallas kernels, kernel_call(): pl.pallas_call(body, out_shape=outs, in_specs=[SMEM] + [VMEM] * len(args)...  12.1 us
    ppermute x3, starting transfers between devices, per_device(): lax.ppermute(w_zh, Z, [(i, (i - step) % n_z) for i in range(n_z)])  10 us
    ppermute x1, waiting for transfers between devices, per_device(): lax.ppermute(rows[:, Q - HALO:], Z, [(i, (i + 1) % n_z) for i in range(n_...  4.82 us
  transfers between devices with their start and end apart: 8, of which 4 were waited for; matrix products, arithmetic and copies ran while one was open for 0% of the time, Pallas kernels for 2%

profile of v3, /device:TPU:32, one launch (start us, length us, event | category | flops | bytes accessed | tf_op | source)
XLA Modules:
  0.0 139.1 jit_solution(7454137549700248106)
XLA Ops:
  0.7 0.1 pad_add_fusion.place
  0.7 0.9 copy-done.1
  1.7 1.6 %shard_map.109 = bf16[4,128,1024]{2,1,0:T(8,128)(2,1)} custom-call(s32[4]{0:T(128)S(1)} %pad_add_fusion.place, bf16[128,1024]{1,0:T(8,128)(2,1)S(1)} %copy-done.1), custom_call_target="tpu_custom_call" | custom-call | flops 1000000 | bytes 1000000 | tf_op jit(solution)/shard_map/pallas_call | solution.py:48
  3.3 4.4 %all-to-all-start = ((bf16[4,128,1024]{2,1,0:T(8,128)(2,1)}), bf16[4,128,1024]{2,1,0:T(8,128)(2,1)S(1)}, u32[]{:S(2)}, u32[]{:S(2)}) async-start(bf16[4,128,1024]{2,1,0:T(8,128)(2,1)} %shard_map.109), calls=%async_computation | async-start | bytes 2097152 | tf_op jit(solution)/shard_map/all_to_all | solution.py:29
  7.7 25.7 %all-gather = bf16[128,1024]{1,0:T(8,128)(2,1)S(1)} all-gather(bf16[32,1024]{1,0:T(8,128)(2,1)S(1)} %bitcast.18), channel_id=2, replica_groups=mesh['x'=4,'zh'=4,'zl'=4,'y'=4,'core'=2] {'zh'}, dimensions={0}, use_global_device_ids=true | all-gather | bytes 327680 | tf_op jit(solution)/shard_map/all_gather | solution.py:267
  33.4 4.2 %collective-permute-start = (bf16[4,32,1024]{2,1,0:T(8,128)(2,1)S(1)}, bf16[4,32,1024]{2,1,0:T(8,128)(2,1)S(1)}, u32[]{:S(2)}, u32[]{:S(2)}) collective-permute-start(bf16[4,32,1024]{2,1,0:T(8,128)(2,1)S(1)} %bitcast.11), channel_id=1, source_target_pairs={{0,112},{8,120},{16,0},{24,8},{32,16},{40,24},{48,32},{56,40},{64,... | collective-permute-start | bytes 786440 | tf_op jit(solution)/shard_map/ppermute | solution.py:270
  37.6 2.0 %collective-permute-start.1 = (bf16[4,32,1024]{2,1,0:T(8,128)(2,1)S(1)}, bf16[4,32,1024]{2,1,0:T(8,128)(2,1)S(1)}, u32[]{:S(2)}, u32[]{:S(2)}) collective-permute-start(bf16[4,32,1024]{2,1,0:T(8,128)(2,1)S(1)} %bitcast.12), channel_id=1, source_target_pairs={{0,8},{8,16},{16,24},{24,32},{32,40},{40,48},{48,56},{56,64},{64,7... | collective-permute-start | bytes 786440 | tf_op jit(solution)/shard_map/ppermute | solution.py:270
  39.6 3.8 %collective-permute-start.2 = (bf16[4,32,1024]{2,1,0:T(8,128)(2,1)S(1)}, bf16[4,32,1024]{2,1,0:T(8,128)(2,1)S(1)}, u32[]{:S(2)}, u32[]{:S(2)}) collective-permute-start(bf16[4,32,1024]{2,1,0:T(8,128)(2,1)S(1)} %bitcast.13), channel_id=1, source_target_pairs={{0,120},{8,0},{16,8},{24,16},{32,24},{40,32},{48,40},{56,48},{64,5... | collective-permute-start | bytes 786440 | tf_op jit(solution)/shard_map/ppermute | solution.py:270
  43.4 2.0 %collective-permute-start.3 = (bf16[4,16,1024]{2,1,0:T(8,128)(2,1)S(1)}, bf16[4,16,1024]{2,1,0:T(8,128)(2,1)S(1)}, u32[]{:S(2)}, u32[]{:S(2)}) collective-permute-start(bf16[4,16,1024]{2,1,0:T(8,128)(2,1)S(1)} %slice.3), channel_id=1, source_target_pairs={{0,8},{8,16},{16,24},{24,32},{32,40},{40,48},{48,56},{56,64},{64,7... | collective-permute-start | bytes 393224 | tf_op jit(solution)/shard_map/ppermute | solution.py:273
  45.5 4.8 %collective-permute-done.3.tails = bf16[4,16,1024]{2,1,0:T(8,128)(2,1)S(1)} collective-permute-done((bf16[4,16,1024]{2,1,0:T(8,128)(2,1)S(1)}, bf16[4,16,1024]{2,1,0:T(8,128)(2,1)S(1)}, u32[]{:S(2)}, u32[]{:S(2)}) %collective-permute-start.3) | collective-permute-done | bytes 131104 | tf_op jit(solution)/shard_map/ppermute | solution.py:273
  50.3 2.2 %collective-permute-done.2.w3 = bf16[4,32,1024]{2,1,0:T(8,128)(2,1)S(1)} collective-permute-done((bf16[4,32,1024]{2,1,0:T(8,128)(2,1)S(1)}, bf16[4,32,1024]{2,1,0:T(8,128)(2,1)S(1)}, u32[]{:S(2)}, u32[]{:S(2)}) %collective-permute-start.2) | collective-permute-done | bytes 262176 | tf_op jit(solution)/shard_map/ppermute | solution.py:270
  52.5 2.3 %shard_map.110 = bf16[4,2,144,256]{3,2,1,0:T(8,128)(2,1)} custom-call(s32[4]{0:T(128)S(1)} %pad_add_fusion.place, bf16[4,32,1024]{2,1,0:T(8,128)(2,1)S(1)} %bitcast.14, bf16[4,32,1024]{2,1,0:T(8,128)(2,1)S(1)} %collective-permute-done.w1, bf16[4,32,1024]{2,1,0:T(8,128)(2,1)S(1)} %collective-permute-done.1.w2, ...), custom_call_target="tpu_custom_call" | custom-call | flops 1000000 | bytes 1000000 | tf_op jit(solution)/shard_map/pallas_call | solution.py:48
  54.8 4.6 %all-to-all-start.1 = ((bf16[8,144,256]{2,1,0:T(8,128)(2,1)}), bf16[8,144,256]{2,1,0:T(8,128)(2,1)S(1)}, u32[]{:S(2)}, u32[]{:S(2)}) async-start(bf16[8,144,256]{2,1,0:T(8,128)(2,1)} %bitcast.5), calls=%async_computation.1 | async-start | bytes 1179648 | tf_op jit(solution)/shard_map/all_to_all | solution.py:29
  59.4 0.0 copy-start.3
  59.4 0.1 copy.13.step
  59.5 0.6 copy-done.3
  60.2 0.0 copy-done.5
  60.2 1.8 %shard_map.111 = (bf16[128,1024]{1,0:T(8,128)(2,1)S(1)}, f32[128,16]{1,0:T(8,128)S(1)}, f32[16,128]{1,0:T(8,128)S(1)}, bf16[1024,128]{1,0:T(8,128)(2,1)S(1)}, bf16[16,16,128]{2,1,0:T(8,128)(2,1)S(1)}) custom-call(s32[4]{0:T(128)S(1)} %pad_add_fusion.place, bf16[128,1024]{1,0:T(8,128)(2,1)S(1)} %copy-done, bf16[16,1024]{1,0:T(8,128)(2,1)S(1)} %copy-done.3, ...), custom_call_target="tpu_custom_call" | custom-call | flops 1000000 | bytes 1000000 | tf_op jit(solution)/shard_map/pallas_call | solution.py:48
  61.9 8.5 %all-to-all-done.1.parts = bf16[8,144,256]{2,1,0:T(8,128)(2,1)S(1)} async-done(((bf16[8,144,256]{2,1,0:T(8,128)(2,1)}), bf16[8,144,256]{2,1,0:T(8,128)(2,1)S(1)}, u32[]{:S(2)}, u32[]{:S(2)}) %all-to-all-start.1) | async-done | bytes 589856 | tf_op jit(solution)/shard_map/all_to_all | solution.py:29
  70.5 0.6 shard_map.112
  71.1 0.7 collective-permute-start.4
  71.8 0.8 shard_map.113
  72.6 27.9 %all_to_all.20.got = bf16[16,80,128]{2,1,0:T(8,128)(2,1)S(1)} all-to-all(bf16[16,80,128]{2,1,0:T(8,128)(2,1)S(1)} %get-tuple-element.27), channel_id=1, replica_groups=mesh['x'=4,'zh'=4,'zl'=4,'y'=4,'core'=2] {'x','zl'}, dimensions={0} | all-to-all | bytes 655360 | tf_op jit(solution)/shard_map/all_to_all | solution.py:29
  100.6 0.6 shard_map.114
  101.2 21.4 %all-gather.1 = bf16[16,80,128]{2,1,0:T(8,128)(2,1)S(1)} all-gather(bf16[4,80,128]{2,1,0:T(8,128)(2,1)S(1)} %shard_map.114), channel_id=3, replica_groups=mesh['x'=4,'zh'=4,'zl'=4,'y'=4,'core'=2] {'zh'}, dimensions={0}, use_global_device_ids=true | all-gather | bytes 409600 | tf_op jit(solution)/shard_map/all_gather | solution.py:318
  122.6 1.4 %shard_map.115 = bf16[16,64,128]{2,1,0:T(8,128)(2,1)} custom-call(s32[4]{0:T(128)S(1)} %pad_add_fusion.place, bf16[4,4,80,128]{3,2,1,0:T(8,128)(2,1)S(1)} %bitcast.10, bf16[16,80,128]{2,1,0:T(8,128)(2,1)S(1)} %all_to_all.20.got), custom_call_target="tpu_custom_call" | custom-call | flops 1000000 | bytes 1000000 | tf_op jit(solution)/shard_map/pallas_call | solution.py:48
  124.1 5.0 %all-to-all-start.3 = ((bf16[16,64,128]{2,1,0:T(8,128)(2,1)}), bf16[16,64,128]{2,1,0:T(8,128)(2,1)S(1)}, u32[]{:S(2)}, u32[]{:S(2)}) async-start(bf16[16,64,128]{2,1,0:T(8,128)(2,1)} %shard_map.115), calls=%async_computation.3 | async-start | bytes 524288 | tf_op jit(solution)/shard_map/all_to_all | solution.py:29
  129.1 0.0 copy-start.6
  129.1 0.6 copy-done.6
  129.7 1.3 shard_map.116
  131.1 6.4 %all-to-all-done.3 = bf16[16,64,128]{2,1,0:T(8,128)(2,1)S(1)} async-done(((bf16[16,64,128]{2,1,0:T(8,128)(2,1)}), bf16[16,64,128]{2,1,0:T(8,128)(2,1)S(1)}, u32[]{:S(2)}, u32[]{:S(2)}) %all-to-all-start.3) | async-done | bytes 262176 | tf_op jit(solution)/shard_map/all_to_all | solution.py:29
  137.5 1.6 %shard_map.117 = bf16[128,1024]{1,0:T(8,128)(2,1)} custom-call(s32[4]{0:T(128)S(1)} %pad_add_fusion.place, bf16[128,256]{1,0:T(8,128)(2,1)S(1)} %get-tuple-element.26.keys, bf16[1024,128]{1,0:T(8,128)(2,1)S(1)} %bitcast.15, f32[128,1024]{1,0:T(8,128)S(1)} %get-tuple-element.31.mixed, f32[128,1024]{1,0:T(8,128)S(1)} %get-tuple-element.32.grown, ...), custom_call_target="tpu_custom_call" | custom-call | flops 1000000 | bytes 1000000 | tf_op jit(solution)/shard_map/pallas_call | solution.py:48
  (20 shorter events, 0.1 us)
Async XLA Ops:
  0.7 1.0 copy-start.1
  3.3 4.4 %copy-start.7 = (bf16[1024,32]{0,1:T(8,128)(2,1)S(1)}, bf16[1024,32]{0,1:T(8,128)(2,1)}, u32[]{:S(2)}) copy-start(bf16[1024,32]{0,1:T(8,128)(2,1)} %param.12) | copy-start | bytes 196612
  3.3 30.1 %all-to-all-start = ((bf16[4,128,1024]{2,1,0:T(8,128)(2,1)}), bf16[4,128,1024]{2,1,0:T(8,128)(2,1)S(1)}, u32[]{:S(2)}, u32[]{:S(2)}) async-start(bf16[4,128,1024]{2,1,0:T(8,128)(2,1)} %shard_map.109), calls=%async_computation | async-start | bytes 2097152 | tf_op jit(solution)/shard_map/all_to_all | solution.py:29
  33.4 16.9 %collective-permute-start = (bf16[4,32,1024]{2,1,0:T(8,128)(2,1)S(1)}, bf16[4,32,1024]{2,1,0:T(8,128)(2,1)S(1)}, u32[]{:S(2)}, u32[]{:S(2)}) collective-permute-start(bf16[4,32,1024]{2,1,0:T(8,128)(2,1)S(1)} %bitcast.11), channel_id=1, source_target_pairs={{0,112},{8,120},{16,0},{24,8},{32,16},{40,24},{48,32},{56,40},{64,... | collective-permute-start | bytes 786440 | tf_op jit(solution)/shard_map/ppermute | solution.py:270
  37.6 12.7 %collective-permute-start.1 = (bf16[4,32,1024]{2,1,0:T(8,128)(2,1)S(1)}, bf16[4,32,1024]{2,1,0:T(8,128)(2,1)S(1)}, u32[]{:S(2)}, u32[]{:S(2)}) collective-permute-start(bf16[4,32,1024]{2,1,0:T(8,128)(2,1)S(1)} %bitcast.12), channel_id=1, source_target_pairs={{0,8},{8,16},{16,24},{24,32},{32,40},{40,48},{48,56},{56,64},{64,7... | collective-permute-start | bytes 786440 | tf_op jit(solution)/shard_map/ppermute | solution.py:270
  39.6 12.9 %collective-permute-start.2 = (bf16[4,32,1024]{2,1,0:T(8,128)(2,1)S(1)}, bf16[4,32,1024]{2,1,0:T(8,128)(2,1)S(1)}, u32[]{:S(2)}, u32[]{:S(2)}) collective-permute-start(bf16[4,32,1024]{2,1,0:T(8,128)(2,1)S(1)} %bitcast.13), channel_id=1, source_target_pairs={{0,120},{8,0},{16,8},{24,16},{32,24},{40,32},{48,40},{56,48},{64,5... | collective-permute-start | bytes 786440 | tf_op jit(solution)/shard_map/ppermute | solution.py:270
  43.4 6.9 %collective-permute-start.3 = (bf16[4,16,1024]{2,1,0:T(8,128)(2,1)S(1)}, bf16[4,16,1024]{2,1,0:T(8,128)(2,1)S(1)}, u32[]{:S(2)}, u32[]{:S(2)}) collective-permute-start(bf16[4,16,1024]{2,1,0:T(8,128)(2,1)S(1)} %slice.3), channel_id=1, source_target_pairs={{0,8},{8,16},{16,24},{24,32},{32,40},{40,48},{48,56},{56,64},{64,7... | collective-permute-start | bytes 393224 | tf_op jit(solution)/shard_map/ppermute | solution.py:273
  54.8 4.6 %copy-start.8 = (f32[128,16]{0,1:T(8,128)S(1)}, f32[128,16]{0,1:T(8,128)}, u32[]{:S(2)}) copy-start(f32[128,16]{0,1:T(8,128)} %param.16) | copy-start | bytes 24580
  54.8 4.7 %copy-start = (bf16[128,1024]{1,0:T(8,128)(2,1)S(1)}, bf16[128,1024]{1,0:T(8,128)(2,1)}, u32[]{:S(2)}) copy-start(bf16[128,1024]{1,0:T(8,128)(2,1)} %inner.3) | copy-start | bytes 786436
  54.8 15.7 %all-to-all-start.1 = ((bf16[8,144,256]{2,1,0:T(8,128)(2,1)}), bf16[8,144,256]{2,1,0:T(8,128)(2,1)S(1)}, u32[]{:S(2)}, u32[]{:S(2)}) async-start(bf16[8,144,256]{2,1,0:T(8,128)(2,1)} %bitcast.5), calls=%async_computation.1 | async-start | bytes 1179648 | tf_op jit(solution)/shard_map/all_to_all | solution.py:29
  59.4 0.8 copy-start.3
  59.5 0.7 copy-start.5
  70.5 1.3 copy-start.4
  71.1 0.7 collective-permute-start.4
  124.1 5.0 %copy-start.9 = (bf16[1024]{0:T(1024)(128)(2,1)S(1)}, bf16[1024]{0:T(1024)(128)(2,1)}, u32[]{:S(2)}) copy-start(bf16[1024]{0:T(1024)(128)(2,1)} %param.21) | copy-start | bytes 6148
  124.1 5.0 %copy-start.2 = (bf16[128,1024]{1,0:T(8,128)(2,1)S(1)}, bf16[128,1024]{1,0:T(8,128)(2,1)}, u32[]{:S(2)}) copy-start(bf16[128,1024]{1,0:T(8,128)(2,1)} %gate.1) | copy-start | bytes 786436
  124.1 13.4 %all-to-all-start.3 = ((bf16[16,64,128]{2,1,0:T(8,128)(2,1)}), bf16[16,64,128]{2,1,0:T(8,128)(2,1)S(1)}, u32[]{:S(2)}, u32[]{:S(2)}) async-start(bf16[16,64,128]{2,1,0:T(8,128)(2,1)} %shard_map.115), calls=%async_computation.3 | async-start | bytes 524288 | tf_op jit(solution)/shard_map/all_to_all | solution.py:29
  129.1 0.7 copy-start.6

commit v4 on v3

--- a/solution.py
+++ b/solution.py
@@ -34,9 +34,11 @@
     return swap(jnp.broadcast_to(block[None], (peers,) + block.shape), axis)
 
 
-def transpose_xy(block):
+def to_owner(block):
     side = lax.axis_size("x")
-    pairs = [(i * side + j, j * side + i) for i in range(side) for j in range(side)]
+    pairs = [
+        (i * side + j, (j + side // 2) % side * side + i) for i in range(side) for j in range(side)
+    ]
     return lax.ppermute(block, ("x", "y"), pairs)
 
 
@@ -66,10 +68,14 @@
     return jnp.dot(columns, onehot, precision=EXACT, preferred_element_type=f32)
 
 
-def log_rows(row):
+def split3(row):
     hi = row.astype(bf16).astype(f32)
     mid = (row - hi).astype(bf16).astype(f32)
-    low = row - hi - mid
+    return hi, mid, row - hi - mid
+
+
+def log_rows(row):
+    hi, mid, low = split3(row)
     at = lax.broadcasted_iota(jnp.int32, (LOG_ROWS, row.shape[1]), 0)
     rows = jnp.where(at == 0, hi, jnp.where(at == 1, mid, jnp.where(at == 2, low, 0.0)))
     return rows.astype(bf16)
@@ -107,18 +113,29 @@
         logs[h] = log_rows(jnp.broadcast_to(end[:, h : h + 1], (1, N)))
 
 
-def share_kernel(place, block, out):
-    for i in range(out.shape[0]):
-        out[i] = block[...]
-
-
-def project_kernel(place, w0, w1, w2, w3, rows, tails, out, w_in_order, all_rows):
-    halves, n_part = w0.shape[:2]
+def share_kernel(block, out, held, arrived, sent):
+    fetch = pltpu.make_async_copy(block, held, arrived)
+    fetch.start()
+    fetch.wait()
+    copies = [pltpu.make_async_copy(held, out.at[i], sent.at[i]) for i in range(out.shape[0])]
+    for copy in copies:
+        copy.start()
+    for copy in copies:
+        copy.wait()
+
+
+def project_kernel(place, w0, w1, w2, w3, rows, out, w_in_order, all_rows):
+    n_part = N // QUAD
+    halves = w0.shape[0] // n_part
     for w, step in zip((w0, w1, w2, w3), W_STEPS):
         s = lax.rem(place[2] + step + QUAD, QUAD)
         for i in range(halves):
             at = pl.multiple_of(i * N + s * n_part, n_part)
-            w_in_order[pl.ds(at, n_part)] = w[i]
+            w_in_order[pl.ds(at, n_part)] = w[i * n_part : (i + 1) * n_part]
+    tails = [
+        w2[halves * n_part + i * HALO : halves * n_part + (i + 1) * HALO]
+        for i in range(rows.shape[0])
+    ]
     first = (place[1] == 0) & (place[2] == 0)
     size = HALO + Q
     for block in range(rows.shape[0]):
@@ -133,7 +150,8 @@
             preferred_element_type=f32,
         ).astype(bf16)
         for block in range(rows.shape[0]):
-            out[block, c] = sums[block * size : (block + 1) * size]
+            to = (block + rows.shape[0] // 2) % rows.shape[0]
+            out[to, c] = sums[block * size : (block + 1) * size]
 
 
 def sum_kernel(place, parts, out):
@@ -161,26 +179,34 @@
 
 def total_kernel(place, got, total):
     head_width = got.shape[1] - LOG_ROWS
-    for row in range(total.shape[0]):
+    rows = got.shape[0] // QUAD
+    at = lax.broadcasted_iota(jnp.int32, (LOG_ROWS, N), 0)
+    logs = jnp.zeros((LOG_ROWS, N), f32)
+    for row in range(rows):
         acc = jnp.zeros((head_width, N), f32)
         log_acc = jnp.zeros((1, N), f32)
         for b in range(QUAD):
             log = log_row(got[row * QUAD + b, head_width:])
             acc = jnp.exp(log) * acc + got[row * QUAD + b, :head_width].astype(f32)
             log_acc = log_acc + log
-        total[row, :head_width] = acc.astype(bf16)
-        total[row, head_width:] = log_rows(log_acc)
+        total[row * head_width : (row + 1) * head_width] = acc.astype(bf16)
+        for i, part in enumerate(split3(log_acc)):
+            logs = jnp.where(at == row * 3 + i, part, logs)
+    total[rows * head_width :] = logs.astype(bf16)
 
 
 def states_kernel(place, totals, got, out):
     head_width = out.shape[1]
+    rows = out.shape[0] // QUAD
+    logs = [totals[quad, rows * head_width :].astype(f32) for quad in range(totals.shape[0])]
     acc = jnp.zeros((head_width, N), f32)
-    for row in range(totals.shape[1]):
+    for row in range(rows):
         carry = acc
         for quad in range(totals.shape[0]):
             carry = jnp.where(place[1] == quad, acc, carry)
-            log = log_row(totals[quad, row, head_width:])
-            acc = jnp.exp(log) * acc + totals[quad, row, :head_width].astype(f32)
+            log = jnp.sum(logs[quad][3 * row : 3 * row + 3], axis=0, keepdims=True)
+            update = totals[quad, row * head_width : (row + 1) * head_width]
+            acc = jnp.exp(log) * acc + update.astype(f32)
         for b in range(QUAD):
             at = row * QUAD + b
             out[at] = carry.astype(bf16)
@@ -256,21 +282,37 @@
     n_x = lax.axis_size("x")
     depth = hidden_states.shape[1]
 
-    rows = swap(
-        kernel_call(
-            share_kernel, shape((n_x,) + hidden_states.shape, bf16), place, [hidden_states]
-        ),
-        "x",
-    )
+    rows = pl.pallas_call(
+        share_kernel,
+        out_shape=shape((n_x,) + hidden_states.shape, bf16),
+        in_specs=[pl.BlockSpec(memory_space=pl.ANY)],
+        out_specs=pl.BlockSpec(memory_space=pl.ANY),
+        scratch_shapes=[
+            pltpu.VMEM(hidden_states.shape, bf16),
+            pltpu.SemaphoreType.DMA,
+            pltpu.SemaphoreType.DMA((n_x,)),
+        ],
+        cost_estimate=pl.CostEstimate(flops=0, bytes_accessed=1_000_000, transcendentals=0),
+    )(hidden_states)
+    rows = swap(rows, "x")
 
     n_part = select_weight.shape[1]
-    w_zh = lax.all_gather(select_weight.T, "zh")
+    w_zh = lax.all_gather(select_weight.T, "zh", axis=0, tiled=True)
     w_zh, rows = lax.optimization_barrier((w_zh, rows))
+    n_core = lax.axis_size("core")
+    tails = rows[:, Q - HALO :].reshape(n_x * HALO, depth)
     w_all = [w_zh] + [
-        lax.ppermute(w_zh, Z, [(i, (i - step) % n_z) for i in range(n_z)]) for step in W_STEPS[1:]
+        lax.ppermute(
+            jnp.concatenate([w_zh, tails], axis=0) if step == -1 else w_zh,
+            Z + ("core",),
+            [
+                (i * n_core + c, (i - step * (1 if c == 0 else turn)) % n_z * n_core + c)
+                for i in range(n_z)
+                for c in range(n_core)
+            ],
+        )
+        for step, turn in zip(W_STEPS[1:], (-1, 1, 1))
     ]
-
-    tails = lax.ppermute(rows[:, Q - HALO :], Z, [(i, (i + 1) % n_z) for i in range(n_z)])
 
     driven, cum, cum_t, weighted_t, logs = kernel_call(
         drive_kernel,
@@ -286,20 +328,21 @@
     )
 
 
+    w_all, weighted_t, logs = lax.optimization_barrier((w_all, weighted_t, logs))
+
     size = HALO + Q
     sums = kernel_call(
         project_kernel,
         shape((n_x, lax.axis_size("core"), size, 2 * N), bf16),
         place,
-        [*w_all, rows, tails],
+        [*w_all, rows],
         [
-            pltpu.VMEM((w_zh.shape[0] * QUAD * n_part, depth), bf16),
+            pltpu.VMEM((w_zh.shape[0] * QUAD, depth), bf16),
             pltpu.VMEM((n_x * size, depth), bf16),
         ],
     )
     sums = swap(sums.reshape(-1, size, 2 * N), TP)
-    sums, weighted_t, logs = lax.optimization_barrier((sums, weighted_t, logs))
-    sums = transpose_xy(kernel_call(sum_kernel, shape((size, 2 * N), bf16), place, [sums]))
+    sums = to_owner(kernel_call(sum_kernel, shape((size, 2 * N), bf16), place, [sums]))
     keys, update = kernel_call(
         keys_kernel,
         [shape((Q, 2 * N), bf16), shape((heads, head_width + LOG_ROWS, N), bf16)],
@@ -309,7 +352,7 @@
 
     got = swap(update, NEAR)
     total = kernel_call(
-        total_kernel, shape((n_x, head_width + LOG_ROWS, N), bf16), place, [got]
+        total_kernel, shape((n_x * head_width + LOG_ROWS, N), bf16), place, [got]
     )
     states = kernel_call(
         states_kernel,

time: 140 us -> 134 us (0.957)
  waiting for transfers between devices: 22 us -> 14.4 us
  blocking collectives: 75.1 us -> 80 us
  starting transfers between devices: 26.7 us -> 24.9 us
    all_to_all x3 -> x2, waiting for transfers between devices: 14.9 us -> 6.36 us  [swap(): return lax.all_to_all(blocks, axis, 0, 0, tiled=True)]
    all_to_all x1 -> x2, blocking collectives: 27.9 us -> 34.3 us  [swap(): return lax.all_to_all(blocks, axis, 0, 0, tiled=True)]
    all_to_all x3 -> x2, starting transfers between devices: 14 us -> 8.97 us  [swap(): return lax.all_to_all(blocks, axis, 0, 0, tiled=True)]
    ppermute x5 -> x4, starting transfers between devices: 12.7 us -> 15.9 us  [the longest x3 10.2 us: per_device(): lax.ppermute(jnp.concatenate([w_zh, tails], axis=0) if step == -1 else w_...]
    pallas_call x9 -> x8, Pallas kernels: 12.1 us -> 9.65 us  [kernel_call(): pl.pallas_call(body, out_shape=outs, in_specs=[SMEM] + [VMEM] * len(args)...]
    pallas_call x0 -> x1, Pallas kernels: none -> 1.97 us  [per_device(): pl.pallas_call(share_kernel, out_shape=shape((n_x,) + hidden_states.shape...]
    ppermute x5 -> x4, waiting for transfers between devices: 7.05 us -> 8.03 us  [the longest x3 5.86 us: per_device(): lax.ppermute(jnp.concatenate([w_zh, tails], axis=0) if step == -1 else w_...]
  transfers between devices with their start and end apart: 8 -> 6, of which waited for: 4 -> 4; matrix products, arithmetic and copies ran while one was open for 0% -> 0% of each run, Pallas kernels for 2% -> 2%
where the time goes in v4:
time: 134 us; the launch traced here: 133 us
  blocking collectives  80 us (60%)
  starting transfers between devices  24.9 us (19%)
  waiting for transfers between devices  14.4 us (11%)
  Pallas kernels  11.6 us (9%)
  local copies, waits for them, and re-layouts  1.47 us (1%)
    all_to_all x2, blocking collectives, swap(): return lax.all_to_all(blocks, axis, 0, 0, tiled=True)  34.3 us
    all_gather x1, blocking collectives, per_device(): w_zh = lax.all_gather(select_weight.T, 'zh', axis=0, tiled=True)  25.7 us
    all_gather x1, blocking collectives, per_device(): lax.all_gather(total, 'zh')  20 us
    ppermute x3, starting transfers between devices, per_device(): lax.ppermute(jnp.concatenate([w_zh, tails], axis=0) if step == -1 else w_...  10.2 us
    pallas_call x8, Pallas kernels, kernel_call(): pl.pallas_call(body, out_shape=outs, in_specs=[SMEM] + [VMEM] * len(args)...  9.65 us
    all_to_all x2, starting transfers between devices, swap(): return lax.all_to_all(blocks, axis, 0, 0, tiled=True)  8.97 us
    all_to_all x2, waiting for transfers between devices, swap(): return lax.all_to_all(blocks, axis, 0, 0, tiled=True)  6.36 us
    ppermute x3, waiting for transfers between devices, per_device(): lax.ppermute(jnp.concatenate([w_zh, tails], axis=0) if step == -1 else w_...  5.86 us
  transfers between devices with their start and end apart: 6, of which 4 were waited for; matrix products, arithmetic and copies ran while one was open for 0% of the time, Pallas kernels for 2%

profile of v4, /device:TPU:32, one launch (start us, length us, event | category | flops | bytes accessed | tf_op | source)
XLA Modules:
  0.0 133.3 jit_solution(2327854964301424450)
XLA Ops:
  0.0 2.0 %shard_map.109 = bf16[4,128,1024]{2,1,0:T(8,128)(2,1)} custom-call(bf16[128,1024]{1,0:T(8,128)(2,1)} %block.1), custom_call_target="tpu_custom_call" | custom-call | bytes 1000000 | tf_op jit(solution)/shard_map/pallas_call | solution.py:285
  2.0 0.0 copy-start.6
  2.0 4.4 %all-to-all-start = ((bf16[4,128,1024]{2,1,0:T(8,128)(2,1)}), bf16[4,128,1024]{2,1,0:T(8,128)(2,1)S(1)}, u32[]{:S(2)}, u32[]{:S(2)}) async-start(bf16[4,128,1024]{2,1,0:T(8,128)(2,1)} %shard_map.109), calls=%async_computation | async-start | bytes 2097152 | tf_op jit(solution)/shard_map/all_to_all | solution.py:29
  6.4 25.7 %all_gather.9.w0 = bf16[128,1024]{1,0:T(8,128)(2,1)S(1)} all-gather(bf16[32,1024]{1,0:T(8,128)(2,1)S(1)} %bitcast.16), channel_id=1, replica_groups=mesh['x'=4,'zh'=4,'zl'=4,'y'=4,'core'=2] {'zh'}, dimensions={0}, use_global_device_ids=true | all-gather | bytes 327680 | tf_op jit(solution)/shard_map/all_gather | solution.py:300
  32.1 0.0 copy-start
  32.2 3.1 %collective-permute-start.1 = (bf16[192,1024]{1,0:T(8,128)(2,1)S(1)}, bf16[192,1024]{1,0:T(8,128)(2,1)S(1)}, u32[]{:S(2)}, u32[]{:S(2)}) collective-permute-start(bf16[192,1024]{1,0:T(8,128)(2,1)S(1)} %pad_maximum_fusion), channel_id=1, source_target_pairs={{0,8},{1,9},{8,16},{9,17},{16,24},{17,25},{24,32},{25,33},{32,40},... | collective-permute-start | bytes 1179656 | tf_op jit(solution)/shard_map/ppermute | solution.py:305
  35.3 4.5 %collective-permute-start = (bf16[128,1024]{1,0:T(8,128)(2,1)S(1)}, bf16[128,1024]{1,0:T(8,128)(2,1)S(1)}, u32[]{:S(2)}, u32[]{:S(2)}) collective-permute-start(bf16[128,1024]{1,0:T(8,128)(2,1)S(1)} %all_gather.9.w0), channel_id=1, source_target_pairs={{0,112},{1,17},{8,120},{9,25},{16,0},{17,33},{24,8},{25,41},{32,16... | collective-permute-start | bytes 786440 | tf_op jit(solution)/shard_map/ppermute | solution.py:305
  39.7 2.6 %collective-permute-start.2 = (bf16[128,1024]{1,0:T(8,128)(2,1)S(1)}, bf16[128,1024]{1,0:T(8,128)(2,1)S(1)}, u32[]{:S(2)}, u32[]{:S(2)}) collective-permute-start(bf16[128,1024]{1,0:T(8,128)(2,1)S(1)} %all_gather.9.w0), channel_id=1, source_target_pairs={{0,120},{1,121},{8,0},{9,1},{16,8},{17,9},{24,16},{25,17},{32,24},... | collective-permute-start | bytes 786440 | tf_op jit(solution)/shard_map/ppermute | solution.py:305
  43.0 0.0 copy-done.7
  43.1 0.1 copy.12.step
  43.2 0.1 pad_add_fusion.place
  43.2 0.6 copy-done.2
  43.8 0.1 copy-done.4
  43.9 1.8 %shard_map.110 = (bf16[128,1024]{1,0:T(8,128)(2,1)S(1)}, f32[128,16]{1,0:T(8,128)S(1)}, f32[16,128]{1,0:T(8,128)S(1)}, bf16[1024,128]{1,0:T(8,128)(2,1)S(1)}, bf16[16,16,128]{2,1,0:T(8,128)(2,1)S(1)}) custom-call(s32[4]{0:T(128)S(1)} %pad_add_fusion.place, bf16[128,1024]{1,0:T(8,128)(2,1)S(1)} %copy-done, bf16[16,1024]{1,0:T(8,128)(2,1)S(1)} %copy-done.2, ...), custom_call_target="tpu_custom_call" | custom-call | flops 1000000 | bytes 1000000 | tf_op jit(solution)/shard_map/pallas_call | solution.py:50
  45.7 1.6 %collective-permute-done.w1 = bf16[128,1024]{1,0:T(8,128)(2,1)S(1)} collective-permute-done((bf16[128,1024]{1,0:T(8,128)(2,1)S(1)}, bf16[128,1024]{1,0:T(8,128)(2,1)S(1)}, u32[]{:S(2)}, u32[]{:S(2)}) %collective-permute-start) | collective-permute-done | bytes 262176 | tf_op jit(solution)/shard_map/ppermute | solution.py:305
  47.3 4.2 %collective-permute-done.2.w3 = bf16[128,1024]{1,0:T(8,128)(2,1)S(1)} collective-permute-done((bf16[128,1024]{1,0:T(8,128)(2,1)S(1)}, bf16[128,1024]{1,0:T(8,128)(2,1)S(1)}, u32[]{:S(2)}, u32[]{:S(2)}) %collective-permute-start.2) | collective-permute-done | bytes 262176 | tf_op jit(solution)/shard_map/ppermute | solution.py:305
  51.5 1.4 %shard_map.111 = bf16[4,2,144,256]{3,2,1,0:T(8,128)(2,1)S(1)} custom-call(s32[4]{0:T(128)S(1)} %pad_add_fusion.place, bf16[128,1024]{1,0:T(8,128)(2,1)S(1)} %all_gather.9.w0, bf16[128,1024]{1,0:T(8,128)(2,1)S(1)} %collective-permute-done.w1, bf16[192,1024]{1,0:T(8,128)(2,1)S(1)} %collective-permute-done.1.w2, ...), custom_call_target="tpu_custom_call" | custom-call | flops 1000000 | bytes 1000000 | tf_op jit(solution)/shard_map/pallas_call | solution.py:50
  53.0 15.4 %all_to_all.20.parts = bf16[8,144,256]{2,1,0:T(8,128)(2,1)S(1)} all-to-all(bf16[8,144,256]{2,1,0:T(8,128)(2,1)S(1)} %bitcast.10), channel_id=1, replica_groups=mesh['x'=4,'zh'=4,'zl'=4,'y'=4,'core'=2] {'y','core'}, dimensions={0} | all-to-all | bytes 1179648 | tf_op jit(solution)/shard_map/all_to_all | solution.py:29
  68.3 0.6 shard_map.112
  69.0 5.7 %collective-permute-start.3 = (bf16[144,256]{1,0:T(8,128)(2,1)S(1)}, bf16[144,256]{1,0:T(8,128)(2,1)S(1)}, u32[]{:S(2)}, u32[]{:S(2)}) collective-permute-start(bf16[144,256]{1,0:T(8,128)(2,1)S(1)} %shard_map.112), channel_id=1, source_target_pairs={{0,256},{2,384},{4,0},{6,128},{128,258},{130,386},{132,2},{134,130... | collective-permute-start | bytes 221192 | tf_op jit(solution)/shard_map/ppermute | solution.py:42
  74.7 2.2 %collective-permute-done.3.sums = bf16[144,256]{1,0:T(8,128)(2,1)S(1)} collective-permute-done((bf16[144,256]{1,0:T(8,128)(2,1)S(1)}, bf16[144,256]{1,0:T(8,128)(2,1)S(1)}, u32[]{:S(2)}, u32[]{:S(2)}) %collective-permute-start.3) | collective-permute-done | bytes 73760 | tf_op jit(solution)/shard_map/ppermute | solution.py:42
  76.9 0.8 shard_map.113
  77.7 19.0 %all_to_all.21.got = bf16[16,80,128]{2,1,0:T(8,128)(2,1)S(1)} all-to-all(bf16[16,80,128]{2,1,0:T(8,128)(2,1)S(1)} %get-tuple-element.33), channel_id=1, replica_groups=mesh['x'=4,'zh'=4,'zl'=4,'y'=4,'core'=2] {'x','zl'}, dimensions={0} | all-to-all | bytes 655360 | tf_op jit(solution)/shard_map/all_to_all | solution.py:29
  96.7 0.6 shard_map.114
  97.3 20.0 %all-gather = bf16[1088,128]{1,0:T(8,128)(2,1)S(1)} all-gather(bf16[272,128]{1,0:T(8,128)(2,1)S(1)} %shard_map.114), channel_id=2, replica_groups=mesh['x'=4,'zh'=4,'zl'=4,'y'=4,'core'=2] {'zh'}, dimensions={0}, use_global_device_ids=true | all-gather | bytes 348160 | tf_op jit(solution)/shard_map/all_gather | solution.py:361
  117.4 1.4 %shard_map.115 = bf16[16,64,128]{2,1,0:T(8,128)(2,1)} custom-call(s32[4]{0:T(128)S(1)} %pad_add_fusion.place, bf16[4,272,128]{2,1,0:T(8,128)(2,1)S(1)} %bitcast.11, bf16[16,80,128]{2,1,0:T(8,128)(2,1)S(1)} %all_to_all.21.got), custom_call_target="tpu_custom_call" | custom-call | flops 1000000 | bytes 1000000 | tf_op jit(solution)/shard_map/pallas_call | solution.py:50
  118.8 4.5 %all-to-all-start.3 = ((bf16[16,64,128]{2,1,0:T(8,128)(2,1)}), bf16[16,64,128]{2,1,0:T(8,128)(2,1)S(1)}, u32[]{:S(2)}, u32[]{:S(2)}) async-start(bf16[16,64,128]{2,1,0:T(8,128)(2,1)} %shard_map.115), calls=%async_computation.3 | async-start | bytes 524288 | tf_op jit(solution)/shard_map/all_to_all | solution.py:29
  123.3 0.0 copy-start.5
  123.4 0.6 copy-done.5
  124.0 1.4 %shard_map.116 = (f32[128,1024]{1,0:T(8,128)S(1)}, f32[128,1024]{1,0:T(8,128)S(1)}) custom-call(s32[4]{0:T(128)S(1)} %pad_add_fusion.place, bf16[128,256]{1,0:T(8,128)(2,1)S(1)} %get-tuple-element.32.keys, bf16[128,1024]{1,0:T(8,128)(2,1)S(1)} %get-tuple-element.34.driven, f32[128,16]{1,0:T(8,128)S(1)} %get-tuple-element.35.cum, ...), custom_call_target="tpu_custom_call" | custom-call | flops 1000000 | bytes 1000000 | tf_op jit(solution)/shard_map/pallas_call | solution.py:50
  125.4 6.4 %all-to-all-done.3 = bf16[16,64,128]{2,1,0:T(8,128)(2,1)S(1)} async-done(((bf16[16,64,128]{2,1,0:T(8,128)(2,1)}), bf16[16,64,128]{2,1,0:T(8,128)(2,1)S(1)}, u32[]{:S(2)}, u32[]{:S(2)}) %all-to-all-start.3) | async-done | bytes 262176 | tf_op jit(solution)/shard_map/all_to_all | solution.py:29
  131.7 1.6 %shard_map.117 = bf16[128,1024]{1,0:T(8,128)(2,1)} custom-call(s32[4]{0:T(128)S(1)} %pad_add_fusion.place, bf16[128,256]{1,0:T(8,128)(2,1)S(1)} %get-tuple-element.32.keys, bf16[1024,128]{1,0:T(8,128)(2,1)S(1)} %bitcast.12, f32[128,1024]{1,0:T(8,128)S(1)} %get-tuple-element.37.mixed, f32[128,1024]{1,0:T(8,128)S(1)} %get-tuple-element.38.grown, ...), custom_call_target="tpu_custom_call" | custom-call | flops 1000000 | bytes 1000000 | tf_op jit(solution)/shard_map/pallas_call | solution.py:50
  (16 shorter events, 0.1 us)
Async XLA Ops:
  2.0 4.5 %copy-start.6 = (bf16[1024,32]{0,1:T(8,128)(2,1)S(1)}, bf16[1024,32]{0,1:T(8,128)(2,1)}, u32[]{:S(2)}) copy-start(bf16[1024,32]{0,1:T(8,128)(2,1)} %param.12) | copy-start | bytes 196612
  2.0 30.1 %all-to-all-start = ((bf16[4,128,1024]{2,1,0:T(8,128)(2,1)}), bf16[4,128,1024]{2,1,0:T(8,128)(2,1)S(1)}, u32[]{:S(2)}, u32[]{:S(2)}) async-start(bf16[4,128,1024]{2,1,0:T(8,128)(2,1)} %shard_map.109), calls=%async_computation | async-start | bytes 2097152 | tf_op jit(solution)/shard_map/all_to_all | solution.py:29
  32.1 11.1 %copy-start = (bf16[128,1024]{1,0:T(8,128)(2,1)S(1)}, bf16[128,1024]{1,0:T(8,128)(2,1)}, u32[]{:S(2)}) copy-start(bf16[128,1024]{1,0:T(8,128)(2,1)} %inner.3) | copy-start | bytes 786436
  32.2 19.3 %collective-permute-start.1 = (bf16[192,1024]{1,0:T(8,128)(2,1)S(1)}, bf16[192,1024]{1,0:T(8,128)(2,1)S(1)}, u32[]{:S(2)}, u32[]{:S(2)}) collective-permute-start(bf16[192,1024]{1,0:T(8,128)(2,1)S(1)} %pad_maximum_fusion), channel_id=1, source_target_pairs={{0,8},{1,9},{8,16},{9,17},{16,24},{17,25},{24,32},{25,33},{32,40},... | collective-permute-start | bytes 1179656 | tf_op jit(solution)/shard_map/ppermute | solution.py:305
  35.3 12.0 %collective-permute-start = (bf16[128,1024]{1,0:T(8,128)(2,1)S(1)}, bf16[128,1024]{1,0:T(8,128)(2,1)S(1)}, u32[]{:S(2)}, u32[]{:S(2)}) collective-permute-start(bf16[128,1024]{1,0:T(8,128)(2,1)S(1)} %all_gather.9.w0), channel_id=1, source_target_pairs={{0,112},{1,17},{8,120},{9,25},{16,0},{17,33},{24,8},{25,41},{32,16... | collective-permute-start | bytes 786440 | tf_op jit(solution)/shard_map/ppermute | solution.py:305
  39.7 11.8 %collective-permute-start.2 = (bf16[128,1024]{1,0:T(8,128)(2,1)S(1)}, bf16[128,1024]{1,0:T(8,128)(2,1)S(1)}, u32[]{:S(2)}, u32[]{:S(2)}) collective-permute-start(bf16[128,1024]{1,0:T(8,128)(2,1)S(1)} %all_gather.9.w0), channel_id=1, source_target_pairs={{0,120},{1,121},{8,0},{9,1},{16,8},{17,9},{24,16},{25,17},{32,24},... | collective-permute-start | bytes 786440 | tf_op jit(solution)/shard_map/ppermute | solution.py:305
  42.4 0.7 copy-start.7
  43.1 0.8 copy-start.2
  43.2 0.7 copy-start.4
  68.3 8.6 %copy-start.3 = (f32[4,256]{1,0:T(4,128)S(1)}, f32[4,256]{1,0:T(4,128)}, u32[]{:S(2)}) copy-start(f32[4,256]{1,0:T(4,128)} %taps.1) | copy-start | bytes 12292
  69.0 7.9 %collective-permute-start.3 = (bf16[144,256]{1,0:T(8,128)(2,1)S(1)}, bf16[144,256]{1,0:T(8,128)(2,1)S(1)}, u32[]{:S(2)}, u32[]{:S(2)}) collective-permute-start(bf16[144,256]{1,0:T(8,128)(2,1)S(1)} %shard_map.112), channel_id=1, source_target_pairs={{0,256},{2,384},{4,0},{6,128},{128,258},{130,386},{132,2},{134,130... | collective-permute-start | bytes 221192 | tf_op jit(solution)/shard_map/ppermute | solution.py:42
  118.8 4.5 %copy-start.8 = (bf16[1024]{0:T(1024)(128)(2,1)S(1)}, bf16[1024]{0:T(1024)(128)(2,1)}, u32[]{:S(2)}) copy-start(bf16[1024]{0:T(1024)(128)(2,1)} %param.21) | copy-start | bytes 6148
  118.8 4.6 %copy-start.1 = (bf16[128,1024]{1,0:T(8,128)(2,1)S(1)}, bf16[128,1024]{1,0:T(8,128)(2,1)}, u32[]{:S(2)}) copy-start(bf16[128,1024]{1,0:T(8,128)(2,1)} %gate.1) | copy-start | bytes 786436
  118.8 13.0 %all-to-all-start.3 = ((bf16[16,64,128]{2,1,0:T(8,128)(2,1)}), bf16[16,64,128]{2,1,0:T(8,128)(2,1)S(1)}, u32[]{:S(2)}, u32[]{:S(2)}) async-start(bf16[16,64,128]{2,1,0:T(8,128)(2,1)} %shard_map.115), calls=%async_computation.3 | async-start | bytes 524288 | tf_op jit(solution)/shard_map/all_to_all | solution.py:29
  123.3 0.7 copy-start.5

commit v5 on v4

--- a/solution.py
+++ b/solution.py
@@ -8,8 +8,9 @@
 N = 128
 Q = 128
 QUAD = 4
-W_STEPS = (0, 2, -1, 1)
+W_STEPS = (0, 1, -1, 2)
 HALO = 16
+REACH = 3
 LOG_ROWS = 16
 Z = ("zh", "zl")
 CTX = ("x",) + Z
@@ -132,8 +133,9 @@
         for i in range(halves):
             at = pl.multiple_of(i * N + s * n_part, n_part)
             w_in_order[pl.ds(at, n_part)] = w[i * n_part : (i + 1) * n_part]
+    packed = w2[halves * n_part :].astype(f32)
     tails = [
-        w2[halves * n_part + i * HALO : halves * n_part + (i + 1) * HALO]
+        pltpu.roll(packed, (HALO - (i + 1) * REACH) % HALO, 0).astype(bf16)
         for i in range(rows.shape[0])
     ]
     first = (place[1] == 0) & (place[2] == 0)
@@ -300,7 +302,9 @@
     w_zh = lax.all_gather(select_weight.T, "zh", axis=0, tiled=True)
     w_zh, rows = lax.optimization_barrier((w_zh, rows))
     n_core = lax.axis_size("core")
-    tails = rows[:, Q - HALO :].reshape(n_x * HALO, depth)
+    tails = jnp.pad(
+        rows[:, Q - REACH :].reshape(n_x * REACH, depth), ((0, HALO - n_x * REACH), (0, 0))
+    )
     w_all = [w_zh] + [
         lax.ppermute(
             jnp.concatenate([w_zh, tails], axis=0) if step == -1 else w_zh,
@@ -311,7 +315,7 @@
                 for c in range(n_core)
             ],
         )
-        for step, turn in zip(W_STEPS[1:], (-1, 1, 1))
+        for step, turn in zip(W_STEPS[1:], (1, 1, -1))
     ]
 
     driven, cum, cum_t, weighted_t, logs = kernel_call(

time: 134 us -> 133 us (level)
  waiting for transfers between devices: 14.4 us -> 10.2 us
  blocking collectives: 80 us -> 81.7 us
  starting transfers between devices: 24.9 us -> 26.4 us
    ppermute x3, waiting for transfers between devices: 5.86 us -> 1.91 us  [per_device(): lax.ppermute(jnp.concatenate([w_zh, tails], axis=0) if step == -1 else w_...]
    all_to_all x2, blocking collectives: 34.3 us -> 36 us  [swap(): return lax.all_to_all(blocks, axis, 0, 0, tiled=True)]
    ppermute x1, starting transfers between devices: 5.74 us -> 7.08 us  [to_owner(): return lax.ppermute(block, ('x', 'y'), pairs)]
  transfers between devices with their start and end apart: 6 -> 6, of which waited for: 4 -> 3; matrix products, arithmetic and copies ran while one was open for 0% -> 0% of each run, Pallas kernels for 2% -> 2%
where the time goes in v5:
time: 133 us; the launch traced here: 132 us
  blocking collectives  81.7 us (61%)
  starting transfers between devices  26.4 us (20%)
  Pallas kernels  11.6 us (9%)
  waiting for transfers between devices  10.2 us (8%)
  local copies, waits for them, and re-layouts  1.51 us (1%)
    all_to_all x2, blocking collectives, swap(): return lax.all_to_all(blocks, axis, 0, 0, tiled=True)  36 us
    all_gather x1, blocking collectives, per_device(): w_zh = lax.all_gather(select_weight.T, 'zh', axis=0, tiled=True)  25.7 us
    all_gather x1, blocking collectives, per_device(): lax.all_gather(total, 'zh')  20 us
    ppermute x3, starting transfers between devices, per_device(): lax.ppermute(jnp.concatenate([w_zh, tails], axis=0) if step == -1 else w_...  10.2 us
    pallas_call x8, Pallas kernels, kernel_call(): pl.pallas_call(body, out_shape=outs, in_specs=[SMEM] + [VMEM] * len(args)...  9.66 us
    all_to_all x2, starting transfers between devices, swap(): return lax.all_to_all(blocks, axis, 0, 0, tiled=True)  9.19 us
    ppermute x1, starting transfers between devices, to_owner(): return lax.ppermute(block, ('x', 'y'), pairs)  7.08 us
    all_to_all x2, waiting for transfers between devices, swap(): return lax.all_to_all(blocks, axis, 0, 0, tiled=True)  6.36 us
  transfers between devices with their start and end apart: 6, of which 3 were waited for; matrix products, arithmetic and copies ran while one was open for 0% of the time, Pallas kernels for 2%

profile of v5, /device:TPU:32, one launch (start us, length us, event | category | flops | bytes accessed | tf_op | source)
XLA Modules:
  0.0 132.4 jit_solution(7358649418308841042)
XLA Ops:
  0.0 2.0 %shard_map.109 = bf16[4,128,1024]{2,1,0:T(8,128)(2,1)} custom-call(bf16[128,1024]{1,0:T(8,128)(2,1)} %block.1), custom_call_target="tpu_custom_call" | custom-call | bytes 1000000 | tf_op jit(solution)/shard_map/pallas_call | solution.py:287
  2.0 0.0 copy-start.6
  2.0 4.4 %all-to-all-start = ((bf16[4,128,1024]{2,1,0:T(8,128)(2,1)}), bf16[4,128,1024]{2,1,0:T(8,128)(2,1)S(1)}, u32[]{:S(2)}, u32[]{:S(2)}) async-start(bf16[4,128,1024]{2,1,0:T(8,128)(2,1)} %shard_map.109), calls=%async_computation | async-start | bytes 2097152 | tf_op jit(solution)/shard_map/all_to_all | solution.py:30
  6.4 25.7 %all_gather.9.w0 = bf16[128,1024]{1,0:T(8,128)(2,1)S(1)} all-gather(bf16[32,1024]{1,0:T(8,128)(2,1)S(1)} %bitcast.14), channel_id=1, replica_groups=mesh['x'=4,'zh'=4,'zl'=4,'y'=4,'core'=2] {'zh'}, dimensions={0}, use_global_device_ids=true | all-gather | bytes 327680 | tf_op jit(solution)/shard_map/all_gather | solution.py:302
  32.2 0.0 copy-start
  32.2 3.1 %collective-permute-start.1 = (bf16[144,1024]{1,0:T(8,128)(2,1)S(1)}, bf16[144,1024]{1,0:T(8,128)(2,1)S(1)}, u32[]{:S(2)}, u32[]{:S(2)}) collective-permute-start(bf16[144,1024]{1,0:T(8,128)(2,1)S(1)} %fusion.1), channel_id=1, source_target_pairs={{0,8},{1,9},{8,16},{9,17},{16,24},{17,25},{24,32},{25,33},{32,40},... | collective-permute-start | bytes 884744 | tf_op jit(solution)/shard_map/ppermute | solution.py:309
  35.3 2.9 %collective-permute-start = (bf16[128,1024]{1,0:T(8,128)(2,1)S(1)}, bf16[128,1024]{1,0:T(8,128)(2,1)S(1)}, u32[]{:S(2)}, u32[]{:S(2)}) collective-permute-start(bf16[128,1024]{1,0:T(8,128)(2,1)S(1)} %all_gather.9.w0), channel_id=1, source_target_pairs={{0,120},{1,121},{8,0},{9,1},{16,8},{17,9},{24,16},{25,17},{32,24},... | collective-permute-start | bytes 786440 | tf_op jit(solution)/shard_map/ppermute | solution.py:309
  38.2 4.2 %collective-permute-start.2 = (bf16[128,1024]{1,0:T(8,128)(2,1)S(1)}, bf16[128,1024]{1,0:T(8,128)(2,1)S(1)}, u32[]{:S(2)}, u32[]{:S(2)}) collective-permute-start(bf16[128,1024]{1,0:T(8,128)(2,1)S(1)} %all_gather.9.w0), channel_id=1, source_target_pairs={{0,112},{1,17},{8,120},{9,25},{16,0},{17,33},{24,8},{25,41},{32,16... | collective-permute-start | bytes 786440 | tf_op jit(solution)/shard_map/ppermute | solution.py:309
  42.4 0.0 copy-start.7
  43.1 0.0 copy-done.7
  43.1 0.1 copy.13.step
  43.2 0.1 pad_add_fusion.place
  43.3 0.6 copy-done.2
  43.9 0.1 copy-done.4
  43.9 1.8 %shard_map.110 = (bf16[128,1024]{1,0:T(8,128)(2,1)S(1)}, f32[128,16]{1,0:T(8,128)S(1)}, f32[16,128]{1,0:T(8,128)S(1)}, bf16[1024,128]{1,0:T(8,128)(2,1)S(1)}, bf16[16,16,128]{2,1,0:T(8,128)(2,1)S(1)}) custom-call(s32[4]{0:T(128)S(1)} %pad_add_fusion.place, bf16[128,1024]{1,0:T(8,128)(2,1)S(1)} %copy-done, bf16[16,1024]{1,0:T(8,128)(2,1)S(1)} %copy-done.2, ...), custom_call_target="tpu_custom_call" | custom-call | flops 1000000 | bytes 1000000 | tf_op jit(solution)/shard_map/pallas_call | solution.py:51
  45.7 1.9 %collective-permute-done.2.w3 = bf16[128,1024]{1,0:T(8,128)(2,1)S(1)} collective-permute-done((bf16[128,1024]{1,0:T(8,128)(2,1)S(1)}, bf16[128,1024]{1,0:T(8,128)(2,1)S(1)}, u32[]{:S(2)}, u32[]{:S(2)}) %collective-permute-start.2) | collective-permute-done | bytes 262176 | tf_op jit(solution)/shard_map/ppermute | solution.py:309
  47.6 1.5 %shard_map.111 = bf16[4,2,144,256]{3,2,1,0:T(8,128)(2,1)S(1)} custom-call(s32[4]{0:T(128)S(1)} %pad_add_fusion.place, bf16[128,1024]{1,0:T(8,128)(2,1)S(1)} %all_gather.9.w0, bf16[128,1024]{1,0:T(8,128)(2,1)S(1)} %collective-permute-done.w1, bf16[144,1024]{1,0:T(8,128)(2,1)S(1)} %collective-permute-done.1.w2, ...), custom_call_target="tpu_custom_call" | custom-call | flops 1000000 | bytes 1000000 | tf_op jit(solution)/shard_map/pallas_call | solution.py:51
  49.1 15.4 %all_to_all.20.parts = bf16[8,144,256]{2,1,0:T(8,128)(2,1)S(1)} all-to-all(bf16[8,144,256]{2,1,0:T(8,128)(2,1)S(1)} %bitcast.9), channel_id=1, replica_groups=mesh['x'=4,'zh'=4,'zl'=4,'y'=4,'core'=2] {'y','core'}, dimensions={0} | all-to-all | bytes 1179648 | tf_op jit(solution)/shard_map/all_to_all | solution.py:30
  64.4 0.6 shard_map.112
  65.1 7.1 %collective-permute-start.3 = (bf16[144,256]{1,0:T(8,128)(2,1)S(1)}, bf16[144,256]{1,0:T(8,128)(2,1)S(1)}, u32[]{:S(2)}, u32[]{:S(2)}) collective-permute-start(bf16[144,256]{1,0:T(8,128)(2,1)S(1)} %shard_map.112), channel_id=1, source_target_pairs={{0,256},{2,384},{4,0},{6,128},{128,258},{130,386},{132,2},{134,130... | collective-permute-start | bytes 221192 | tf_op jit(solution)/shard_map/ppermute | solution.py:43
  72.2 2.0 %collective-permute-done.3.sums = bf16[144,256]{1,0:T(8,128)(2,1)S(1)} collective-permute-done((bf16[144,256]{1,0:T(8,128)(2,1)S(1)}, bf16[144,256]{1,0:T(8,128)(2,1)S(1)}, u32[]{:S(2)}, u32[]{:S(2)}) %collective-permute-start.3) | collective-permute-done | bytes 73760 | tf_op jit(solution)/shard_map/ppermute | solution.py:43
  74.1 0.8 shard_map.113
  75.0 20.7 %all_to_all.21.got = bf16[16,80,128]{2,1,0:T(8,128)(2,1)S(1)} all-to-all(bf16[16,80,128]{2,1,0:T(8,128)(2,1)S(1)} %get-tuple-element.33), channel_id=1, replica_groups=mesh['x'=4,'zh'=4,'zl'=4,'y'=4,'core'=2] {'x','zl'}, dimensions={0} | all-to-all | bytes 655360 | tf_op jit(solution)/shard_map/all_to_all | solution.py:30
  95.6 0.6 shard_map.114
  96.3 20.0 %all-gather = bf16[1088,128]{1,0:T(8,128)(2,1)S(1)} all-gather(bf16[272,128]{1,0:T(8,128)(2,1)S(1)} %shard_map.114), channel_id=2, replica_groups=mesh['x'=4,'zh'=4,'zl'=4,'y'=4,'core'=2] {'zh'}, dimensions={0}, use_global_device_ids=true | all-gather | bytes 348160 | tf_op jit(solution)/shard_map/all_gather | solution.py:365
  116.2 1.4 %shard_map.115 = bf16[16,64,128]{2,1,0:T(8,128)(2,1)} custom-call(s32[4]{0:T(128)S(1)} %pad_add_fusion.place, bf16[4,272,128]{2,1,0:T(8,128)(2,1)S(1)} %bitcast.10, bf16[16,80,128]{2,1,0:T(8,128)(2,1)S(1)} %all_to_all.21.got), custom_call_target="tpu_custom_call" | custom-call | flops 1000000 | bytes 1000000 | tf_op jit(solution)/shard_map/pallas_call | solution.py:51
  117.6 4.7 %all-to-all-start.3 = ((bf16[16,64,128]{2,1,0:T(8,128)(2,1)}), bf16[16,64,128]{2,1,0:T(8,128)(2,1)S(1)}, u32[]{:S(2)}, u32[]{:S(2)}) async-start(bf16[16,64,128]{2,1,0:T(8,128)(2,1)} %shard_map.115), calls=%async_computation.3 | async-start | bytes 524288 | tf_op jit(solution)/shard_map/all_to_all | solution.py:30
  122.4 0.0 copy-start.5
  122.4 0.6 copy-done.5
  123.1 1.4 %shard_map.116 = (f32[128,1024]{1,0:T(8,128)S(1)}, f32[128,1024]{1,0:T(8,128)S(1)}) custom-call(s32[4]{0:T(128)S(1)} %pad_add_fusion.place, bf16[128,256]{1,0:T(8,128)(2,1)S(1)} %get-tuple-element.32.keys, bf16[128,1024]{1,0:T(8,128)(2,1)S(1)} %get-tuple-element.34.driven, f32[128,16]{1,0:T(8,128)S(1)} %get-tuple-element.35.cum, ...), custom_call_target="tpu_custom_call" | custom-call | flops 1000000 | bytes 1000000 | tf_op jit(solution)/shard_map/pallas_call | solution.py:51
  124.4 6.4 %all-to-all-done.3 = bf16[16,64,128]{2,1,0:T(8,128)(2,1)S(1)} async-done(((bf16[16,64,128]{2,1,0:T(8,128)(2,1)}), bf16[16,64,128]{2,1,0:T(8,128)(2,1)S(1)}, u32[]{:S(2)}, u32[]{:S(2)}) %all-to-all-start.3) | async-done | bytes 262176 | tf_op jit(solution)/shard_map/all_to_all | solution.py:30
  130.8 1.6 %shard_map.117 = bf16[128,1024]{1,0:T(8,128)(2,1)} custom-call(s32[4]{0:T(128)S(1)} %pad_add_fusion.place, bf16[128,256]{1,0:T(8,128)(2,1)S(1)} %get-tuple-element.32.keys, bf16[1024,128]{1,0:T(8,128)(2,1)S(1)} %bitcast.11, f32[128,1024]{1,0:T(8,128)S(1)} %get-tuple-element.37.mixed, f32[128,1024]{1,0:T(8,128)S(1)} %get-tuple-element.38.grown, ...), custom_call_target="tpu_custom_call" | custom-call | flops 1000000 | bytes 1000000 | tf_op jit(solution)/shard_map/pallas_call | solution.py:51
  (17 shorter events, 0.1 us)
Async XLA Ops:
  2.0 4.5 %copy-start.6 = (bf16[1024,32]{0,1:T(8,128)(2,1)S(1)}, bf16[1024,32]{0,1:T(8,128)(2,1)}, u32[]{:S(2)}) copy-start(bf16[1024,32]{0,1:T(8,128)(2,1)} %param.12) | copy-start | bytes 196612
  2.0 30.1 %all-to-all-start = ((bf16[4,128,1024]{2,1,0:T(8,128)(2,1)}), bf16[4,128,1024]{2,1,0:T(8,128)(2,1)S(1)}, u32[]{:S(2)}, u32[]{:S(2)}) async-start(bf16[4,128,1024]{2,1,0:T(8,128)(2,1)} %shard_map.109), calls=%async_computation | async-start | bytes 2097152 | tf_op jit(solution)/shard_map/all_to_all | solution.py:30
  32.2 11.1 %copy-start = (bf16[128,1024]{1,0:T(8,128)(2,1)S(1)}, bf16[128,1024]{1,0:T(8,128)(2,1)}, u32[]{:S(2)}) copy-start(bf16[128,1024]{1,0:T(8,128)(2,1)} %inner.3) | copy-start | bytes 786436
  32.2 15.4 %collective-permute-start.1 = (bf16[144,1024]{1,0:T(8,128)(2,1)S(1)}, bf16[144,1024]{1,0:T(8,128)(2,1)S(1)}, u32[]{:S(2)}, u32[]{:S(2)}) collective-permute-start(bf16[144,1024]{1,0:T(8,128)(2,1)S(1)} %fusion.1), channel_id=1, source_target_pairs={{0,8},{1,9},{8,16},{9,17},{16,24},{17,25},{24,32},{25,33},{32,40},... | collective-permute-start | bytes 884744 | tf_op jit(solution)/shard_map/ppermute | solution.py:309
  35.3 10.4 %collective-permute-start = (bf16[128,1024]{1,0:T(8,128)(2,1)S(1)}, bf16[128,1024]{1,0:T(8,128)(2,1)S(1)}, u32[]{:S(2)}, u32[]{:S(2)}) collective-permute-start(bf16[128,1024]{1,0:T(8,128)(2,1)S(1)} %all_gather.9.w0), channel_id=1, source_target_pairs={{0,120},{1,121},{8,0},{9,1},{16,8},{17,9},{24,16},{25,17},{32,24},... | collective-permute-start | bytes 786440 | tf_op jit(solution)/shard_map/ppermute | solution.py:309
  38.2 9.4 %collective-permute-start.2 = (bf16[128,1024]{1,0:T(8,128)(2,1)S(1)}, bf16[128,1024]{1,0:T(8,128)(2,1)S(1)}, u32[]{:S(2)}, u32[]{:S(2)}) collective-permute-start(bf16[128,1024]{1,0:T(8,128)(2,1)S(1)} %all_gather.9.w0), channel_id=1, source_target_pairs={{0,112},{1,17},{8,120},{9,25},{16,0},{17,33},{24,8},{25,41},{32,16... | collective-permute-start | bytes 786440 | tf_op jit(solution)/shard_map/ppermute | solution.py:309
  42.4 0.7 copy-start.7
  43.1 0.8 copy-start.2
  43.3 0.7 copy-start.4
  64.4 9.7 %copy-start.3 = (f32[4,256]{1,0:T(4,128)S(1)}, f32[4,256]{1,0:T(4,128)}, u32[]{:S(2)}) copy-start(f32[4,256]{1,0:T(4,128)} %taps.1) | copy-start | bytes 12292
  65.1 9.0 %collective-permute-start.3 = (bf16[144,256]{1,0:T(8,128)(2,1)S(1)}, bf16[144,256]{1,0:T(8,128)(2,1)S(1)}, u32[]{:S(2)}, u32[]{:S(2)}) collective-permute-start(bf16[144,256]{1,0:T(8,128)(2,1)S(1)} %shard_map.112), channel_id=1, source_target_pairs={{0,256},{2,384},{4,0},{6,128},{128,258},{130,386},{132,2},{134,130... | collective-permute-start | bytes 221192 | tf_op jit(solution)/shard_map/ppermute | solution.py:43
  117.6 4.8 %copy-start.8 = (bf16[1024]{0:T(1024)(128)(2,1)S(1)}, bf16[1024]{0:T(1024)(128)(2,1)}, u32[]{:S(2)}) copy-start(bf16[1024]{0:T(1024)(128)(2,1)} %param.21) | copy-start | bytes 6148
  117.6 4.8 %copy-start.1 = (bf16[128,1024]{1,0:T(8,128)(2,1)S(1)}, bf16[128,1024]{1,0:T(8,128)(2,1)}, u32[]{:S(2)}) copy-start(bf16[128,1024]{1,0:T(8,128)(2,1)} %gate.1) | copy-start | bytes 786436
  117.6 13.2 %all-to-all-start.3 = ((bf16[16,64,128]{2,1,0:T(8,128)(2,1)}), bf16[16,64,128]{2,1,0:T(8,128)(2,1)S(1)}, u32[]{:S(2)}, u32[]{:S(2)}) async-start(bf16[16,64,128]{2,1,0:T(8,128)(2,1)} %shard_map.115), calls=%async_computation.3 | async-start | bytes 524288 | tf_op jit(solution)/shard_map/all_to_all | solution.py:30
  122.4 0.7 copy-start.5

commit v6 on v5

--- a/solution.py
+++ b/solution.py
@@ -8,7 +8,6 @@
 N = 128
 Q = 128
 QUAD = 4
-W_STEPS = (0, 1, -1, 2)
 HALO = 16
 REACH = 3
 LOG_ROWS = 16
@@ -125,15 +124,19 @@
         copy.wait()
 
 
-def project_kernel(place, w0, w1, w2, w3, rows, out, w_in_order, all_rows):
+def project_kernel(place, own, one, other, across, rows, out, w_in_order, all_rows):
     n_part = N // QUAD
-    halves = w0.shape[0] // n_part
-    for w, step in zip((w0, w1, w2, w3), W_STEPS):
-        s = lax.rem(place[2] + step + QUAD, QUAD)
+    halves = own.shape[0] // n_part
+    zl, core = place[2], place[4]
+    steps = (0, 2 * core - 1, 1 - 2 * core, 2)
+    for w, step in zip((own, one, other, across), steps):
+        s = lax.rem(zl + step + QUAD, QUAD)
         for i in range(halves):
             at = pl.multiple_of(i * N + s * n_part, n_part)
             w_in_order[pl.ds(at, n_part)] = w[i * n_part : (i + 1) * n_part]
-    packed = w2[halves * n_part :].astype(f32)
+    packed = jnp.where(
+        core == 0, one[halves * n_part :].astype(f32), other[halves * n_part :].astype(f32)
+    )
     tails = [
         pltpu.roll(packed, (HALO - (i + 1) * REACH) % HALO, 0).astype(bf16)
         for i in range(rows.shape[0])
@@ -279,7 +282,7 @@
     width = inner_input.shape[1]
     head_width = width // heads
     x, zh, zl = (lax.axis_index(a) for a in CTX)
-    place = jnp.stack([x, zh, zl, tenant_index[0]])
+    place = jnp.stack([x, zh, zl, tenant_index[0], lax.axis_index("core")])
     n_z = lax.axis_size(Z)
     n_x = lax.axis_size("x")
     depth = hidden_states.shape[1]
@@ -305,18 +308,17 @@
     tails = jnp.pad(
         rows[:, Q - REACH :].reshape(n_x * REACH, depth), ((0, HALO - n_x * REACH), (0, 0))
     )
-    w_all = [w_zh] + [
-        lax.ppermute(
-            jnp.concatenate([w_zh, tails], axis=0) if step == -1 else w_zh,
-            Z + ("core",),
-            [
-                (i * n_core + c, (i - step * (1 if c == 0 else turn)) % n_z * n_core + c)
-                for i in range(n_z)
-                for c in range(n_core)
-            ],
-        )
-        for step, turn in zip(W_STEPS[1:], (1, 1, -1))
-    ]
+    both = jnp.concatenate([w_zh, tails], axis=0)
+
+    def from_side(block, step):
+        pairs = [
+            (i * n_core + c, (i + step * (1 - 2 * c)) % n_z * n_core + c)
+            for i in range(n_z)
+            for c in range(n_core)
+        ]
+        return lax.ppermute(block, Z + ("core",), pairs)
+
+    w_all = [w_zh, from_side(both, 1), from_side(both, -1), from_side(w_zh, 2)]
 
     driven, cum, cum_t, weighted_t, logs = kernel_call(
         drive_kernel,

time: 133 us -> 132 us (level)
  waiting for transfers between devices: 10.2 us -> 13.3 us
  blocking collectives: 81.7 us -> 79.5 us
  starting transfers between devices: 26.4 us -> 24.4 us
    ppermute x3, waiting for transfers between devices: 1.91 us -> 4.59 us  [from_side(): return lax.ppermute(block, Z + ('core',), pairs)]
    ppermute x1, starting transfers between devices: 7.08 us -> 5.53 us  [to_owner(): return lax.ppermute(block, ('x', 'y'), pairs)]
    all_to_all x2, blocking collectives: 36 us -> 34.7 us  [swap(): return lax.all_to_all(blocks, axis, 0, 0, tiled=True)]
where the time goes in v6:
time: 132 us; the launch traced here: 131 us
  blocking collectives  79.5 us (60%)
  starting transfers between devices  24.4 us (18%)
  waiting for transfers between devices  13.3 us (10%)
  Pallas kernels  11.6 us (9%)
  local copies, waits for them, and re-layouts  1.59 us (1%)
    all_to_all x2, blocking collectives, swap(): return lax.all_to_all(blocks, axis, 0, 0, tiled=True)  34.7 us
    all_gather x1, blocking collectives, per_device(): w_zh = lax.all_gather(select_weight.T, 'zh', axis=0, tiled=True)  25.7 us
    all_gather x1, blocking collectives, per_device(): lax.all_gather(total, 'zh')  19.2 us
    pallas_call x8, Pallas kernels, kernel_call(): pl.pallas_call(body, out_shape=outs, in_specs=[SMEM] + [VMEM] * len(args)...  9.64 us
    all_to_all x2, starting transfers between devices, swap(): return lax.all_to_all(blocks, axis, 0, 0, tiled=True)  9.54 us
    ppermute x3, starting transfers between devices, from_side(): return lax.ppermute(block, Z + ('core',), pairs)  9.28 us
    all_to_all x2, waiting for transfers between devices, swap(): return lax.all_to_all(blocks, axis, 0, 0, tiled=True)  6.36 us
    ppermute x1, starting transfers between devices, to_owner(): return lax.ppermute(block, ('x', 'y'), pairs)  5.53 us
  transfers between devices with their start and end apart: 6, of which 3 were waited for; matrix products, arithmetic and copies ran while one was open for 0% of the time, Pallas kernels for 2%

profile of v6, /device:TPU:32, one launch (start us, length us, event | category | flops | bytes accessed | tf_op | source)
XLA Modules:
  0.0 131.3 jit_solution(13337193921652388273)
XLA Ops:
  0.0 2.0 %shard_map.109 = bf16[4,128,1024]{2,1,0:T(8,128)(2,1)} custom-call(bf16[128,1024]{1,0:T(8,128)(2,1)} %block.1), custom_call_target="tpu_custom_call" | custom-call | bytes 1000000 | tf_op jit(solution)/shard_map/pallas_call | solution.py:290
  2.0 0.0 copy-start.6
  2.0 4.4 %all-to-all-start = ((bf16[4,128,1024]{2,1,0:T(8,128)(2,1)}), bf16[4,128,1024]{2,1,0:T(8,128)(2,1)S(1)}, u32[]{:S(2)}, u32[]{:S(2)}) async-start(bf16[4,128,1024]{2,1,0:T(8,128)(2,1)} %shard_map.109), calls=%async_computation | async-start | bytes 2097152 | tf_op jit(solution)/shard_map/all_to_all | solution.py:29
  6.4 25.7 %all_gather.9.own = bf16[128,1024]{1,0:T(8,128)(2,1)S(1)} all-gather(bf16[32,1024]{1,0:T(8,128)(2,1)S(1)} %bitcast.15), channel_id=1, replica_groups=mesh['x'=4,'zh'=4,'zl'=4,'y'=4,'core'=2] {'zh'}, dimensions={0}, use_global_device_ids=true | all-gather | bytes 327680 | tf_op jit(solution)/shard_map/all_gather | solution.py:305
  32.2 0.0 copy-start
  32.2 3.1 %collective-permute-start = (bf16[144,1024]{1,0:T(8,128)(2,1)S(1)}, bf16[144,1024]{1,0:T(8,128)(2,1)S(1)}, u32[]{:S(2)}, u32[]{:S(2)}) collective-permute-start(bf16[144,1024]{1,0:T(8,128)(2,1)S(1)} %fusion.1), channel_id=1, source_target_pairs={{0,8},{1,121},{8,16},{9,1},{16,24},{17,9},{24,32},{25,17},{32,40},... | collective-permute-start | bytes 884744 | tf_op jit(solution)/shard_map/ppermute | solution.py:319
  35.3 2.9 %collective-permute-start.1 = (bf16[144,1024]{1,0:T(8,128)(2,1)S(1)}, bf16[144,1024]{1,0:T(8,128)(2,1)S(1)}, u32[]{:S(2)}, u32[]{:S(2)}) collective-permute-start(bf16[144,1024]{1,0:T(8,128)(2,1)S(1)} %fusion.1), channel_id=1, source_target_pairs={{0,120},{1,9},{8,0},{9,17},{16,8},{17,25},{24,16},{25,33},{32,24},... | collective-permute-start | bytes 884744 | tf_op jit(solution)/shard_map/ppermute | solution.py:319
  38.2 3.3 %collective-permute-start.2 = (bf16[128,1024]{1,0:T(8,128)(2,1)S(1)}, bf16[128,1024]{1,0:T(8,128)(2,1)S(1)}, u32[]{:S(2)}, u32[]{:S(2)}) collective-permute-start(bf16[128,1024]{1,0:T(8,128)(2,1)S(1)} %all_gather.9.own), channel_id=1, source_target_pairs={{0,16},{1,113},{8,24},{9,121},{16,32},{17,1},{24,40},{25,9},{32,48... | collective-permute-start | bytes 786440 | tf_op jit(solution)/shard_map/ppermute | solution.py:319
  41.5 0.0 copy-start.7
  42.2 0.0 copy-done.7
  42.2 0.1 copy.13.step
  42.3 0.1 stack.19.place
  42.4 0.6 copy-done.2
  43.0 0.1 copy-done.4
  43.1 1.8 %shard_map.110 = (bf16[128,1024]{1,0:T(8,128)(2,1)S(1)}, f32[128,16]{1,0:T(8,128)S(1)}, f32[16,128]{1,0:T(8,128)S(1)}, bf16[1024,128]{1,0:T(8,128)(2,1)S(1)}, bf16[16,16,128]{2,1,0:T(8,128)(2,1)S(1)}) custom-call(s32[5]{0:T(128)S(1)} %stack.19.place, bf16[128,1024]{1,0:T(8,128)(2,1)S(1)} %copy-done, bf16[16,1024]{1,0:T(8,128)(2,1)S(1)} %copy-done.2, ...), custom_call_target="tpu_custom_call" | custom-call | flops 1000000 | bytes 1000000 | tf_op jit(solution)/shard_map/pallas_call | solution.py:50
  44.8 4.6 %collective-permute-done.2.across = bf16[128,1024]{1,0:T(8,128)(2,1)S(1)} collective-permute-done((bf16[128,1024]{1,0:T(8,128)(2,1)S(1)}, bf16[128,1024]{1,0:T(8,128)(2,1)S(1)}, u32[]{:S(2)}, u32[]{:S(2)}) %collective-permute-start.2) | collective-permute-done | bytes 262176 | tf_op jit(solution)/shard_map/ppermute | solution.py:319
  49.4 1.4 %shard_map.111 = bf16[4,2,144,256]{3,2,1,0:T(8,128)(2,1)S(1)} custom-call(s32[5]{0:T(128)S(1)} %stack.19.place, bf16[128,1024]{1,0:T(8,128)(2,1)S(1)} %all_gather.9.own, bf16[144,1024]{1,0:T(8,128)(2,1)S(1)} %collective-permute-done.one, bf16[144,1024]{1,0:T(8,128)(2,1)S(1)} %collective-permute-done.1.other, ...), custom_call_target="tpu_custom_call" | custom-call | flops 1000000 | bytes 1000000 | tf_op jit(solution)/shard_map/pallas_call | solution.py:50
  50.9 15.4 %all_to_all.20.parts = bf16[8,144,256]{2,1,0:T(8,128)(2,1)S(1)} all-to-all(bf16[8,144,256]{2,1,0:T(8,128)(2,1)S(1)} %bitcast.10), channel_id=1, replica_groups=mesh['x'=4,'zh'=4,'zl'=4,'y'=4,'core'=2] {'y','core'}, dimensions={0} | all-to-all | bytes 1179648 | tf_op jit(solution)/shard_map/all_to_all | solution.py:29
  66.2 0.6 shard_map.112
  66.9 5.5 %collective-permute-start.3 = (bf16[144,256]{1,0:T(8,128)(2,1)S(1)}, bf16[144,256]{1,0:T(8,128)(2,1)S(1)}, u32[]{:S(2)}, u32[]{:S(2)}) collective-permute-start(bf16[144,256]{1,0:T(8,128)(2,1)S(1)} %shard_map.112), channel_id=1, source_target_pairs={{0,256},{2,384},{4,0},{6,128},{128,258},{130,386},{132,2},{134,130... | collective-permute-start | bytes 221192 | tf_op jit(solution)/shard_map/ppermute | solution.py:42
  72.4 2.4 %collective-permute-done.3.sums = bf16[144,256]{1,0:T(8,128)(2,1)S(1)} collective-permute-done((bf16[144,256]{1,0:T(8,128)(2,1)S(1)}, bf16[144,256]{1,0:T(8,128)(2,1)S(1)}, u32[]{:S(2)}, u32[]{:S(2)}) %collective-permute-start.3) | collective-permute-done | bytes 73760 | tf_op jit(solution)/shard_map/ppermute | solution.py:42
  74.8 0.8 shard_map.113
  75.6 19.3 %all_to_all.21.got = bf16[16,80,128]{2,1,0:T(8,128)(2,1)S(1)} all-to-all(bf16[16,80,128]{2,1,0:T(8,128)(2,1)S(1)} %get-tuple-element.33), channel_id=1, replica_groups=mesh['x'=4,'zh'=4,'zl'=4,'y'=4,'core'=2] {'x','zl'}, dimensions={0} | all-to-all | bytes 655360 | tf_op jit(solution)/shard_map/all_to_all | solution.py:29
  94.9 0.6 shard_map.114
  95.5 19.2 %all-gather = bf16[1088,128]{1,0:T(8,128)(2,1)S(1)} all-gather(bf16[272,128]{1,0:T(8,128)(2,1)S(1)} %shard_map.114), channel_id=2, replica_groups=mesh['x'=4,'zh'=4,'zl'=4,'y'=4,'core'=2] {'zh'}, dimensions={0}, use_global_device_ids=true | all-gather | bytes 348160 | tf_op jit(solution)/shard_map/all_gather | solution.py:367
  114.8 1.4 %shard_map.115 = bf16[16,64,128]{2,1,0:T(8,128)(2,1)} custom-call(s32[5]{0:T(128)S(1)} %stack.19.place, bf16[4,272,128]{2,1,0:T(8,128)(2,1)S(1)} %bitcast.11, bf16[16,80,128]{2,1,0:T(8,128)(2,1)S(1)} %all_to_all.21.got), custom_call_target="tpu_custom_call" | custom-call | flops 1000000 | bytes 1000000 | tf_op jit(solution)/shard_map/pallas_call | solution.py:50
  116.2 5.1 %all-to-all-start.3 = ((bf16[16,64,128]{2,1,0:T(8,128)(2,1)}), bf16[16,64,128]{2,1,0:T(8,128)(2,1)S(1)}, u32[]{:S(2)}, u32[]{:S(2)}) async-start(bf16[16,64,128]{2,1,0:T(8,128)(2,1)} %shard_map.115), calls=%async_computation.3 | async-start | bytes 524288 | tf_op jit(solution)/shard_map/all_to_all | solution.py:29
  121.3 0.0 copy-start.5
  121.3 0.6 copy-done.5
  121.9 1.4 %shard_map.116 = (f32[128,1024]{1,0:T(8,128)S(1)}, f32[128,1024]{1,0:T(8,128)S(1)}) custom-call(s32[5]{0:T(128)S(1)} %stack.19.place, bf16[128,256]{1,0:T(8,128)(2,1)S(1)} %get-tuple-element.32.keys, bf16[128,1024]{1,0:T(8,128)(2,1)S(1)} %get-tuple-element.34.driven, f32[128,16]{1,0:T(8,128)S(1)} %get-tuple-element.35.cum, ...), custom_call_target="tpu_custom_call" | custom-call | flops 1000000 | bytes 1000000 | tf_op jit(solution)/shard_map/pallas_call | solution.py:50
  123.3 6.4 %all-to-all-done.3 = bf16[16,64,128]{2,1,0:T(8,128)(2,1)S(1)} async-done(((bf16[16,64,128]{2,1,0:T(8,128)(2,1)}), bf16[16,64,128]{2,1,0:T(8,128)(2,1)S(1)}, u32[]{:S(2)}, u32[]{:S(2)}) %all-to-all-start.3) | async-done | bytes 262176 | tf_op jit(solution)/shard_map/all_to_all | solution.py:29
  129.7 1.6 %shard_map.117 = bf16[128,1024]{1,0:T(8,128)(2,1)} custom-call(s32[5]{0:T(128)S(1)} %stack.19.place, bf16[128,256]{1,0:T(8,128)(2,1)S(1)} %get-tuple-element.32.keys, bf16[1024,128]{1,0:T(8,128)(2,1)S(1)} %bitcast.12, f32[128,1024]{1,0:T(8,128)S(1)} %get-tuple-element.37.mixed, f32[128,1024]{1,0:T(8,128)S(1)} %get-tuple-element.38.grown, ...), custom_call_target="tpu_custom_call" | custom-call | flops 1000000 | bytes 1000000 | tf_op jit(solution)/shard_map/pallas_call | solution.py:50
  (17 shorter events, 0.1 us)
Async XLA Ops:
  2.0 4.5 %copy-start.6 = (bf16[1024,32]{0,1:T(8,128)(2,1)S(1)}, bf16[1024,32]{0,1:T(8,128)(2,1)}, u32[]{:S(2)}) copy-start(bf16[1024,32]{0,1:T(8,128)(2,1)} %param.12) | copy-start | bytes 196612
  2.0 30.1 %all-to-all-start = ((bf16[4,128,1024]{2,1,0:T(8,128)(2,1)}), bf16[4,128,1024]{2,1,0:T(8,128)(2,1)S(1)}, u32[]{:S(2)}, u32[]{:S(2)}) async-start(bf16[4,128,1024]{2,1,0:T(8,128)(2,1)} %shard_map.109), calls=%async_computation | async-start | bytes 2097152 | tf_op jit(solution)/shard_map/all_to_all | solution.py:29
  32.2 10.2 %copy-start = (bf16[128,1024]{1,0:T(8,128)(2,1)S(1)}, bf16[128,1024]{1,0:T(8,128)(2,1)}, u32[]{:S(2)}) copy-start(bf16[128,1024]{1,0:T(8,128)(2,1)} %inner.3) | copy-start | bytes 786436
  32.2 17.2 %collective-permute-start = (bf16[144,1024]{1,0:T(8,128)(2,1)S(1)}, bf16[144,1024]{1,0:T(8,128)(2,1)S(1)}, u32[]{:S(2)}, u32[]{:S(2)}) collective-permute-start(bf16[144,1024]{1,0:T(8,128)(2,1)S(1)} %fusion.1), channel_id=1, source_target_pairs={{0,8},{1,121},{8,16},{9,1},{16,24},{17,9},{24,32},{25,17},{32,40},... | collective-permute-start | bytes 884744 | tf_op jit(solution)/shard_map/ppermute | solution.py:319
  35.3 14.1 %collective-permute-start.1 = (bf16[144,1024]{1,0:T(8,128)(2,1)S(1)}, bf16[144,1024]{1,0:T(8,128)(2,1)S(1)}, u32[]{:S(2)}, u32[]{:S(2)}) collective-permute-start(bf16[144,1024]{1,0:T(8,128)(2,1)S(1)} %fusion.1), channel_id=1, source_target_pairs={{0,120},{1,9},{8,0},{9,17},{16,8},{17,25},{24,16},{25,33},{32,24},... | collective-permute-start | bytes 884744 | tf_op jit(solution)/shard_map/ppermute | solution.py:319
  38.2 11.2 %collective-permute-start.2 = (bf16[128,1024]{1,0:T(8,128)(2,1)S(1)}, bf16[128,1024]{1,0:T(8,128)(2,1)S(1)}, u32[]{:S(2)}, u32[]{:S(2)}) collective-permute-start(bf16[128,1024]{1,0:T(8,128)(2,1)S(1)} %all_gather.9.own), channel_id=1, source_target_pairs={{0,16},{1,113},{8,24},{9,121},{16,32},{17,1},{24,40},{25,9},{32,48... | collective-permute-start | bytes 786440 | tf_op jit(solution)/shard_map/ppermute | solution.py:319
  41.5 0.7 copy-start.7
  42.2 0.8 copy-start.2
  42.4 0.7 copy-start.4
  66.2 8.6 %copy-start.3 = (f32[4,256]{1,0:T(4,128)S(1)}, f32[4,256]{1,0:T(4,128)}, u32[]{:S(2)}) copy-start(f32[4,256]{1,0:T(4,128)} %taps.1) | copy-start | bytes 12292
  66.9 7.9 %collective-permute-start.3 = (bf16[144,256]{1,0:T(8,128)(2,1)S(1)}, bf16[144,256]{1,0:T(8,128)(2,1)S(1)}, u32[]{:S(2)}, u32[]{:S(2)}) collective-permute-start(bf16[144,256]{1,0:T(8,128)(2,1)S(1)} %shard_map.112), channel_id=1, source_target_pairs={{0,256},{2,384},{4,0},{6,128},{128,258},{130,386},{132,2},{134,130... | collective-permute-start | bytes 221192 | tf_op jit(solution)/shard_map/ppermute | solution.py:42
  116.2 5.1 %copy-start.8 = (bf16[1024]{0:T(1024)(128)(2,1)S(1)}, bf16[1024]{0:T(1024)(128)(2,1)}, u32[]{:S(2)}) copy-start(bf16[1024]{0:T(1024)(128)(2,1)} %param.21) | copy-start | bytes 6148
  116.2 5.1 %copy-start.1 = (bf16[128,1024]{1,0:T(8,128)(2,1)S(1)}, bf16[128,1024]{1,0:T(8,128)(2,1)}, u32[]{:S(2)}) copy-start(bf16[128,1024]{1,0:T(8,128)(2,1)} %gate.1) | copy-start | bytes 786436
  116.2 13.5 %all-to-all-start.3 = ((bf16[16,64,128]{2,1,0:T(8,128)(2,1)}), bf16[16,64,128]{2,1,0:T(8,128)(2,1)S(1)}, u32[]{:S(2)}, u32[]{:S(2)}) async-start(bf16[16,64,128]{2,1,0:T(8,128)(2,1)} %shard_map.115), calls=%async_computation.3 | async-start | bytes 524288 | tf_op jit(solution)/shard_map/all_to_all | solution.py:29
  121.3 0.7 copy-start.5

commit v7 on v6

--- a/solution.py
+++ b/solution.py
@@ -101,7 +101,11 @@
     so_far = jnp.dot(lower, log_decay, precision=EXACT, preferred_element_type=f32)
     cum[...] = so_far
     cum_t[...] = lax.dot_general(
-        log_decay, lower, (((0,), (1,)), ((), ())), precision=EXACT, preferred_element_type=f32
+        so_far,
+        jnp.where(rows == cols, 1.0, 0.0),
+        (((0,), (0,)), ((), ())),
+        precision=EXACT,
+        preferred_element_type=f32,
     )
     end = so_far[Q - 1 :]
     scaled = scaled_by_tenant(place[3], inner, scale)

time: 132 us -> 132 us (level)
  transfers between devices with their start and end apart: 6 -> 6, of which waited for: 3 -> 3; matrix products, arithmetic and copies ran while one was open for 0% -> 0% of each run, Pallas kernels for 2% -> 3%
where the time goes in v7:
time: 132 us; the launch traced here: 131 us
  blocking collectives  79.5 us (60%)
  starting transfers between devices  24.4 us (18%)
  waiting for transfers between devices  13.1 us (10%)
  Pallas kernels  11.8 us (9%)
  local copies, waits for them, and re-layouts  1.59 us (1%)
    all_to_all x2, blocking collectives, swap(): return lax.all_to_all(blocks, axis, 0, 0, tiled=True)  34.7 us
    all_gather x1, blocking collectives, per_device(): w_zh = lax.all_gather(select_weight.T, 'zh', axis=0, tiled=True)  25.7 us
    all_gather x1, blocking collectives, per_device(): lax.all_gather(total, 'zh')  19.2 us
    pallas_call x8, Pallas kernels, kernel_call(): pl.pallas_call(body, out_shape=outs, in_specs=[SMEM] + [VMEM] * len(args)...  9.83 us
    all_to_all x2, starting transfers between devices, swap(): return lax.all_to_all(blocks, axis, 0, 0, tiled=True)  9.54 us
    ppermute x3, starting transfers between devices, from_side(): return lax.ppermute(block, Z + ('core',), pairs)  9.28 us
    all_to_all x2, waiting for transfers between devices, swap(): return lax.all_to_all(blocks, axis, 0, 0, tiled=True)  6.36 us
    ppermute x1, starting transfers between devices, to_owner(): return lax.ppermute(block, ('x', 'y'), pairs)  5.53 us
  transfers between devices with their start and end apart: 6, of which 3 were waited for; matrix products, arithmetic and copies ran while one was open for 0% of the time, Pallas kernels for 3%

profile of v7, /device:TPU:32, one launch (start us, length us, event | category | flops | bytes accessed | tf_op | source)
XLA Modules:
  0.0 131.3 jit_solution(4133458636622883790)
XLA Ops:
  0.0 2.0 %shard_map.109 = bf16[4,128,1024]{2,1,0:T(8,128)(2,1)} custom-call(bf16[128,1024]{1,0:T(8,128)(2,1)} %block.1), custom_call_target="tpu_custom_call" | custom-call | bytes 1000000 | tf_op jit(solution)/shard_map/pallas_call | solution.py:294
  2.0 0.0 copy-start.6
  2.0 4.4 %all-to-all-start = ((bf16[4,128,1024]{2,1,0:T(8,128)(2,1)}), bf16[4,128,1024]{2,1,0:T(8,128)(2,1)S(1)}, u32[]{:S(2)}, u32[]{:S(2)}) async-start(bf16[4,128,1024]{2,1,0:T(8,128)(2,1)} %shard_map.109), calls=%async_computation | async-start | bytes 2097152 | tf_op jit(solution)/shard_map/all_to_all | solution.py:29
  6.4 25.7 %all_gather.9.own = bf16[128,1024]{1,0:T(8,128)(2,1)S(1)} all-gather(bf16[32,1024]{1,0:T(8,128)(2,1)S(1)} %bitcast.15), channel_id=1, replica_groups=mesh['x'=4,'zh'=4,'zl'=4,'y'=4,'core'=2] {'zh'}, dimensions={0}, use_global_device_ids=true | all-gather | bytes 327680 | tf_op jit(solution)/shard_map/all_gather | solution.py:309
  32.2 0.0 copy-start
  32.2 3.1 %collective-permute-start = (bf16[144,1024]{1,0:T(8,128)(2,1)S(1)}, bf16[144,1024]{1,0:T(8,128)(2,1)S(1)}, u32[]{:S(2)}, u32[]{:S(2)}) collective-permute-start(bf16[144,1024]{1,0:T(8,128)(2,1)S(1)} %fusion.1), channel_id=1, source_target_pairs={{0,8},{1,121},{8,16},{9,1},{16,24},{17,9},{24,32},{25,17},{32,40},... | collective-permute-start | bytes 884744 | tf_op jit(solution)/shard_map/ppermute | solution.py:323
  35.3 2.9 %collective-permute-start.1 = (bf16[144,1024]{1,0:T(8,128)(2,1)S(1)}, bf16[144,1024]{1,0:T(8,128)(2,1)S(1)}, u32[]{:S(2)}, u32[]{:S(2)}) collective-permute-start(bf16[144,1024]{1,0:T(8,128)(2,1)S(1)} %fusion.1), channel_id=1, source_target_pairs={{0,120},{1,9},{8,0},{9,17},{16,8},{17,25},{24,16},{25,33},{32,24},... | collective-permute-start | bytes 884744 | tf_op jit(solution)/shard_map/ppermute | solution.py:323
  38.2 3.3 %collective-permute-start.2 = (bf16[128,1024]{1,0:T(8,128)(2,1)S(1)}, bf16[128,1024]{1,0:T(8,128)(2,1)S(1)}, u32[]{:S(2)}, u32[]{:S(2)}) collective-permute-start(bf16[128,1024]{1,0:T(8,128)(2,1)S(1)} %all_gather.9.own), channel_id=1, source_target_pairs={{0,16},{1,113},{8,24},{9,121},{16,32},{17,1},{24,40},{25,9},{32,48... | collective-permute-start | bytes 786440 | tf_op jit(solution)/shard_map/ppermute | solution.py:323
  41.5 0.0 copy-start.7
  42.2 0.0 copy-done.7
  42.2 0.1 copy.13.step
  42.3 0.1 stack.19.place
  42.4 0.6 copy-done.2
  43.0 0.1 copy-done.4
  43.1 1.9 %shard_map.110 = (bf16[128,1024]{1,0:T(8,128)(2,1)S(1)}, f32[128,16]{1,0:T(8,128)S(1)}, f32[16,128]{1,0:T(8,128)S(1)}, bf16[1024,128]{1,0:T(8,128)(2,1)S(1)}, bf16[16,16,128]{2,1,0:T(8,128)(2,1)S(1)}) custom-call(s32[5]{0:T(128)S(1)} %stack.19.place, bf16[128,1024]{1,0:T(8,128)(2,1)S(1)} %copy-done, bf16[16,1024]{1,0:T(8,128)(2,1)S(1)} %copy-done.2, ...), custom_call_target="tpu_custom_call" | custom-call | flops 1000000 | bytes 1000000 | tf_op jit(solution)/shard_map/pallas_call | solution.py:50
  45.0 4.4 %collective-permute-done.2.across = bf16[128,1024]{1,0:T(8,128)(2,1)S(1)} collective-permute-done((bf16[128,1024]{1,0:T(8,128)(2,1)S(1)}, bf16[128,1024]{1,0:T(8,128)(2,1)S(1)}, u32[]{:S(2)}, u32[]{:S(2)}) %collective-permute-start.2) | collective-permute-done | bytes 262176 | tf_op jit(solution)/shard_map/ppermute | solution.py:323
  49.4 1.4 %shard_map.111 = bf16[4,2,144,256]{3,2,1,0:T(8,128)(2,1)S(1)} custom-call(s32[5]{0:T(128)S(1)} %stack.19.place, bf16[128,1024]{1,0:T(8,128)(2,1)S(1)} %all_gather.9.own, bf16[144,1024]{1,0:T(8,128)(2,1)S(1)} %collective-permute-done.one, bf16[144,1024]{1,0:T(8,128)(2,1)S(1)} %collective-permute-done.1.other, ...), custom_call_target="tpu_custom_call" | custom-call | flops 1000000 | bytes 1000000 | tf_op jit(solution)/shard_map/pallas_call | solution.py:50
  50.9 15.4 %all_to_all.20.parts = bf16[8,144,256]{2,1,0:T(8,128)(2,1)S(1)} all-to-all(bf16[8,144,256]{2,1,0:T(8,128)(2,1)S(1)} %bitcast.10), channel_id=1, replica_groups=mesh['x'=4,'zh'=4,'zl'=4,'y'=4,'core'=2] {'y','core'}, dimensions={0} | all-to-all | bytes 1179648 | tf_op jit(solution)/shard_map/all_to_all | solution.py:29
  66.2 0.6 shard_map.112
  66.9 5.5 %collective-permute-start.3 = (bf16[144,256]{1,0:T(8,128)(2,1)S(1)}, bf16[144,256]{1,0:T(8,128)(2,1)S(1)}, u32[]{:S(2)}, u32[]{:S(2)}) collective-permute-start(bf16[144,256]{1,0:T(8,128)(2,1)S(1)} %shard_map.112), channel_id=1, source_target_pairs={{0,256},{2,384},{4,0},{6,128},{128,258},{130,386},{132,2},{134,130... | collective-permute-start | bytes 221192 | tf_op jit(solution)/shard_map/ppermute | solution.py:42
  72.4 2.4 %collective-permute-done.3.sums = bf16[144,256]{1,0:T(8,128)(2,1)S(1)} collective-permute-done((bf16[144,256]{1,0:T(8,128)(2,1)S(1)}, bf16[144,256]{1,0:T(8,128)(2,1)S(1)}, u32[]{:S(2)}, u32[]{:S(2)}) %collective-permute-start.3) | collective-permute-done | bytes 73760 | tf_op jit(solution)/shard_map/ppermute | solution.py:42
  74.8 0.8 shard_map.113
  75.6 19.3 %all_to_all.21.got = bf16[16,80,128]{2,1,0:T(8,128)(2,1)S(1)} all-to-all(bf16[16,80,128]{2,1,0:T(8,128)(2,1)S(1)} %get-tuple-element.33), channel_id=1, replica_groups=mesh['x'=4,'zh'=4,'zl'=4,'y'=4,'core'=2] {'x','zl'}, dimensions={0} | all-to-all | bytes 655360 | tf_op jit(solution)/shard_map/all_to_all | solution.py:29
  94.9 0.6 shard_map.114
  95.5 19.2 %all-gather = bf16[1088,128]{1,0:T(8,128)(2,1)S(1)} all-gather(bf16[272,128]{1,0:T(8,128)(2,1)S(1)} %shard_map.114), channel_id=2, replica_groups=mesh['x'=4,'zh'=4,'zl'=4,'y'=4,'core'=2] {'zh'}, dimensions={0}, use_global_device_ids=true | all-gather | bytes 348160 | tf_op jit(solution)/shard_map/all_gather | solution.py:371
  114.8 1.4 %shard_map.115 = bf16[16,64,128]{2,1,0:T(8,128)(2,1)} custom-call(s32[5]{0:T(128)S(1)} %stack.19.place, bf16[4,272,128]{2,1,0:T(8,128)(2,1)S(1)} %bitcast.11, bf16[16,80,128]{2,1,0:T(8,128)(2,1)S(1)} %all_to_all.21.got), custom_call_target="tpu_custom_call" | custom-call | flops 1000000 | bytes 1000000 | tf_op jit(solution)/shard_map/pallas_call | solution.py:50
  116.2 5.1 %all-to-all-start.3 = ((bf16[16,64,128]{2,1,0:T(8,128)(2,1)}), bf16[16,64,128]{2,1,0:T(8,128)(2,1)S(1)}, u32[]{:S(2)}, u32[]{:S(2)}) async-start(bf16[16,64,128]{2,1,0:T(8,128)(2,1)} %shard_map.115), calls=%async_computation.3 | async-start | bytes 524288 | tf_op jit(solution)/shard_map/all_to_all | solution.py:29
  121.3 0.0 copy-start.5
  121.3 0.6 copy-done.5
  121.9 1.4 %shard_map.116 = (f32[128,1024]{1,0:T(8,128)S(1)}, f32[128,1024]{1,0:T(8,128)S(1)}) custom-call(s32[5]{0:T(128)S(1)} %stack.19.place, bf16[128,256]{1,0:T(8,128)(2,1)S(1)} %get-tuple-element.32.keys, bf16[128,1024]{1,0:T(8,128)(2,1)S(1)} %get-tuple-element.34.driven, f32[128,16]{1,0:T(8,128)S(1)} %get-tuple-element.35.cum, ...), custom_call_target="tpu_custom_call" | custom-call | flops 1000000 | bytes 1000000 | tf_op jit(solution)/shard_map/pallas_call | solution.py:50
  123.3 6.4 %all-to-all-done.3 = bf16[16,64,128]{2,1,0:T(8,128)(2,1)S(1)} async-done(((bf16[16,64,128]{2,1,0:T(8,128)(2,1)}), bf16[16,64,128]{2,1,0:T(8,128)(2,1)S(1)}, u32[]{:S(2)}, u32[]{:S(2)}) %all-to-all-start.3) | async-done | bytes 262176 | tf_op jit(solution)/shard_map/all_to_all | solution.py:29
  129.7 1.6 %shard_map.117 = bf16[128,1024]{1,0:T(8,128)(2,1)} custom-call(s32[5]{0:T(128)S(1)} %stack.19.place, bf16[128,256]{1,0:T(8,128)(2,1)S(1)} %get-tuple-element.32.keys, bf16[1024,128]{1,0:T(8,128)(2,1)S(1)} %bitcast.12, f32[128,1024]{1,0:T(8,128)S(1)} %get-tuple-element.37.mixed, f32[128,1024]{1,0:T(8,128)S(1)} %get-tuple-element.38.grown, ...), custom_call_target="tpu_custom_call" | custom-call | flops 1000000 | bytes 1000000 | tf_op jit(solution)/shard_map/pallas_call | solution.py:50
  (17 shorter events, 0.1 us)
Async XLA Ops:
  2.0 4.5 %copy-start.6 = (bf16[1024,32]{0,1:T(8,128)(2,1)S(1)}, bf16[1024,32]{0,1:T(8,128)(2,1)}, u32[]{:S(2)}) copy-start(bf16[1024,32]{0,1:T(8,128)(2,1)} %param.12) | copy-start | bytes 196612
  2.0 30.1 %all-to-all-start = ((bf16[4,128,1024]{2,1,0:T(8,128)(2,1)}), bf16[4,128,1024]{2,1,0:T(8,128)(2,1)S(1)}, u32[]{:S(2)}, u32[]{:S(2)}) async-start(bf16[4,128,1024]{2,1,0:T(8,128)(2,1)} %shard_map.109), calls=%async_computation | async-start | bytes 2097152 | tf_op jit(solution)/shard_map/all_to_all | solution.py:29
  32.2 10.2 %copy-start = (bf16[128,1024]{1,0:T(8,128)(2,1)S(1)}, bf16[128,1024]{1,0:T(8,128)(2,1)}, u32[]{:S(2)}) copy-start(bf16[128,1024]{1,0:T(8,128)(2,1)} %inner.3) | copy-start | bytes 786436
  32.2 17.2 %collective-permute-start = (bf16[144,1024]{1,0:T(8,128)(2,1)S(1)}, bf16[144,1024]{1,0:T(8,128)(2,1)S(1)}, u32[]{:S(2)}, u32[]{:S(2)}) collective-permute-start(bf16[144,1024]{1,0:T(8,128)(2,1)S(1)} %fusion.1), channel_id=1, source_target_pairs={{0,8},{1,121},{8,16},{9,1},{16,24},{17,9},{24,32},{25,17},{32,40},... | collective-permute-start | bytes 884744 | tf_op jit(solution)/shard_map/ppermute | solution.py:323
  35.3 14.1 %collective-permute-start.1 = (bf16[144,1024]{1,0:T(8,128)(2,1)S(1)}, bf16[144,1024]{1,0:T(8,128)(2,1)S(1)}, u32[]{:S(2)}, u32[]{:S(2)}) collective-permute-start(bf16[144,1024]{1,0:T(8,128)(2,1)S(1)} %fusion.1), channel_id=1, source_target_pairs={{0,120},{1,9},{8,0},{9,17},{16,8},{17,25},{24,16},{25,33},{32,24},... | collective-permute-start | bytes 884744 | tf_op jit(solution)/shard_map/ppermute | solution.py:323
  38.2 11.2 %collective-permute-start.2 = (bf16[128,1024]{1,0:T(8,128)(2,1)S(1)}, bf16[128,1024]{1,0:T(8,128)(2,1)S(1)}, u32[]{:S(2)}, u32[]{:S(2)}) collective-permute-start(bf16[128,1024]{1,0:T(8,128)(2,1)S(1)} %all_gather.9.own), channel_id=1, source_target_pairs={{0,16},{1,113},{8,24},{9,121},{16,32},{17,1},{24,40},{25,9},{32,48... | collective-permute-start | bytes 786440 | tf_op jit(solution)/shard_map/ppermute | solution.py:323
  41.5 0.7 copy-start.7
  42.2 0.8 copy-start.2
  42.4 0.7 copy-start.4
  66.2 8.6 %copy-start.3 = (f32[4,256]{1,0:T(4,128)S(1)}, f32[4,256]{1,0:T(4,128)}, u32[]{:S(2)}) copy-start(f32[4,256]{1,0:T(4,128)} %taps.1) | copy-start | bytes 12292
  66.9 7.9 %collective-permute-start.3 = (bf16[144,256]{1,0:T(8,128)(2,1)S(1)}, bf16[144,256]{1,0:T(8,128)(2,1)S(1)}, u32[]{:S(2)}, u32[]{:S(2)}) collective-permute-start(bf16[144,256]{1,0:T(8,128)(2,1)S(1)} %shard_map.112), channel_id=1, source_target_pairs={{0,256},{2,384},{4,0},{6,128},{128,258},{130,386},{132,2},{134,130... | collective-permute-start | bytes 221192 | tf_op jit(solution)/shard_map/ppermute | solution.py:42
  116.2 5.1 %copy-start.8 = (bf16[1024]{0:T(1024)(128)(2,1)S(1)}, bf16[1024]{0:T(1024)(128)(2,1)}, u32[]{:S(2)}) copy-start(bf16[1024]{0:T(1024)(128)(2,1)} %param.21) | copy-start | bytes 6148
  116.2 5.1 %copy-start.1 = (bf16[128,1024]{1,0:T(8,128)(2,1)S(1)}, bf16[128,1024]{1,0:T(8,128)(2,1)}, u32[]{:S(2)}) copy-start(bf16[128,1024]{1,0:T(8,128)(2,1)} %gate.1) | copy-start | bytes 786436
  116.2 13.5 %all-to-all-start.3 = ((bf16[16,64,128]{2,1,0:T(8,128)(2,1)}), bf16[16,64,128]{2,1,0:T(8,128)(2,1)S(1)}, u32[]{:S(2)}, u32[]{:S(2)}) async-start(bf16[16,64,128]{2,1,0:T(8,128)(2,1)} %shard_map.115), calls=%async_computation.3 | async-start | bytes 524288 | tf_op jit(solution)/shard_map/all_to_all | solution.py:29
  121.3 0.7 copy-start.5

commit v8 on v7

--- a/solution.py
+++ b/solution.py
@@ -46,16 +46,17 @@
     return jax.ShapeDtypeStruct(dims, kind)
 
 
-def kernel_call(body, outs, place, args, scratch=(), flops=1_000_000):
+def kernel_call(body, outs, scalars, args, scratch=(), flops=1_000_000):
+    placed = [] if scalars is None else [scalars]
     return pl.pallas_call(
         body,
         out_shape=outs,
-        in_specs=[SMEM] + [VMEM] * len(args),
+        in_specs=[SMEM] * len(placed) + [VMEM] * len(args),
         out_specs=jax.tree.map(lambda _: VMEM, outs),
         scratch_shapes=scratch,
         compiler_params=pltpu.CompilerParams(vmem_limit_bytes=32 * 1024 * 1024),
         cost_estimate=pl.CostEstimate(flops=flops, bytes_accessed=1_000_000, transcendentals=0),
-    )(place, *args)
+    )(*placed, *args)
 
 
 def expand(columns, head_width):
@@ -91,7 +92,7 @@
     return inner_ref[...].astype(f32) * jnp.sum(chosen, axis=0, keepdims=True)
 
 
-def drive_kernel(place, inner, scale, step, decay, driven, cum, cum_t, weighted_t, logs):
+def drive_kernel(tenant, inner, scale, step, decay, driven, cum, cum_t, weighted_t, logs):
     heads = step.shape[1]
     head_width = inner.shape[1] // heads
     log_decay = -step[...] * decay[...]
@@ -108,7 +109,7 @@
         preferred_element_type=f32,
     )
     end = so_far[Q - 1 :]
-    scaled = scaled_by_tenant(place[3], inner, scale)
+    scaled = scaled_by_tenant(tenant[0], inner, scale)
     drive = (scaled * expand(step[...], head_width)).astype(bf16)
     driven[...] = drive
     tail = expand(jnp.exp(end - so_far), head_width)
@@ -128,10 +129,10 @@
         copy.wait()
 
 
-def project_kernel(place, own, one, other, across, rows, out, w_in_order, all_rows):
+def project_kernel(own, one, other, across, rows, out, w_in_order, all_rows):
     n_part = N // QUAD
     halves = own.shape[0] // n_part
-    zl, core = place[2], place[4]
+    zh, zl, core = (lax.axis_index(a) for a in Z + ("core",))
     steps = (0, 2 * core - 1, 1 - 2 * core, 2)
     for w, step in zip((own, one, other, across), steps):
         s = lax.rem(zl + step + QUAD, QUAD)
@@ -145,7 +146,7 @@
         pltpu.roll(packed, (HALO - (i + 1) * REACH) % HALO, 0).astype(bf16)
         for i in range(rows.shape[0])
     ]
-    first = (place[1] == 0) & (place[2] == 0)
+    first = (zh == 0) & (zl == 0)
     size = HALO + Q
     for block in range(rows.shape[0]):
         behind = tails[block - 1] if block > 0 else jnp.zeros_like(tails[0])
@@ -163,14 +164,14 @@
             out[to, c] = sums[block * size : (block + 1) * size]
 
 
-def sum_kernel(place, parts, out):
+def sum_kernel(parts, out):
     raw = parts[0].astype(f32)
     for i in range(1, parts.shape[0]):
         raw = raw + parts[i].astype(f32)
     out[...] = raw.astype(bf16)
 
 
-def keys_kernel(place, sums, taps, weighted_t, logs, keys_out, out):
+def keys_kernel(sums, taps, weighted_t, logs, keys_out, out):
     raw = sums[...].astype(f32)
     n_taps = taps.shape[0]
     summed = taps[n_taps - 1 :] * raw[HALO:]
@@ -186,7 +187,7 @@
         out[h, head_width:] = logs[h]
 
 
-def total_kernel(place, got, total):
+def total_kernel(got, total):
     head_width = got.shape[1] - LOG_ROWS
     rows = got.shape[0] // QUAD
     at = lax.broadcasted_iota(jnp.int32, (LOG_ROWS, N), 0)
@@ -204,7 +205,8 @@
     total[rows * head_width :] = logs.astype(bf16)
 
 
-def states_kernel(place, totals, got, out):
+def states_kernel(totals, got, out):
+    zh = lax.axis_index("zh")
     head_width = out.shape[1]
     rows = out.shape[0] // QUAD
     logs = [totals[quad, rows * head_width :].astype(f32) for quad in range(totals.shape[0])]
@@ -212,7 +214,7 @@
     for row in range(rows):
         carry = acc
         for quad in range(totals.shape[0]):
-            carry = jnp.where(place[1] == quad, acc, carry)
+            carry = jnp.where(zh == quad, acc, carry)
             log = jnp.sum(logs[quad][3 * row : 3 * row + 3], axis=0, keepdims=True)
             update = totals[quad, row * head_width : (row + 1) * head_width]
             acc = jnp.exp(log) * acc + update.astype(f32)
@@ -224,7 +226,7 @@
                 carry = jnp.exp(log) * carry + got[at, :head_width].astype(f32)
 
 
-def within_kernel(place, keys, driven, cum, cum_t, inner, scale, skip, gate, out, grown):
+def within_kernel(tenant, keys, driven, cum, cum_t, inner, scale, skip, gate, out, grown):
     scores = lax.dot_general(
         keys[:, N:], keys[:, :N], (((1,), (1,)), ((), ())), preferred_element_type=f32
     )
@@ -234,7 +236,7 @@
     heads = cum.shape[1]
     head_width = driven.shape[1] // heads
     per_tile = Q // head_width
-    skipped = expand(skip[...], head_width) * scaled_by_tenant(place[3], inner, scale)
+    skipped = expand(skip[...], head_width) * scaled_by_tenant(tenant[0], inner, scale)
     g = gate[...].astype(f32)
     gates = g / (1.0 + jnp.exp(-g))
     grown[...] = gates * expand(jnp.exp(cum[...]), head_width)
@@ -250,7 +252,7 @@
         out[:, at] = (mixed + skipped[:, at]) * gates[:, at]
 
 
-def output_kernel(place, keys, start, mixed, grown, gain, out):
+def output_kernel(keys, start, mixed, grown, gain, out):
     width = out.shape[1]
     quarter = width // QUAD
     gated = []
@@ -285,8 +287,6 @@
     heads = decay_rate.shape[0]
     width = inner_input.shape[1]
     head_width = width // heads
-    x, zh, zl = (lax.axis_index(a) for a in CTX)
-    place = jnp.stack([x, zh, zl, tenant_index[0], lax.axis_index("core")])
     n_z = lax.axis_size(Z)
     n_x = lax.axis_size("x")
     depth = hidden_states.shape[1]
@@ -333,7 +333,7 @@
             shape((width, Q), bf16),
             shape((heads, LOG_ROWS, N), bf16),
         ],
-        place,
+        tenant_index,
         [inner_input, tenant_scale, step_size, decay_rate[None]],
     )
 
@@ -344,7 +344,7 @@
     sums = kernel_call(
         project_kernel,
         shape((n_x, lax.axis_size("core"), size, 2 * N), bf16),
-        place,
+        None,
         [*w_all, rows],
         [
             pltpu.VMEM((w_zh.shape[0] * QUAD, depth), bf16),
@@ -352,22 +352,22 @@
         ],
     )
     sums = swap(sums.reshape(-1, size, 2 * N), TP)
-    sums = to_owner(kernel_call(sum_kernel, shape((size, 2 * N), bf16), place, [sums]))
+    sums = to_owner(kernel_call(sum_kernel, shape((size, 2 * N), bf16), None, [sums]))
     keys, update = kernel_call(
         keys_kernel,
         [shape((Q, 2 * N), bf16), shape((heads, head_width + LOG_ROWS, N), bf16)],
-        place,
+        None,
         [sums, conv_taps, weighted_t, logs],
     )
 
     got = swap(update, NEAR)
     total = kernel_call(
-        total_kernel, shape((n_x * head_width + LOG_ROWS, N), bf16), place, [got]
+        total_kernel, shape((n_x * head_width + LOG_ROWS, N), bf16), None, [got]
     )
     states = kernel_call(
         states_kernel,
         shape((heads, head_width, N), bf16),
-        place,
+        None,
         [lax.all_gather(total, "zh"), got],
     )
     start = swap(states, NEAR).reshape(width, N)
@@ -375,13 +375,13 @@
     mixed, grown = kernel_call(
         within_kernel,
         [shape((Q, width), f32)] * 2,
-        place,
+        tenant_index,
         [keys, driven, cum, cum_t, inner_input, tenant_scale, skip_gain[None], gate_input],
     )
     return kernel_call(
         output_kernel,
         shape((Q, width), bf16),
-        place,
+        None,
         [keys, start, mixed, grown, norm_gain[None]],
     )
 

time: 132 us -> 129 us (0.977)
  Pallas kernels: 11.8 us -> 7.47 us
    pallas_call x8, Pallas kernels: 9.83 us -> 5.5 us  [kernel_call(): pl.pallas_call(body, out_shape=outs, in_specs=[SMEM] * len(placed) + [VME...]
  transfers between devices with their start and end apart: 6 -> 6, of which waited for: 3 -> 3; matrix products, arithmetic and copies ran while one was open for 0% -> 0% of each run, Pallas kernels for 3% -> 2%
where the time goes in v8:
time: 129 us; the launch traced here: 128 us
  blocking collectives  79.7 us (62%)
  starting transfers between devices  24.2 us (19%)
  waiting for transfers between devices  14.4 us (11%)
  Pallas kernels  7.47 us (6%)
  local copies, waits for them, and re-layouts  1.47 us (1%)
    all_to_all x2, blocking collectives, swap(): return lax.all_to_all(blocks, axis, 0, 0, tiled=True)  34.6 us
    all_gather x1, blocking collectives, per_device(): w_zh = lax.all_gather(select_weight.T, 'zh', axis=0, tiled=True)  25.7 us
    all_gather x1, blocking collectives, per_device(): lax.all_gather(total, 'zh')  19.4 us
    all_to_all x2, starting transfers between devices, swap(): return lax.all_to_all(blocks, axis, 0, 0, tiled=True)  9.39 us
    ppermute x3, starting transfers between devices, from_side(): return lax.ppermute(block, Z + ('core',), pairs)  9.28 us
    all_to_all x2, waiting for transfers between devices, swap(): return lax.all_to_all(blocks, axis, 0, 0, tiled=True)  6.92 us
    ppermute x1, starting transfers between devices, to_owner(): return lax.ppermute(block, ('x', 'y'), pairs)  5.54 us
    pallas_call x8, Pallas kernels, kernel_call(): pl.pallas_call(body, out_shape=outs, in_specs=[SMEM] * len(placed) + [VME...  5.5 us
  transfers between devices with their start and end apart: 6, of which 3 were waited for; matrix products, arithmetic and copies ran while one was open for 0% of the time, Pallas kernels for 2%

profile of v8, /device:TPU:32, one launch (start us, length us, event | category | flops | bytes accessed | tf_op | source)
XLA Modules:
  0.0 128.0 jit_solution(3193449715385071827)
XLA Ops:
  0.0 2.0 %shard_map.109 = bf16[4,128,1024]{2,1,0:T(8,128)(2,1)} custom-call(bf16[128,1024]{1,0:T(8,128)(2,1)} %block.1), custom_call_target="tpu_custom_call" | custom-call | bytes 1000000 | tf_op jit(solution)/shard_map/pallas_call | solution.py:294
  2.0 0.0 copy-start.6
  2.0 4.4 %all-to-all-start = ((bf16[4,128,1024]{2,1,0:T(8,128)(2,1)}), bf16[4,128,1024]{2,1,0:T(8,128)(2,1)S(1)}, u32[]{:S(2)}, u32[]{:S(2)}) async-start(bf16[4,128,1024]{2,1,0:T(8,128)(2,1)} %shard_map.109), calls=%async_computation | async-start | bytes 2097152 | tf_op jit(solution)/shard_map/all_to_all | solution.py:29
  6.4 25.7 %all_gather.9.own = bf16[128,1024]{1,0:T(8,128)(2,1)S(1)} all-gather(bf16[32,1024]{1,0:T(8,128)(2,1)S(1)} %bitcast.11), channel_id=1, replica_groups=mesh['x'=4,'zh'=4,'zl'=4,'y'=4,'core'=2] {'zh'}, dimensions={0}, use_global_device_ids=true | all-gather | bytes 327680 | tf_op jit(solution)/shard_map/all_gather | solution.py:309
  32.1 0.0 all-to-all-done.rows
  32.2 0.0 copy-start.7
  32.2 0.0 copy-start
  32.2 3.1 %collective-permute-start = (bf16[144,1024]{1,0:T(8,128)(2,1)S(1)}, bf16[144,1024]{1,0:T(8,128)(2,1)S(1)}, u32[]{:S(2)}, u32[]{:S(2)}) collective-permute-start(bf16[144,1024]{1,0:T(8,128)(2,1)S(1)} %fusion.1), channel_id=1, source_target_pairs={{0,8},{1,121},{8,16},{9,1},{16,24},{17,9},{24,32},{25,17},{32,40},... | collective-permute-start | bytes 884744 | tf_op jit(solution)/shard_map/ppermute | solution.py:323
  35.3 2.9 %collective-permute-start.1 = (bf16[144,1024]{1,0:T(8,128)(2,1)S(1)}, bf16[144,1024]{1,0:T(8,128)(2,1)S(1)}, u32[]{:S(2)}, u32[]{:S(2)}) collective-permute-start(bf16[144,1024]{1,0:T(8,128)(2,1)S(1)} %fusion.1), channel_id=1, source_target_pairs={{0,120},{1,9},{8,0},{9,17},{16,8},{17,25},{24,16},{25,33},{32,24},... | collective-permute-start | bytes 884744 | tf_op jit(solution)/shard_map/ppermute | solution.py:323
  38.2 3.3 %collective-permute-start.2 = (bf16[128,1024]{1,0:T(8,128)(2,1)S(1)}, bf16[128,1024]{1,0:T(8,128)(2,1)S(1)}, u32[]{:S(2)}, u32[]{:S(2)}) collective-permute-start(bf16[128,1024]{1,0:T(8,128)(2,1)S(1)} %all_gather.9.own), channel_id=1, source_target_pairs={{0,16},{1,113},{8,24},{9,121},{16,32},{17,1},{24,40},{25,9},{32,48... | collective-permute-start | bytes 786440 | tf_op jit(solution)/shard_map/ppermute | solution.py:323
  42.2 0.0 copy-start.2
  42.2 0.1 copy.13.step
  42.3 0.6 copy-done.2
  42.9 0.0 copy-done.4
  42.9 1.4 %shard_map.110 = (bf16[128,1024]{1,0:T(8,128)(2,1)S(1)}, f32[128,16]{1,0:T(8,128)S(1)}, f32[16,128]{1,0:T(8,128)S(1)}, bf16[1024,128]{1,0:T(8,128)(2,1)S(1)}, bf16[16,16,128]{2,1,0:T(8,128)(2,1)S(1)}) custom-call(s32[1]{0:T(128)S(6)} %copy.14.tenant, bf16[128,1024]{1,0:T(8,128)(2,1)S(1)} %copy-done, bf16[16,1024]{1,0:T(8,128)(2,1)S(1)} %copy-done.2, ...), custom_call_target="tpu_custom_call" | custom-call | flops 1000000 | bytes 1000000 | tf_op jit(solution)/shard_map/pallas_call | solution.py:51
  44.4 5.1 %collective-permute-done.2.across = bf16[128,1024]{1,0:T(8,128)(2,1)S(1)} collective-permute-done((bf16[128,1024]{1,0:T(8,128)(2,1)S(1)}, bf16[128,1024]{1,0:T(8,128)(2,1)S(1)}, u32[]{:S(2)}, u32[]{:S(2)}) %collective-permute-start.2) | collective-permute-done | bytes 262176 | tf_op jit(solution)/shard_map/ppermute | solution.py:323
  49.4 0.9 shard_map.111
  50.3 15.4 %all_to_all.20.parts = bf16[8,144,256]{2,1,0:T(8,128)(2,1)S(1)} all-to-all(bf16[8,144,256]{2,1,0:T(8,128)(2,1)S(1)} %bitcast.6), channel_id=1, replica_groups=mesh['x'=4,'zh'=4,'zl'=4,'y'=4,'core'=2] {'y','core'}, dimensions={0} | all-to-all | bytes 1179648 | tf_op jit(solution)/shard_map/all_to_all | solution.py:29
  65.7 0.1 shard_map.112
  65.8 5.5 %collective-permute-start.3 = (bf16[144,256]{1,0:T(8,128)(2,1)S(1)}, bf16[144,256]{1,0:T(8,128)(2,1)S(1)}, u32[]{:S(2)}, u32[]{:S(2)}) collective-permute-start(bf16[144,256]{1,0:T(8,128)(2,1)S(1)} %shard_map.112), channel_id=1, source_target_pairs={{0,256},{2,384},{4,0},{6,128},{128,258},{130,386},{132,2},{134,130... | collective-permute-start | bytes 221192 | tf_op jit(solution)/shard_map/ppermute | solution.py:42
  71.3 2.4 %collective-permute-done.3.sums = bf16[144,256]{1,0:T(8,128)(2,1)S(1)} collective-permute-done((bf16[144,256]{1,0:T(8,128)(2,1)S(1)}, bf16[144,256]{1,0:T(8,128)(2,1)S(1)}, u32[]{:S(2)}, u32[]{:S(2)}) %collective-permute-start.3) | collective-permute-done | bytes 73760 | tf_op jit(solution)/shard_map/ppermute | solution.py:42
  73.7 0.3 shard_map.113
  74.0 19.3 %all_to_all.21.got = bf16[16,80,128]{2,1,0:T(8,128)(2,1)S(1)} all-to-all(bf16[16,80,128]{2,1,0:T(8,128)(2,1)S(1)} %get-tuple-element.33), channel_id=1, replica_groups=mesh['x'=4,'zh'=4,'zl'=4,'y'=4,'core'=2] {'x','zl'}, dimensions={0} | all-to-all | bytes 655360 | tf_op jit(solution)/shard_map/all_to_all | solution.py:29
  93.3 0.1 shard_map.114
  93.4 19.4 %all-gather = bf16[1088,128]{1,0:T(8,128)(2,1)S(1)} all-gather(bf16[272,128]{1,0:T(8,128)(2,1)S(1)} %shard_map.114), channel_id=2, replica_groups=mesh['x'=4,'zh'=4,'zl'=4,'y'=4,'core'=2] {'zh'}, dimensions={0}, use_global_device_ids=true | all-gather | bytes 348160 | tf_op jit(solution)/shard_map/all_gather | solution.py:371
  112.8 0.9 shard_map.115
  113.6 5.0 %all-to-all-start.3 = ((bf16[16,64,128]{2,1,0:T(8,128)(2,1)}), bf16[16,64,128]{2,1,0:T(8,128)(2,1)S(1)}, u32[]{:S(2)}, u32[]{:S(2)}) async-start(bf16[16,64,128]{2,1,0:T(8,128)(2,1)} %shard_map.115), calls=%async_computation.3 | async-start | bytes 524288 | tf_op jit(solution)/shard_map/all_to_all | solution.py:29
  118.6 0.0 copy-start.5
  118.6 0.6 copy-done.5
  119.3 0.8 shard_map.116
  120.1 6.9 %all-to-all-done.3 = bf16[16,64,128]{2,1,0:T(8,128)(2,1)S(1)} async-done(((bf16[16,64,128]{2,1,0:T(8,128)(2,1)}), bf16[16,64,128]{2,1,0:T(8,128)(2,1)S(1)}, u32[]{:S(2)}, u32[]{:S(2)}) %all-to-all-start.3) | async-done | bytes 262176 | tf_op jit(solution)/shard_map/all_to_all | solution.py:29
  127.0 1.0 shard_map.117
  (16 shorter events, 0.1 us)
Async XLA Ops:
  2.0 4.5 %copy-start.6 = (bf16[1024,32]{0,1:T(8,128)(2,1)S(1)}, bf16[1024,32]{0,1:T(8,128)(2,1)}, u32[]{:S(2)}) copy-start(bf16[1024,32]{0,1:T(8,128)(2,1)} %param.12) | copy-start | bytes 196612
  2.0 30.1 %all-to-all-start = ((bf16[4,128,1024]{2,1,0:T(8,128)(2,1)}), bf16[4,128,1024]{2,1,0:T(8,128)(2,1)S(1)}, u32[]{:S(2)}, u32[]{:S(2)}) async-start(bf16[4,128,1024]{2,1,0:T(8,128)(2,1)} %shard_map.109), calls=%async_computation | async-start | bytes 2097152 | tf_op jit(solution)/shard_map/all_to_all | solution.py:29
  32.2 10.0 %copy-start.7 = (f32[128,16]{0,1:T(8,128)S(1)}, f32[128,16]{0,1:T(8,128)}, u32[]{:S(2)}) copy-start(f32[128,16]{0,1:T(8,128)} %param.16) | copy-start | bytes 24580
  32.2 10.1 %copy-start = (bf16[128,1024]{1,0:T(8,128)(2,1)S(1)}, bf16[128,1024]{1,0:T(8,128)(2,1)}, u32[]{:S(2)}) copy-start(bf16[128,1024]{1,0:T(8,128)(2,1)} %inner.3) | copy-start | bytes 786436
  32.2 17.2 %collective-permute-start = (bf16[144,1024]{1,0:T(8,128)(2,1)S(1)}, bf16[144,1024]{1,0:T(8,128)(2,1)S(1)}, u32[]{:S(2)}, u32[]{:S(2)}) collective-permute-start(bf16[144,1024]{1,0:T(8,128)(2,1)S(1)} %fusion.1), channel_id=1, source_target_pairs={{0,8},{1,121},{8,16},{9,1},{16,24},{17,9},{24,32},{25,17},{32,40},... | collective-permute-start | bytes 884744 | tf_op jit(solution)/shard_map/ppermute | solution.py:323
  35.3 14.1 %collective-permute-start.1 = (bf16[144,1024]{1,0:T(8,128)(2,1)S(1)}, bf16[144,1024]{1,0:T(8,128)(2,1)S(1)}, u32[]{:S(2)}, u32[]{:S(2)}) collective-permute-start(bf16[144,1024]{1,0:T(8,128)(2,1)S(1)} %fusion.1), channel_id=1, source_target_pairs={{0,120},{1,9},{8,0},{9,17},{16,8},{17,25},{24,16},{25,33},{32,24},... | collective-permute-start | bytes 884744 | tf_op jit(solution)/shard_map/ppermute | solution.py:323
  38.2 11.2 %collective-permute-start.2 = (bf16[128,1024]{1,0:T(8,128)(2,1)S(1)}, bf16[128,1024]{1,0:T(8,128)(2,1)S(1)}, u32[]{:S(2)}, u32[]{:S(2)}) collective-permute-start(bf16[128,1024]{1,0:T(8,128)(2,1)S(1)} %all_gather.9.own), channel_id=1, source_target_pairs={{0,16},{1,113},{8,24},{9,121},{16,32},{17,1},{24,40},{25,9},{32,48... | collective-permute-start | bytes 786440 | tf_op jit(solution)/shard_map/ppermute | solution.py:323
  42.2 0.8 copy-start.2
  42.3 0.7 copy-start.4
  65.7 8.0 %copy-start.3 = (f32[4,256]{1,0:T(4,128)S(1)}, f32[4,256]{1,0:T(4,128)}, u32[]{:S(2)}) copy-start(f32[4,256]{1,0:T(4,128)} %taps.1) | copy-start | bytes 12292
  65.8 7.9 %collective-permute-start.3 = (bf16[144,256]{1,0:T(8,128)(2,1)S(1)}, bf16[144,256]{1,0:T(8,128)(2,1)S(1)}, u32[]{:S(2)}, u32[]{:S(2)}) collective-permute-start(bf16[144,256]{1,0:T(8,128)(2,1)S(1)} %shard_map.112), channel_id=1, source_target_pairs={{0,256},{2,384},{4,0},{6,128},{128,258},{130,386},{132,2},{134,130... | collective-permute-start | bytes 221192 | tf_op jit(solution)/shard_map/ppermute | solution.py:42
  113.6 5.0 %copy-start.8 = (bf16[1024]{0:T(1024)(128)(2,1)S(1)}, bf16[1024]{0:T(1024)(128)(2,1)}, u32[]{:S(2)}) copy-start(bf16[1024]{0:T(1024)(128)(2,1)} %param.21) | copy-start | bytes 6148
  113.6 5.0 %copy-start.1 = (bf16[128,1024]{1,0:T(8,128)(2,1)S(1)}, bf16[128,1024]{1,0:T(8,128)(2,1)}, u32[]{:S(2)}) copy-start(bf16[128,1024]{1,0:T(8,128)(2,1)} %gate.1) | copy-start | bytes 786436
  113.6 13.4 %all-to-all-start.3 = ((bf16[16,64,128]{2,1,0:T(8,128)(2,1)}), bf16[16,64,128]{2,1,0:T(8,128)(2,1)S(1)}, u32[]{:S(2)}, u32[]{:S(2)}) async-start(bf16[16,64,128]{2,1,0:T(8,128)(2,1)} %shard_map.115), calls=%async_computation.3 | async-start | bytes 524288 | tf_op jit(solution)/shard_map/all_to_all | solution.py:29
  118.6 0.7 copy-start.5

commit v9 on v8

--- a/solution.py
+++ b/solution.py
@@ -92,7 +92,10 @@
     return inner_ref[...].astype(f32) * jnp.sum(chosen, axis=0, keepdims=True)
 
 
-def drive_kernel(tenant, inner, scale, step, decay, driven, cum, cum_t, weighted_t, logs):
+def drive_kernel(
+    tenant, inner, scale, step, decay, skip, gate, gain, driven, cum, cum_t, weighted_t, logs,
+    skipped, gates, grown, gains,
+):
     heads = step.shape[1]
     head_width = inner.shape[1] // heads
     log_decay = -step[...] * decay[...]
@@ -114,6 +117,12 @@
     driven[...] = drive
     tail = expand(jnp.exp(end - so_far), head_width)
     weighted_t[...] = jnp.transpose(tail * drive.astype(f32)).astype(bf16)
+    g = gate[...].astype(f32)
+    g = g / (1.0 + jnp.exp(-g))
+    gates[...] = g
+    skipped[...] = expand(skip[...], head_width) * scaled * g
+    grown[...] = expand(jnp.exp(so_far), head_width) * g
+    gains[...] = gain[...].astype(f32)
     for h in range(heads):
         logs[h] = log_rows(jnp.broadcast_to(end[:, h : h + 1], (1, N)))
 
@@ -226,7 +235,9 @@
                 carry = jnp.exp(log) * carry + got[at, :head_width].astype(f32)
 
 
-def within_kernel(tenant, keys, driven, cum, cum_t, inner, scale, skip, gate, out, grown):
+def output_kernel(
+    keys, start, driven, cum, cum_t, skipped, gates, grown, gain, out
+):
     scores = lax.dot_general(
         keys[:, N:], keys[:, :N], (((1,), (1,)), ((), ())), preferred_element_type=f32
     )
@@ -234,12 +245,11 @@
     cols = lax.broadcasted_iota(jnp.int32, (Q, Q), 1)
     causal = rows >= cols
     heads = cum.shape[1]
-    head_width = driven.shape[1] // heads
+    width = out.shape[1]
+    head_width = width // heads
     per_tile = Q // head_width
-    skipped = expand(skip[...], head_width) * scaled_by_tenant(tenant[0], inner, scale)
-    g = gate[...].astype(f32)
-    gates = g / (1.0 + jnp.exp(-g))
-    grown[...] = gates * expand(jnp.exp(cum[...]), head_width)
+    gated = []
+    squares = jnp.zeros((Q, 1), f32)
     for tile in range(heads // per_tile):
         at = slice(tile * Q, (tile + 1) * Q)
         mixed = None
@@ -249,26 +259,16 @@
             weights = jnp.where(causal, scores * jnp.exp(jnp.where(causal, lag, 0.0)), 0.0)
             summed = jnp.dot(weights.astype(bf16), driven[:, at], preferred_element_type=f32)
             mixed = summed if mixed is None else jnp.where(cols < i * head_width, mixed, summed)
-        out[:, at] = (mixed + skipped[:, at]) * gates[:, at]
-
-
-def output_kernel(keys, start, mixed, grown, gain, out):
-    width = out.shape[1]
-    quarter = width // QUAD
-    gated = []
-    squares = jnp.zeros((Q, 1), f32)
-    for q in range(QUAD):
-        at = slice(q * quarter, (q + 1) * quarter)
         carried = lax.dot_general(
             keys[:, N:], start[at], (((1,), (1,)), ((), ())), preferred_element_type=f32
         )
-        value = mixed[:, at] + grown[:, at] * carried
+        value = mixed * gates[:, at] + skipped[:, at] + grown[:, at] * carried
         squares = squares + jnp.sum(value * value, axis=1, keepdims=True)
         gated.append(value)
     inverse = lax.rsqrt(squares / width + epsilon)
-    for q in range(QUAD):
-        at = slice(q * quarter, (q + 1) * quarter)
-        out[:, at] = (gated[q] * inverse * gain[:, at].astype(f32)).astype(bf16)
+    for tile, value in enumerate(gated):
+        at = slice(tile * Q, (tile + 1) * Q)
+        out[:, at] = (value * inverse * gain[:, at]).astype(bf16)
 
 
 def per_device(
@@ -324,7 +324,7 @@
 
     w_all = [w_zh, from_side(both, 1), from_side(both, -1), from_side(w_zh, 2)]
 
-    driven, cum, cum_t, weighted_t, logs = kernel_call(
+    driven, cum, cum_t, weighted_t, logs, skipped, gates, grown, gains = kernel_call(
         drive_kernel,
         [
             shape((Q, width), bf16),
@@ -332,9 +332,21 @@
             shape((heads, Q), f32),
             shape((width, Q), bf16),
             shape((heads, LOG_ROWS, N), bf16),
+            shape((Q, width), f32),
+            shape((Q, width), f32),
+            shape((Q, width), f32),
+            shape((1, width), f32),
         ],
         tenant_index,
-        [inner_input, tenant_scale, step_size, decay_rate[None]],
+        [
+            inner_input,
+            tenant_scale,
+            step_size,
+            decay_rate[None],
+            skip_gain[None],
+            gate_input,
+            norm_gain[None],
+        ],
     )
 
 
@@ -372,17 +384,11 @@
     )
     start = swap(states, NEAR).reshape(width, N)
 
-    mixed, grown = kernel_call(
-        within_kernel,
-        [shape((Q, width), f32)] * 2,
-        tenant_index,
-        [keys, driven, cum, cum_t, inner_input, tenant_scale, skip_gain[None], gate_input],
-    )
     return kernel_call(
         output_kernel,
         shape((Q, width), bf16),
         None,
-        [keys, start, mixed, grown, norm_gain[None]],
+        [keys, start, driven, cum, cum_t, skipped, gates, grown, gains],
     )
 
 

time: 129 us -> 129 us (level)
  blocking collectives: 79.7 us -> 91.5 us
  waiting for transfers between devices: 14.4 us -> 8.29 us
  starting transfers between devices: 24.2 us -> 20.5 us
    all_to_all x2 -> x3, blocking collectives: 34.6 us -> 45.6 us  [swap(): return lax.all_to_all(blocks, axis, 0, 0, tiled=True)]
    all_to_all x2 -> x1, waiting for transfers between devices: 6.92 us -> 0.01 us  [swap(): return lax.all_to_all(blocks, axis, 0, 0, tiled=True)]
    all_to_all x2 -> x1, starting transfers between devices: 9.39 us -> 4.44 us  [swap(): return lax.all_to_all(blocks, axis, 0, 0, tiled=True)]
    pallas_call x8 -> x7, Pallas kernels: 5.5 us -> 4.97 us  [kernel_call(): pl.pallas_call(body, out_shape=outs, in_specs=[SMEM] * len(placed) + [VME...]
  transfers between devices with their start and end apart: 6 -> 5, of which waited for: 3 -> 2; matrix products, arithmetic and copies ran while one was open for 0% -> 0% of each run, Pallas kernels for 2% -> 1%
where the time goes in v9:
time: 129 us
  blocking collectives  91.5 us (71%)
  starting transfers between devices  20.5 us (16%)
  waiting for transfers between devices  8.29 us (6%)
  Pallas kernels  6.94 us (5%)
    all_to_all x3, blocking collectives, swap(): return lax.all_to_all(blocks, axis, 0, 0, tiled=True)  45.6 us
    all_gather x1, blocking collectives, per_device(): w_zh = lax.all_gather(select_weight.T, 'zh', axis=0, tiled=True)  25.7 us
    all_gather x1, blocking collectives, per_device(): lax.all_gather(total, 'zh')  20.2 us
    ppermute x3, starting transfers between devices, from_side(): return lax.ppermute(block, Z + ('core',), pairs)  10.5 us
    ppermute x3, waiting for transfers between devices, from_side(): return lax.ppermute(block, Z + ('core',), pairs)  5.96 us
    ppermute x1, starting transfers between devices, to_owner(): return lax.ppermute(block, ('x', 'y'), pairs)  5.59 us
    pallas_call x7, Pallas kernels, kernel_call(): pl.pallas_call(body, out_shape=outs, in_specs=[SMEM] * len(placed) + [VME...  4.97 us
    all_to_all x1, starting transfers between devices, swap(): return lax.all_to_all(blocks, axis, 0, 0, tiled=True)  4.44 us
  transfers between devices with their start and end apart: 5, of which 2 were waited for; matrix products, arithmetic and copies ran while one was open for 0% of the time, Pallas kernels for 1%

profile of v9, /device:TPU:32, one launch (start us, length us, event | category | flops | bytes accessed | tf_op | source)
XLA Modules:
  0.0 128.9 jit_solution(9457042231698752473)
XLA Ops:
  0.0 2.0 %shard_map.109 = bf16[4,128,1024]{2,1,0:T(8,128)(2,1)} custom-call(bf16[128,1024]{1,0:T(8,128)(2,1)} %block.1), custom_call_target="tpu_custom_call" | custom-call | bytes 1000000 | tf_op jit(solution)/shard_map/pallas_call | solution.py:294
  2.0 0.0 copy-start.6
  2.0 4.4 %all-to-all-start = ((bf16[4,128,1024]{2,1,0:T(8,128)(2,1)}), bf16[4,128,1024]{2,1,0:T(8,128)(2,1)S(1)}, u32[]{:S(2)}, u32[]{:S(2)}) async-start(bf16[4,128,1024]{2,1,0:T(8,128)(2,1)} %shard_map.109), calls=%async_computation | async-start | bytes 2097152 | tf_op jit(solution)/shard_map/all_to_all | solution.py:29
  6.4 25.7 %all_gather.9.own = bf16[128,1024]{1,0:T(8,128)(2,1)S(1)} all-gather(bf16[32,1024]{1,0:T(8,128)(2,1)S(1)} %bitcast.11), channel_id=1, replica_groups=mesh['x'=4,'zh'=4,'zl'=4,'y'=4,'core'=2] {'zh'}, dimensions={0}, use_global_device_ids=true | all-gather | bytes 327680 | tf_op jit(solution)/shard_map/all_gather | solution.py:309
  32.1 0.0 all-to-all-done.rows
  32.2 0.0 copy-start.8
  32.2 0.0 copy-start.7
  32.2 0.0 copy-start
  32.2 0.0 copy-start.1
  32.2 3.0 %collective-permute-start.1 = (bf16[144,1024]{1,0:T(8,128)(2,1)S(1)}, bf16[144,1024]{1,0:T(8,128)(2,1)S(1)}, u32[]{:S(2)}, u32[]{:S(2)}) collective-permute-start(bf16[144,1024]{1,0:T(8,128)(2,1)S(1)} %fusion.1), channel_id=1, source_target_pairs={{0,120},{1,9},{8,0},{9,17},{16,8},{17,25},{24,16},{25,33},{32,24},... | collective-permute-start | bytes 884744 | tf_op jit(solution)/shard_map/ppermute | solution.py:323
  35.2 3.0 %collective-permute-start = (bf16[144,1024]{1,0:T(8,128)(2,1)S(1)}, bf16[144,1024]{1,0:T(8,128)(2,1)S(1)}, u32[]{:S(2)}, u32[]{:S(2)}) collective-permute-start(bf16[144,1024]{1,0:T(8,128)(2,1)S(1)} %fusion.1), channel_id=1, source_target_pairs={{0,8},{1,121},{8,16},{9,1},{16,24},{17,9},{24,32},{25,17},{32,40},... | collective-permute-start | bytes 884744 | tf_op jit(solution)/shard_map/ppermute | solution.py:323
  38.2 4.5 %collective-permute-start.2 = (bf16[128,1024]{1,0:T(8,128)(2,1)S(1)}, bf16[128,1024]{1,0:T(8,128)(2,1)S(1)}, u32[]{:S(2)}, u32[]{:S(2)}) collective-permute-start(bf16[128,1024]{1,0:T(8,128)(2,1)S(1)} %all_gather.9.own), channel_id=1, source_target_pairs={{0,16},{1,113},{8,24},{9,121},{16,32},{17,1},{24,40},{25,9},{32,48... | collective-permute-start | bytes 786440 | tf_op jit(solution)/shard_map/ppermute | solution.py:323
  43.4 0.0 copy-start.2
  43.4 0.1 copy.13.step
  43.5 0.0 copy-start.5
  43.6 0.6 copy-done.2
  44.2 0.0 copy-done.4
  44.2 0.0 copy-done.5
  44.2 1.8 %shard_map.110 = (bf16[128,1024]{1,0:T(8,128)(2,1)S(1)}, f32[128,16]{1,0:T(8,128)S(1)}, f32[16,128]{1,0:T(8,128)S(1)}, bf16[1024,128]{1,0:T(8,128)(2,1)S(1)}, bf...) custom-call(s32[1]{0:T(128)S(6)} %copy.14.tenant, ...), custom_call_target="tpu_custom_call" | custom-call | flops 1000000 | bytes 1000000 | tf_op jit(solution)/shard_map/pallas_call | solution.py:51
  46.0 6.0 %collective-permute-done.2.across = bf16[128,1024]{1,0:T(8,128)(2,1)S(1)} collective-permute-done((bf16[128,1024]{1,0:T(8,128)(2,1)S(1)}, bf16[128,1024]{1,0:T(8,128)(2,1)S(1)}, u32[]{:S(2)}, u32[]{:S(2)}) %collective-permute-start.2) | collective-permute-done | bytes 262176 | tf_op jit(solution)/shard_map/ppermute | solution.py:323
  52.0 0.9 shard_map.111
  52.9 15.4 %all_to_all.20.parts = bf16[8,144,256]{2,1,0:T(8,128)(2,1)S(1)} all-to-all(bf16[8,144,256]{2,1,0:T(8,128)(2,1)S(1)} %bitcast.6), channel_id=1, replica_groups=mesh['x'=4,'zh'=4,'zl'=4,'y'=4,'core'=2] {'y','core'}, dimensions={0} | all-to-all | bytes 1179648 | tf_op jit(solution)/shard_map/all_to_all | solution.py:29
  68.3 0.1 shard_map.112
  68.4 5.6 %collective-permute-start.3 = (bf16[144,256]{1,0:T(8,128)(2,1)S(1)}, bf16[144,256]{1,0:T(8,128)(2,1)S(1)}, u32[]{:S(2)}, u32[]{:S(2)}) collective-permute-start(bf16[144,256]{1,0:T(8,128)(2,1)S(1)} %shard_map.112), channel_id=1, source_target_pairs={{0,256},{2,384},{4,0},{6,128},{128,258},{130,386},{132,2},{134,130... | collective-permute-start | bytes 221192 | tf_op jit(solution)/shard_map/ppermute | solution.py:42
  74.0 2.3 %collective-permute-done.3.sums = bf16[144,256]{1,0:T(8,128)(2,1)S(1)} collective-permute-done((bf16[144,256]{1,0:T(8,128)(2,1)S(1)}, bf16[144,256]{1,0:T(8,128)(2,1)S(1)}, u32[]{:S(2)}, u32[]{:S(2)}) %collective-permute-start.3) | collective-permute-done | bytes 73760 | tf_op jit(solution)/shard_map/ppermute | solution.py:42
  76.3 0.3 shard_map.113
  76.6 17.3 %all_to_all.21.got = bf16[16,80,128]{2,1,0:T(8,128)(2,1)S(1)} all-to-all(bf16[16,80,128]{2,1,0:T(8,128)(2,1)S(1)} %get-tuple-element.35), channel_id=1, replica_groups=mesh['x'=4,'zh'=4,'zl'=4,'y'=4,'core'=2] {'x','zl'}, dimensions={0} | all-to-all | bytes 655360 | tf_op jit(solution)/shard_map/all_to_all | solution.py:29
  93.9 0.1 shard_map.114
  94.0 20.2 %all-gather = bf16[1088,128]{1,0:T(8,128)(2,1)S(1)} all-gather(bf16[272,128]{1,0:T(8,128)(2,1)S(1)} %shard_map.114), channel_id=2, replica_groups=mesh['x'=4,'zh'=4,'zl'=4,'y'=4,'core'=2] {'zh'}, dimensions={0}, use_global_device_ids=true | all-gather | bytes 348160 | tf_op jit(solution)/shard_map/all_gather | solution.py:383
  114.2 0.2 shard_map.115
  114.4 12.9 %all_to_all.22 = bf16[16,64,128]{2,1,0:T(8,128)(2,1)S(1)} all-to-all(bf16[16,64,128]{2,1,0:T(8,128)(2,1)S(1)} %shard_map.115), channel_id=1, replica_groups=mesh['x'=4,'zh'=4,'zl'=4,'y'=4,'core'=2] {'x','zl'}, dimensions={0} | all-to-all | bytes 524288 | tf_op jit(solution)/shard_map/all_to_all | solution.py:29
  127.3 1.6 %shard_map.116 = bf16[128,1024]{1,0:T(8,128)(2,1)} custom-call(bf16[128,256]{1,0:T(8,128)(2,1)S(1)} %get-tuple-element.34.keys, bf16[1024,128]{1,0:T(8,128)(2,1)S(1)} %bitcast.8, bf16[128,1024]{1,0:T(8,128)(2,1)S(1)} %get-tuple-element.36.driven, f32[128,16]{1,0:T(8,128)S(1)} %get-tuple-element.37.cum, f32[16,128]{1,0:T(8,128)S(1)} %get-tuple-element.38.cum_t, ...), custom_call_target="tpu_custom_call" | custom-call | flops 1000000 | bytes 1000000 | tf_op jit(solution)/shard_map/pallas_call | solution.py:51
  (14 shorter events, 0.1 us)
Async XLA Ops:
  2.0 4.5 %copy-start.6 = (bf16[1024,32]{0,1:T(8,128)(2,1)S(1)}, bf16[1024,32]{0,1:T(8,128)(2,1)}, u32[]{:S(2)}) copy-start(bf16[1024,32]{0,1:T(8,128)(2,1)} %param.12) | copy-start | bytes 196612
  2.0 30.1 %all-to-all-start = ((bf16[4,128,1024]{2,1,0:T(8,128)(2,1)}), bf16[4,128,1024]{2,1,0:T(8,128)(2,1)S(1)}, u32[]{:S(2)}, u32[]{:S(2)}) async-start(bf16[4,128,1024]{2,1,0:T(8,128)(2,1)} %shard_map.109), calls=%async_computation | async-start | bytes 2097152 | tf_op jit(solution)/shard_map/all_to_all | solution.py:29
  32.2 11.2 %copy-start.8 = (bf16[1024]{0:T(1024)(128)(2,1)S(1)}, bf16[1024]{0:T(1024)(128)(2,1)}, u32[]{:S(2)}) copy-start(bf16[1024]{0:T(1024)(128)(2,1)} %param.21) | copy-start | bytes 6148
  32.2 11.2 %copy-start.7 = (f32[128,16]{0,1:T(8,128)S(1)}, f32[128,16]{0,1:T(8,128)}, u32[]{:S(2)}) copy-start(f32[128,16]{0,1:T(8,128)} %param.16) | copy-start | bytes 24580
  32.2 11.4 %copy-start = (bf16[128,1024]{1,0:T(8,128)(2,1)S(1)}, bf16[128,1024]{1,0:T(8,128)(2,1)}, u32[]{:S(2)}) copy-start(bf16[128,1024]{1,0:T(8,128)(2,1)} %inner.1) | copy-start | bytes 786436
  32.2 11.4 %copy-start.1 = (bf16[128,1024]{1,0:T(8,128)(2,1)S(1)}, bf16[128,1024]{1,0:T(8,128)(2,1)}, u32[]{:S(2)}) copy-start(bf16[128,1024]{1,0:T(8,128)(2,1)} %gate.1) | copy-start | bytes 786436
  32.2 19.8 %collective-permute-start.1 = (bf16[144,1024]{1,0:T(8,128)(2,1)S(1)}, bf16[144,1024]{1,0:T(8,128)(2,1)S(1)}, u32[]{:S(2)}, u32[]{:S(2)}) collective-permute-start(bf16[144,1024]{1,0:T(8,128)(2,1)S(1)} %fusion.1), channel_id=1, source_target_pairs={{0,120},{1,9},{8,0},{9,17},{16,8},{17,25},{24,16},{25,33},{32,24},... | collective-permute-start | bytes 884744 | tf_op jit(solution)/shard_map/ppermute | solution.py:323
  35.2 16.8 %collective-permute-start = (bf16[144,1024]{1,0:T(8,128)(2,1)S(1)}, bf16[144,1024]{1,0:T(8,128)(2,1)S(1)}, u32[]{:S(2)}, u32[]{:S(2)}) collective-permute-start(bf16[144,1024]{1,0:T(8,128)(2,1)S(1)} %fusion.1), channel_id=1, source_target_pairs={{0,8},{1,121},{8,16},{9,1},{16,24},{17,9},{24,32},{25,17},{32,40},... | collective-permute-start | bytes 884744 | tf_op jit(solution)/shard_map/ppermute | solution.py:323
  38.2 13.8 %collective-permute-start.2 = (bf16[128,1024]{1,0:T(8,128)(2,1)S(1)}, bf16[128,1024]{1,0:T(8,128)(2,1)S(1)}, u32[]{:S(2)}, u32[]{:S(2)}) collective-permute-start(bf16[128,1024]{1,0:T(8,128)(2,1)S(1)} %all_gather.9.own), channel_id=1, source_target_pairs={{0,16},{1,113},{8,24},{9,121},{16,32},{17,1},{24,40},{25,9},{32,48... | collective-permute-start | bytes 786440 | tf_op jit(solution)/shard_map/ppermute | solution.py:323
  43.4 0.8 copy-start.2
  43.5 0.7 copy-start.4
  43.5 0.7 copy-start.5
  68.3 8.0 %copy-start.3 = (f32[4,256]{1,0:T(4,128)S(1)}, f32[4,256]{1,0:T(4,128)}, u32[]{:S(2)}) copy-start(f32[4,256]{1,0:T(4,128)} %taps.1) | copy-start | bytes 12292
  68.4 7.9 %collective-permute-start.3 = (bf16[144,256]{1,0:T(8,128)(2,1)S(1)}, bf16[144,256]{1,0:T(8,128)(2,1)S(1)}, u32[]{:S(2)}, u32[]{:S(2)}) collective-permute-start(bf16[144,256]{1,0:T(8,128)(2,1)S(1)} %shard_map.112), channel_id=1, source_target_pairs={{0,256},{2,384},{4,0},{6,128},{128,258},{130,386},{132,2},{134,130... | collective-permute-start | bytes 221192 | tf_op jit(solution)/shard_map/ppermute | solution.py:42

commit v10 on v8

--- a/solution.py
+++ b/solution.py
@@ -324,6 +324,21 @@
 
     w_all = [w_zh, from_side(both, 1), from_side(both, -1), from_side(w_zh, 2)]
 
+    size = HALO + Q
+    sums = kernel_call(
+        project_kernel,
+        shape((n_x, lax.axis_size("core"), size, 2 * N), bf16),
+        None,
+        [*w_all, rows],
+        [
+            pltpu.VMEM((w_zh.shape[0] * QUAD, depth), bf16),
+            pltpu.VMEM((n_x * size, depth), bf16),
+        ],
+    )
+    sums = swap(sums.reshape(-1, size, 2 * N), TP)
+    sums, step_late = lax.optimization_barrier((sums, step_size))
+    sums = to_owner(kernel_call(sum_kernel, shape((size, 2 * N), bf16), None, [sums]))
+
     driven, cum, cum_t, weighted_t, logs = kernel_call(
         drive_kernel,
         [
@@ -334,25 +349,9 @@
             shape((heads, LOG_ROWS, N), bf16),
         ],
         tenant_index,
-        [inner_input, tenant_scale, step_size, decay_rate[None]],
-    )
-
-
-    w_all, weighted_t, logs = lax.optimization_barrier((w_all, weighted_t, logs))
-
-    size = HALO + Q
-    sums = kernel_call(
-        project_kernel,
-        shape((n_x, lax.axis_size("core"), size, 2 * N), bf16),
-        None,
-        [*w_all, rows],
-        [
-            pltpu.VMEM((w_zh.shape[0] * QUAD, depth), bf16),
-            pltpu.VMEM((n_x * size, depth), bf16),
-        ],
-    )
-    sums = swap(sums.reshape(-1, size, 2 * N), TP)
-    sums = to_owner(kernel_call(sum_kernel, shape((size, 2 * N), bf16), None, [sums]))
+        [inner_input, tenant_scale, step_late, decay_rate[None]],
+    )
+
     keys, update = kernel_call(
         keys_kernel,
         [shape((Q, 2 * N), bf16), shape((heads, head_width + LOG_ROWS, N), bf16)],

time: 129 us -> 129 us (level)
    ppermute x3, waiting for transfers between devices: 5.07 us -> 7.9 us  [from_side(): return lax.ppermute(block, Z + ('core',), pairs)]
    ppermute x1, waiting for transfers between devices: 2.37 us -> 0.01 us  [to_owner(): return lax.ppermute(block, ('x', 'y'), pairs)]
  transfers between devices with their start and end apart: 6 -> 6, of which waited for: 3 -> 2; matrix products, arithmetic and copies ran while one was open for 0% -> 0% of each run, Pallas kernels for 2% -> 2%
where the time goes in v10:
time: 129 us; the launch traced here: 128 us
  blocking collectives  79.2 us (61%)
  starting transfers between devices  24.1 us (19%)
  waiting for transfers between devices  14.8 us (11%)
  Pallas kernels  7.49 us (6%)
  local copies, waits for them, and re-layouts  1.47 us (1%)
    all_to_all x2, blocking collectives, swap(): return lax.all_to_all(blocks, axis, 0, 0, tiled=True)  34.2 us
    all_gather x1, blocking collectives, per_device(): w_zh = lax.all_gather(select_weight.T, 'zh', axis=0, tiled=True)  25.7 us
    all_gather x1, blocking collectives, per_device(): lax.all_gather(total, 'zh')  19.4 us
    all_to_all x2, starting transfers between devices, swap(): return lax.all_to_all(blocks, axis, 0, 0, tiled=True)  9.39 us
    ppermute x3, starting transfers between devices, from_side(): return lax.ppermute(block, Z + ('core',), pairs)  9.14 us
    ppermute x3, waiting for transfers between devices, from_side(): return lax.ppermute(block, Z + ('core',), pairs)  7.9 us
    all_to_all x2, waiting for transfers between devices, swap(): return lax.all_to_all(blocks, axis, 0, 0, tiled=True)  6.92 us
    ppermute x1, starting transfers between devices, to_owner(): return lax.ppermute(block, ('x', 'y'), pairs)  5.54 us
  transfers between devices with their start and end apart: 6, of which 2 were waited for; matrix products, arithmetic and copies ran while one was open for 0% of the time, Pallas kernels for 2%

profile of v10, /device:TPU:32, one launch (start us, length us, event | category | flops | bytes accessed | tf_op | source)
XLA Modules:
  0.0 127.9 jit_solution(18395541683234659823)
XLA Ops:
  0.0 2.0 %shard_map.109 = bf16[4,128,1024]{2,1,0:T(8,128)(2,1)} custom-call(bf16[128,1024]{1,0:T(8,128)(2,1)} %block.1), custom_call_target="tpu_custom_call" | custom-call | bytes 1000000 | tf_op jit(solution)/shard_map/pallas_call | solution.py:294
  2.0 0.0 copy-start.6
  2.0 4.4 %all-to-all-start = ((bf16[4,128,1024]{2,1,0:T(8,128)(2,1)}), bf16[4,128,1024]{2,1,0:T(8,128)(2,1)S(1)}, u32[]{:S(2)}, u32[]{:S(2)}) async-start(bf16[4,128,1024]{2,1,0:T(8,128)(2,1)} %shard_map.109), calls=%async_computation | async-start | bytes 2097152 | tf_op jit(solution)/shard_map/all_to_all | solution.py:29
  6.4 25.7 %all_gather.9.own = bf16[128,1024]{1,0:T(8,128)(2,1)S(1)} all-gather(bf16[32,1024]{1,0:T(8,128)(2,1)S(1)} %bitcast.11), channel_id=1, replica_groups=mesh['x'=4,'zh'=4,'zl'=4,'y'=4,'core'=2] {'zh'}, dimensions={0}, use_global_device_ids=true | all-gather | bytes 327680 | tf_op jit(solution)/shard_map/all_gather | solution.py:309
  32.1 0.0 all-to-all-done.rows
  32.2 3.0 %collective-permute-start = (bf16[144,1024]{1,0:T(8,128)(2,1)S(1)}, bf16[144,1024]{1,0:T(8,128)(2,1)S(1)}, u32[]{:S(2)}, u32[]{:S(2)}) collective-permute-start(bf16[144,1024]{1,0:T(8,128)(2,1)S(1)} %fusion.1), channel_id=1, source_target_pairs={{0,8},{1,121},{8,16},{9,1},{16,24},{17,9},{24,32},{25,17},{32,40},... | collective-permute-start | bytes 884744 | tf_op jit(solution)/shard_map/ppermute | solution.py:323
  35.2 2.9 %collective-permute-start.1 = (bf16[144,1024]{1,0:T(8,128)(2,1)S(1)}, bf16[144,1024]{1,0:T(8,128)(2,1)S(1)}, u32[]{:S(2)}, u32[]{:S(2)}) collective-permute-start(bf16[144,1024]{1,0:T(8,128)(2,1)S(1)} %fusion.1), channel_id=1, source_target_pairs={{0,120},{1,9},{8,0},{9,17},{16,8},{17,25},{24,16},{25,33},{32,24},... | collective-permute-start | bytes 884744 | tf_op jit(solution)/shard_map/ppermute | solution.py:323
  38.1 3.3 %collective-permute-start.2 = (bf16[128,1024]{1,0:T(8,128)(2,1)S(1)}, bf16[128,1024]{1,0:T(8,128)(2,1)S(1)}, u32[]{:S(2)}, u32[]{:S(2)}) collective-permute-start(bf16[128,1024]{1,0:T(8,128)(2,1)S(1)} %all_gather.9.own), channel_id=1, source_target_pairs={{0,16},{1,113},{8,24},{9,121},{16,32},{17,1},{24,40},{25,9},{32,48... | collective-permute-start | bytes 786440 | tf_op jit(solution)/shard_map/ppermute | solution.py:323
  41.4 7.9 %collective-permute-done.2.across = bf16[128,1024]{1,0:T(8,128)(2,1)S(1)} collective-permute-done((bf16[128,1024]{1,0:T(8,128)(2,1)S(1)}, bf16[128,1024]{1,0:T(8,128)(2,1)S(1)}, u32[]{:S(2)}, u32[]{:S(2)}) %collective-permute-start.2) | collective-permute-done | bytes 262176 | tf_op jit(solution)/shard_map/ppermute | solution.py:323
  49.3 0.0 collective-permute-done.one
  49.3 0.0 collective-permute-done.1.other
  49.3 0.9 shard_map.110
  50.2 15.4 %all_to_all.20.parts = bf16[8,144,256]{2,1,0:T(8,128)(2,1)S(1)} all-to-all(bf16[8,144,256]{2,1,0:T(8,128)(2,1)S(1)} %bitcast.6), channel_id=1, replica_groups=mesh['x'=4,'zh'=4,'zl'=4,'y'=4,'core'=2] {'y','core'}, dimensions={0} | all-to-all | bytes 1179648 | tf_op jit(solution)/shard_map/all_to_all | solution.py:29
  65.6 0.1 shard_map.111
  65.6 5.5 %collective-permute-start.3 = (bf16[144,256]{1,0:T(8,128)(2,1)S(1)}, bf16[144,256]{1,0:T(8,128)(2,1)S(1)}, u32[]{:S(2)}, u32[]{:S(2)}) collective-permute-start(bf16[144,256]{1,0:T(8,128)(2,1)S(1)} %shard_map.111), channel_id=1, source_target_pairs={{0,256},{2,384},{4,0},{6,128},{128,258},{130,386},{132,2},{134,130... | collective-permute-start | bytes 221192 | tf_op jit(solution)/shard_map/ppermute | solution.py:42
  71.8 0.0 copy-start.2
  71.8 0.1 copy.13.step
  72.0 0.6 copy-done.2
  72.6 0.0 copy-done.4
  72.6 1.4 %shard_map.112 = (bf16[128,1024]{1,0:T(8,128)(2,1)S(1)}, f32[128,16]{1,0:T(8,128)S(1)}, f32[16,128]{1,0:T(8,128)S(1)}, bf16[1024,128]{1,0:T(8,128)(2,1)S(1)}, bf16[16,16,128]{2,1,0:T(8,128)(2,1)S(1)}) custom-call(s32[1]{0:T(128)S(6)} %copy.14.tenant, bf16[128,1024]{1,0:T(8,128)(2,1)S(1)} %copy-done, bf16[16,1024]{1,0:T(8,128)(2,1)S(1)} %copy-done.2, ...), custom_call_target="tpu_custom_call" | custom-call | flops 1000000 | bytes 1000000 | tf_op jit(solution)/shard_map/pallas_call | solution.py:51
  74.0 0.0 collective-permute-done.3.sums
  74.0 0.3 shard_map.113
  74.3 18.8 %all_to_all.21.got = bf16[16,80,128]{2,1,0:T(8,128)(2,1)S(1)} all-to-all(bf16[16,80,128]{2,1,0:T(8,128)(2,1)S(1)} %get-tuple-element.25), channel_id=1, replica_groups=mesh['x'=4,'zh'=4,'zl'=4,'y'=4,'core'=2] {'x','zl'}, dimensions={0} | all-to-all | bytes 655360 | tf_op jit(solution)/shard_map/all_to_all | solution.py:29
  93.2 0.1 shard_map.114
  93.2 19.4 %all-gather = bf16[1088,128]{1,0:T(8,128)(2,1)S(1)} all-gather(bf16[272,128]{1,0:T(8,128)(2,1)S(1)} %shard_map.114), channel_id=2, replica_groups=mesh['x'=4,'zh'=4,'zl'=4,'y'=4,'core'=2] {'zh'}, dimensions={0}, use_global_device_ids=true | all-gather | bytes 348160 | tf_op jit(solution)/shard_map/all_gather | solution.py:370
  112.6 0.9 shard_map.115
  113.5 4.9 %all-to-all-start.3 = ((bf16[16,64,128]{2,1,0:T(8,128)(2,1)}), bf16[16,64,128]{2,1,0:T(8,128)(2,1)S(1)}, u32[]{:S(2)}, u32[]{:S(2)}) async-start(bf16[16,64,128]{2,1,0:T(8,128)(2,1)} %shard_map.115), calls=%async_computation.3 | async-start | bytes 524288 | tf_op jit(solution)/shard_map/all_to_all | solution.py:29
  118.5 0.0 copy-start.5
  118.5 0.6 copy-done.5
  119.1 0.8 shard_map.116
  119.9 6.9 %all-to-all-done.3 = bf16[16,64,128]{2,1,0:T(8,128)(2,1)S(1)} async-done(((bf16[16,64,128]{2,1,0:T(8,128)(2,1)}), bf16[16,64,128]{2,1,0:T(8,128)(2,1)S(1)}, u32[]{:S(2)}, u32[]{:S(2)}) %all-to-all-start.3) | async-done | bytes 262176 | tf_op jit(solution)/shard_map/all_to_all | solution.py:29
  126.9 1.0 shard_map.117
  (16 shorter events, 0.1 us)
Async XLA Ops:
  2.0 4.5 %copy-start.6 = (bf16[1024,32]{0,1:T(8,128)(2,1)S(1)}, bf16[1024,32]{0,1:T(8,128)(2,1)}, u32[]{:S(2)}) copy-start(bf16[1024,32]{0,1:T(8,128)(2,1)} %param.12) | copy-start | bytes 196612
  2.0 30.1 %all-to-all-start = ((bf16[4,128,1024]{2,1,0:T(8,128)(2,1)}), bf16[4,128,1024]{2,1,0:T(8,128)(2,1)S(1)}, u32[]{:S(2)}, u32[]{:S(2)}) async-start(bf16[4,128,1024]{2,1,0:T(8,128)(2,1)} %shard_map.109), calls=%async_computation | async-start | bytes 2097152 | tf_op jit(solution)/shard_map/all_to_all | solution.py:29
  32.2 17.1 %collective-permute-start = (bf16[144,1024]{1,0:T(8,128)(2,1)S(1)}, bf16[144,1024]{1,0:T(8,128)(2,1)S(1)}, u32[]{:S(2)}, u32[]{:S(2)}) collective-permute-start(bf16[144,1024]{1,0:T(8,128)(2,1)S(1)} %fusion.1), channel_id=1, source_target_pairs={{0,8},{1,121},{8,16},{9,1},{16,24},{17,9},{24,32},{25,17},{32,40},... | collective-permute-start | bytes 884744 | tf_op jit(solution)/shard_map/ppermute | solution.py:323
  35.2 14.1 %collective-permute-start.1 = (bf16[144,1024]{1,0:T(8,128)(2,1)S(1)}, bf16[144,1024]{1,0:T(8,128)(2,1)S(1)}, u32[]{:S(2)}, u32[]{:S(2)}) collective-permute-start(bf16[144,1024]{1,0:T(8,128)(2,1)S(1)} %fusion.1), channel_id=1, source_target_pairs={{0,120},{1,9},{8,0},{9,17},{16,8},{17,25},{24,16},{25,33},{32,24},... | collective-permute-start | bytes 884744 | tf_op jit(solution)/shard_map/ppermute | solution.py:323
  38.1 11.2 %collective-permute-start.2 = (bf16[128,1024]{1,0:T(8,128)(2,1)S(1)}, bf16[128,1024]{1,0:T(8,128)(2,1)S(1)}, u32[]{:S(2)}, u32[]{:S(2)}) collective-permute-start(bf16[128,1024]{1,0:T(8,128)(2,1)S(1)} %all_gather.9.own), channel_id=1, source_target_pairs={{0,16},{1,113},{8,24},{9,121},{16,32},{17,1},{24,40},{25,9},{32,48... | collective-permute-start | bytes 786440 | tf_op jit(solution)/shard_map/ppermute | solution.py:323
  65.5 6.3 %copy-start.7 = (f32[128,16]{0,1:T(8,128)S(1)}, f32[128,16]{0,1:T(8,128)}, u32[]{:S(2)}) copy-start(f32[128,16]{0,1:T(8,128)} %param.16) | copy-start | bytes 24580
  65.6 6.4 %copy-start = (bf16[128,1024]{1,0:T(8,128)(2,1)S(1)}, bf16[128,1024]{1,0:T(8,128)(2,1)}, u32[]{:S(2)}) copy-start(bf16[128,1024]{1,0:T(8,128)(2,1)} %inner.3) | copy-start | bytes 786436
  65.6 8.4 %collective-permute-start.3 = (bf16[144,256]{1,0:T(8,128)(2,1)S(1)}, bf16[144,256]{1,0:T(8,128)(2,1)S(1)}, u32[]{:S(2)}, u32[]{:S(2)}) collective-permute-start(bf16[144,256]{1,0:T(8,128)(2,1)S(1)} %shard_map.111), channel_id=1, source_target_pairs={{0,256},{2,384},{4,0},{6,128},{128,258},{130,386},{132,2},{134,130... | collective-permute-start | bytes 221192 | tf_op jit(solution)/shard_map/ppermute | solution.py:42
  71.8 0.8 copy-start.2
  72.0 0.7 copy-start.4
  72.6 1.4 %copy-start.3 = (f32[4,256]{1,0:T(4,128)S(1)}, f32[4,256]{1,0:T(4,128)}, u32[]{:S(2)}) copy-start(f32[4,256]{1,0:T(4,128)} %taps.1) | copy-start | bytes 12292
  113.5 5.0 %copy-start.8 = (bf16[1024]{0:T(1024)(128)(2,1)S(1)}, bf16[1024]{0:T(1024)(128)(2,1)}, u32[]{:S(2)}) copy-start(bf16[1024]{0:T(1024)(128)(2,1)} %param.21) | copy-start | bytes 6148
  113.5 5.0 %copy-start.1 = (bf16[128,1024]{1,0:T(8,128)(2,1)S(1)}, bf16[128,1024]{1,0:T(8,128)(2,1)}, u32[]{:S(2)}) copy-start(bf16[128,1024]{1,0:T(8,128)(2,1)} %gate.1) | copy-start | bytes 786436
  113.5 13.4 %all-to-all-start.3 = ((bf16[16,64,128]{2,1,0:T(8,128)(2,1)}), bf16[16,64,128]{2,1,0:T(8,128)(2,1)S(1)}, u32[]{:S(2)}, u32[]{:S(2)}) async-start(bf16[16,64,128]{2,1,0:T(8,128)(2,1)} %shard_map.115), calls=%async_computation.3 | async-start | bytes 524288 | tf_op jit(solution)/shard_map/all_to_all | solution.py:29
  118.5 0.7 copy-start.5
